TPU v7x, 32 devices: a whole 2x2x4 slice. The times are simulated.
32 devices in a mesh: cond: 4 (over x, core), slab: 8 (over z, y).
Axes of the slice: x: 2, y: 2, z: 4, core: 2. Of those that a mesh axis runs over, the one named last changes fastest.
Arguments:
- adjoint: float32 [4, 32, 512, 128], P('cond', 'slab'), may hold values from -6 to 6
- phase: bfloat16 [4, 32, 512, 128], P('cond', 'slab'), may hold values from -1.09375 to 1.09375
- targets: bfloat16 [4, 256, 128], P('cond', 'slab'), may hold values from -1 to 1
- owners: int32 [4, 256, 1], P('cond', 'slab'), may hold values from 0 to 7; in each aligned block of 32 rows (0 to 31, 32 to 63, ..., all dimensions but the last counted through in order) at most 8 rows name the same one
- target_cell: int32 [4, 256], P('cond', 'slab'), may hold values from 0 to 2047
- rate_index: int32 [4], P('cond'), may hold values from 0 to 7
- inflow_rates: float32 [8], replicated, may hold values from 0.5 to 2
- wall_mask: int32 [2, 32, 512], P(None, 'slab'), may hold values 0 or 1
Outputs:
- adjoint_out: float32 [4, 32, 512, 128], P('cond', 'slab')
- wall_gradient: float32 [2, 32, 512], P(None, 'slab')
Inputs may be any that keep to these rules, and one draw needn't show every extreme that they name: `owners`: within each aligned block of 32 rows, no slab is named by more than 8 rows.
All inputs are finite; a program needn't handle non-finite values. No bound on the sum of `wall_mask` on one device may be relied on, other than what follows from the above.
Results may differ from a plain program's by a relative error of at most 0.0003.
Values may be sent and summed in bfloat16 or wider, within the bound.
No kernel may reach another device: no remote copies, remote signals or barrier semaphores. Data moves between devices by JAX's collectives and lax.ppermute only.
A program may use at most 64 MiB of HBM per device.

v0:
```python
import jax
import jax.numpy as jnp
from jax import lax
from jax.sharding import PartitionSpec as P

mobility_step = 0.02
stiffness_step = 0.01
transport_step = 0.125
wall_weight = 0.25


def extended_2(cells, sides, width):
    for axis, dim in sides:
        count = lax.axis_size(axis)
        ends = count - 1
        head = lax.slice_in_dim(cells, 0, width, axis=dim)
        tail = lax.slice_in_dim(cells, cells.shape[dim] - width, cells.shape[dim], axis=dim)
        cells = jnp.concatenate(
            [
                lax.ppermute(tail, axis, [(i, (i + 1) % count) for i in range(ends)]),
                cells,
                lax.ppermute(head, axis, [((i + 1) % count, i) for i in range(ends)]),
            ],
            axis=dim,
        )
    return cells


def inner_laplacian(field):
    center = field[1:-1]
    along_y = jnp.pad(center, ((0, 0), (1, 1), (0, 0)))
    along_z = jnp.pad(center, ((0, 0), (0, 0), (1, 1)))
    return (
        field[2:]
        + field[:-2]
        + along_y[:, 2:]
        + along_y[:, :-2]
        + along_z[:, :, 2:]
        + along_z[:, :, :-2]
        - 6.0 * center
    )


def within_grid(length, first_row, grid_rows):
    placed = first_row + jnp.arange(length)
    within = (placed >= 0) & (placed < grid_rows)
    return within.astype(jnp.float32)[:, None, None]


def adjoint_step(extended, curvature, inflow, first_row, grid_rows):
    length = extended.shape[0]
    first_lap = inner_laplacian(extended) * within_grid(length - 2, first_row + 1, grid_rows)
    second_lap = inner_laplacian(first_lap)
    center = extended[2:-2]
    column_depth = extended.shape[2]
    height = (jnp.arange(column_depth).astype(jnp.float32) + 0.5) / column_depth
    profile = 4.0 * height * (1.0 - height)
    padded = jnp.pad(center, ((0, 0), (1, 1), (0, 0)))
    transport = (padded[:, 2:] - padded[:, :-2]) * profile
    updated = (
        center
        + mobility_step * curvature * first_lap[1:-1]
        - stiffness_step * second_lap
        + transport_step * inflow * transport
    )
    return updated * within_grid(length - 4, first_row + 2, grid_rows)


def wall_term(state, phase32, wall_mask):
    lower_wall = (1.0 - phase32[:, :, 0] ** 2) * state[:, :, 0]
    upper_wall = (1.0 - phase32[:, :, -1] ** 2) * state[:, :, -1]
    return wall_weight * wall_mask.astype(jnp.float32) * jnp.stack([lower_wall, upper_wall])


def inject(state, flat_phase, arrived, row_index):
    cells_here = flat_phase.shape[0]
    safe_index = jnp.minimum(row_index, cells_here - 1)
    source = flat_phase[safe_index] - arrived.astype(jnp.float32)
    shaped = state.reshape(cells_here, state.shape[2])
    return shaped.at[row_index].add(source, mode="drop").reshape(state.shape)


def on_device(adjoint, phase, targets, owners, target_cell, rate_index, inflow_rates, wall_mask):
    state = adjoint[0]
    phase32 = phase[0].astype(jnp.float32)
    slab_width = state.shape[0]
    column_depth = state.shape[2]
    slab_count = lax.axis_size("slab")
    position = lax.axis_index("slab")
    grid_rows = slab_width * slab_count
    anchor = position * slab_width
    choose = jnp.arange(inflow_rates.shape[0]) == rate_index[0]
    inflow = jnp.sum(jnp.where(choose, inflow_rates, 0.0))
    curvature = 3.0 * phase32 * phase32 - 1.0
    gradient = jnp.zeros(wall_mask.shape, jnp.float32)
    for sweep in range(2):
        extended = extended_2(state, (("slab", 0),), 2)
        state = adjoint_step(extended, curvature, inflow, anchor - 2, grid_rows)
        gradient = gradient + wall_term(state, phase32, wall_mask)
    flat_phase = phase32.reshape(-1, column_depth)
    cells_here = flat_phase.shape[0]
    gathered_rows, gathered_cells, gathered_owners = (
        lax.all_gather(targets, "slab", axis=1, tiled=True),
        lax.all_gather(target_cell, "slab", axis=1, tiled=True),
        lax.all_gather(owners, "slab", axis=1, tiled=True),
    )
    row_index = jnp.where(gathered_owners[0, :, 0] == position, gathered_cells[0], cells_here)
    state = inject(state, flat_phase, gathered_rows[0], row_index)
    wall_gradient = lax.psum(gradient, "cond")
    return (state[None], wall_gradient)


def solution(mesh):
    in_specs = (
        P("cond", "slab", None, None),
        P("cond", "slab", None, None),
        P("cond", "slab", None),
        P("cond", "slab", None),
        P("cond", "slab"),
        P("cond"),
        P(),
        P(None, "slab", None),
    )
    out_specs = (P("cond", "slab", None, None), P(None, "slab", None))
    return jax.shard_map(
        on_device, mesh=mesh, in_specs=in_specs, out_specs=out_specs, check_vma=False
    )
```

profile of v0, /device:TPU:0, one launch (start us, length us, event | category | flops | bytes accessed | tf_op | source)
XLA Modules:
  0.0 108.1 jit_solution(1953793413634695220)
XLA Ops:
  0.6 0.0 copy-start.8
  0.7 2.2 %slice_bitcast_fusion = (f32[2,512,128]{2,1,0:T(8,128)S(1)}, f32[2,512,128]{2,1,0:T(8,128)}) fusion(f32[1,4,512,128]{3,2,1,0:T(8,128)} %param.8), kind=kLoop, calls=%fused_computation.63 | loop fusion | bytes 2097152 | tf_op jit(solution)/shard_map/slice | solution.py:17
  2.9 1.3 %collective-permute-start = (f32[2,512,128]{2,1,0:T(8,128)}, f32[2,512,128]{2,1,0:T(8,128)S(1)}, u32[]{:S(2)}, u32[]{:S(2)}) collective-permute-start(f32[2,512,128]{2,1,0:T(8,128)} %get-tuple-element.13), channel_id=1, source_target_pairs={{1,0},{2,1},{3,2},{4,3},{5,4},{6,5},{7,6},{9,8},{10,9},{11,10},{12... | collective-permute-start | bytes 1572872 | tf_op jit(solution)/shard_map/ppermute | solution.py:22
  4.2 5.5 %collective-permute-start.1 = (f32[2,512,128]{2,1,0:T(8,128)S(1)}, f32[2,512,128]{2,1,0:T(8,128)S(1)}, u32[]{:S(2)}, u32[]{:S(2)}) collective-permute-start(f32[2,512,128]{2,1,0:T(8,128)S(1)} %get-tuple-element.12), channel_id=1, source_target_pairs={{0,1},{1,2},{2,3},{3,4},{4,5},{5,6},{6,7},{8,9},{9,10},{10,11},{11... | collective-permute-start | bytes 1572872 | tf_op jit(solution)/shard_map/ppermute | solution.py:20
  10.4 0.7 fusion.41
  11.1 0.6 dynamic-slice
  12.3 0.1 bitcast_dynamic-update-slice_fusion
  12.5 0.1 bitcast_dynamic-update-slice_fusion.1
  12.5 26.2 %all-reduce.12 = (s32[256]{0:T(256)S(1)}, s32[256]{0:T(256)S(1)}) all-reduce(s32[256]{0:T(256)S(1)} %bitcast_dynamic-update-slice_fusion, s32[256]{0:T(256)S(1)} %bitcast_dynamic-update-slice_fusion.1), channel_id=1, replica_groups=mesh['cond'=4,'slab'=8] {'slab'}, use_global_device_ids=true, to_apply=%add.11 | all-reduce | flops 512 | bytes 4096
  39.5 0.1 convert_bitcast_fusion
  39.6 0.0 collective-permute-done
  39.6 0.1 pad_maximum_fusion.2
  39.7 0.9 fusion.3
  40.6 0.1 slice.174
  40.7 1.2 %fusion.20 = f32[4,512,128]{2,1,0:T(8,128)S(1)} fusion(f32[4,512,128]{2,1,0:T(8,128)S(1)} %slice.174, f32[6,512,128]{2,1,0:T(8,128)S(1)} %fusion.3, f32[4,512,128]{2,1,0:T(8,128)S(1)} %bitcast.38, f32[4]{0:T(128)S(1)} %and_convert_fusion, f32[128]{0:T(128)S(1)} %subtract_multiply_fusion, f32[]{:T(128)S(6)} %mul.193, bf16[1,4,512,128]{3,2,1,0:T(8,128)(2,1)S(1)} %copy-done.2), kind=kLoop, calls=%fused_computation.37 | loop fusion | flops 5505024 | bytes 5767700 | tf_op jit(solution)/shard_map/mul | solution.py:66
  41.9 0.0 copy-start.4
  41.9 0.1 fusion.43
  42.0 1.3 %collective-permute-start.2 = (f32[2,512,128]{2,1,0:T(8,128)S(1)}, f32[2,512,128]{2,1,0:T(8,128)S(1)}, u32[]{:S(2)}, u32[]{:S(2)}) collective-permute-start(f32[2,512,128]{2,1,0:T(8,128)S(1)} %get-tuple-element.11), channel_id=1, source_target_pairs={{1,0},{2,1},{3,2},{4,3},{5,4},{6,5},{7,6},{9,8},{10,9},{11,10},{12... | collective-permute-start | bytes 1572872 | tf_op jit(solution)/shard_map/ppermute | solution.py:22
  43.3 4.6 %collective-permute-start.3 = (f32[2,512,128]{2,1,0:T(8,128)S(1)}, f32[2,512,128]{2,1,0:T(8,128)S(1)}, u32[]{:S(2)}, u32[]{:S(2)}) collective-permute-start(f32[2,512,128]{2,1,0:T(8,128)S(1)} %get-tuple-element.10), channel_id=1, source_target_pairs={{0,1},{1,2},{2,3},{3,4},{4,5},{5,6},{6,7},{8,9},{9,10},{10,11},{11... | collective-permute-start | bytes 1572872 | tf_op jit(solution)/shard_map/ppermute | solution.py:20
  47.9 41.0 %all_gather.11 = bf16[1,256,128]{2,1,0:T(8,128)(2,1)S(1)} all-gather(bf16[1,32,128]{2,1,0:T(8,128)(2,1)S(1)} %copy-done.4), channel_id=1, replica_groups=mesh['cond'=4,'slab'=8] {'slab'}, dimensions={1}, use_global_device_ids=true | all-gather | bytes 73728 | tf_op jit(solution)/shard_map/all_gather | solution.py:103
  88.9 0.1 bitcast_convert_fusion
  89.0 0.0 collective-permute-done.2
  89.0 0.1 pad_maximum_fusion
  89.1 0.9 fusion.7
  90.1 0.1 slice.179
  90.1 1.2 %fusion.27 = f32[4,512,128]{2,1,0:T(8,128)S(1)} fusion(f32[4,512,128]{2,1,0:T(8,128)S(1)} %slice.179, f32[6,512,128]{2,1,0:T(8,128)S(1)} %fusion.7, f32[4,512,128]{2,1,0:T(8,128)S(1)} %fusion.20, f32[4]{0:T(128)S(1)} %and_convert_fusion, f32[128]{0:T(128)S(1)} %subtract_multiply_fusion, f32[]{:T(128)S(6)} %mul.193, bf16[1,4,512,128]{3,2,1,0:T(8,128)(2,1)S(1)} %copy-done.2), kind=kLoop, calls=%fused_computation.44 | loop fusion | flops 5505024 | bytes 5767700 | tf_op jit(solution)/shard_map/mul | solution.py:66
  91.4 0.0 copy-start.3
  91.4 2.0 %fusion.29 = (f32[4,512]{1,0:T(4,128)S(1)}, f32[4,512]{1,0:T(4,128)S(1)}, f32[4,512]{1,0:T(4,128)S(1)}, f32[4,512]{1,0:T(4,128)S(1)}) fusion(f32[4,512,128]{2,1,0:T(8,128)S(1)} %fusion.27, f32[4,512,128]{2,1,0:T(8,128)S(1)} %convert_bitcast_fusion, f32[4,512,128]{2,1,0:T(8,128)S(1)} %fusion.20), kind=kLoop, calls=%fused_computation.48 | loop fusion | flops 16384 | bytes 81920 | tf_op jit(solution)/shard_map/mul | solution.py:70
  93.4 10.7 %psum.7 = f32[2,4,512]{2,1,0:T(4,128)} all-reduce(f32[2,4,512]{2,1,0:T(4,128)S(1)} %fusion.40), channel_id=1, replica_groups=mesh['cond'=4,'slab'=8] {'cond'}, use_global_device_ids=true, to_apply=%region_2.3 | all-reduce | flops 4096 | bytes 32768 | tf_op jit(solution)/shard_map/psum | solution.py:109
  104.1 3.0 %scatter_custom_fusion = f32[2048,128]{1,0:T(8,128)S(1)} fusion(f32[2048,128]{1,0:T(8,128)S(1)} %bitcast.39, s32[256]{0:T(256)S(1)} %bitcast.47, bf16[1,256,128]{2,1,0:T(8,128)(2,1)S(1)} %all_gather.11, f32[2048,128]{1,0:T(8,128)S(1)} %bitcast_convert_fusion, s32[1024]{0:T(1024)S(1)} %pad_clamp_fusion), kind=kCustom, calls=%fused_computation.67 | custom fusion | flops 98304 | bytes 2166784 | tf_op jit(solution)/shard_map/scatter-add | solution.py:80
  107.1 0.0 copy-start.1
  107.1 1.0 copy-done.1
  (24 shorter events, 0.1 us)
Async XLA Ops:
  0.6 10.5 %copy-start.8 = (u32[32]{0:T(128)S(1)}, u32[32]{0:T(128)}, u32[]{:S(2)}) copy-start(u32[32]{0:T(128)} %constant.84) | copy-start | bytes 388
  0.6 38.9 %copy-start = (f32[1,4,512,128]{3,2,1,0:T(8,128)S(1)}, f32[1,4,512,128]{3,2,1,0:T(8,128)}, u32[]{:S(2)}) copy-start(f32[1,4,512,128]{3,2,1,0:T(8,128)} %param.8) | copy-start | bytes 3145732
  0.7 9.7 %copy-start.5 = (f32[8]{0:T(128)S(1)}, f32[8]{0:T(128)}, u32[]{:S(2)}) copy-start(f32[8]{0:T(128)} %param.14) | copy-start | bytes 100
  0.7 11.7 %copy-start.6 = (s32[1,32]{1,0:T(1,128)S(1)}, s32[1,32]{1,0:T(1,128)}, u32[]{:S(2)}) copy-start(s32[1,32]{1,0:T(1,128)} %param.12) | copy-start | bytes 388
  0.7 11.8 %copy-start.7 = (s32[1,32,1]{1,2,0:T(1,128)S(1)}, s32[1,32,1]{1,2,0:T(1,128)}, u32[]{:S(2)}) copy-start(s32[1,32,1]{1,2,0:T(1,128)} %param.11) | copy-start | bytes 388
  0.7 38.8 %copy-start.2 = (bf16[1,4,512,128]{3,2,1,0:T(8,128)(2,1)S(1)}, bf16[1,4,512,128]{3,2,1,0:T(8,128)(2,1)}, u32[]{:S(2)}) copy-start(bf16[1,4,512,128]{3,2,1,0:T(8,128)(2,1)} %param.9) | copy-start | bytes 1572868
  2.9 36.7 %collective-permute-start = (f32[2,512,128]{2,1,0:T(8,128)}, f32[2,512,128]{2,1,0:T(8,128)S(1)}, u32[]{:S(2)}, u32[]{:S(2)}) collective-permute-start(f32[2,512,128]{2,1,0:T(8,128)} %get-tuple-element.13), channel_id=1, source_target_pairs={{1,0},{2,1},{3,2},{4,3},{5,4},{6,5},{7,6},{9,8},{10,9},{11,10},{12... | collective-permute-start | bytes 1572872 | tf_op jit(solution)/shard_map/ppermute | solution.py:22
  4.2 35.4 %collective-permute-start.1 = (f32[2,512,128]{2,1,0:T(8,128)S(1)}, f32[2,512,128]{2,1,0:T(8,128)S(1)}, u32[]{:S(2)}, u32[]{:S(2)}) collective-permute-start(f32[2,512,128]{2,1,0:T(8,128)S(1)} %get-tuple-element.12), channel_id=1, source_target_pairs={{0,1},{1,2},{2,3},{3,4},{4,5},{5,6},{6,7},{8,9},{9,10},{10,11},{11... | collective-permute-start | bytes 1572872 | tf_op jit(solution)/shard_map/ppermute | solution.py:20
  41.9 6.0 %copy-start.4 = (bf16[1,32,128]{2,1,0:T(8,128)(2,1)S(1)}, bf16[1,32,128]{2,1,0:T(8,128)(2,1)}, u32[]{:S(2)}) copy-start(bf16[1,32,128]{2,1,0:T(8,128)(2,1)} %param.10) | copy-start | bytes 24580
  42.0 47.0 %collective-permute-start.2 = (f32[2,512,128]{2,1,0:T(8,128)S(1)}, f32[2,512,128]{2,1,0:T(8,128)S(1)}, u32[]{:S(2)}, u32[]{:S(2)}) collective-permute-start(f32[2,512,128]{2,1,0:T(8,128)S(1)} %get-tuple-element.11), channel_id=1, source_target_pairs={{1,0},{2,1},{3,2},{4,3},{5,4},{6,5},{7,6},{9,8},{10,9},{11,10},{12... | collective-permute-start | bytes 1572872 | tf_op jit(solution)/shard_map/ppermute | solution.py:22
  43.3 45.7 %collective-permute-start.3 = (f32[2,512,128]{2,1,0:T(8,128)S(1)}, f32[2,512,128]{2,1,0:T(8,128)S(1)}, u32[]{:S(2)}, u32[]{:S(2)}) collective-permute-start(f32[2,512,128]{2,1,0:T(8,128)S(1)} %get-tuple-element.10), channel_id=1, source_target_pairs={{0,1},{1,2},{2,3},{3,4},{4,5},{5,6},{6,7},{8,9},{9,10},{10,11},{11... | collective-permute-start | bytes 1572872 | tf_op jit(solution)/shard_map/ppermute | solution.py:20
  91.4 2.1 %copy-start.3 = (s32[2,4,512]{2,1,0:T(4,128)S(1)}, s32[2,4,512]{2,1,0:T(4,128)}, u32[]{:S(2)}) copy-start(s32[2,4,512]{2,1,0:T(4,128)} %param.15) | copy-start | bytes 49156
  107.1 1.0 copy-start.1
where the time goes:
time: 108 us
  blocking collectives  77.9 us (72%)
  starting transfers between devices  12.7 us (12%)
  other arithmetic  10.4 us (10%)
  local copies, waits for them, and re-layouts  4.18 us (4%)
  between operations  2.95 us (3%)
    all_gather x1, blocking collectives, on_device(): lax.all_gather(targets, 'slab', axis=1, tiled=True)  41 us
    unnamed x1, blocking collectives  26.2 us
    psum x1, blocking collectives, on_device(): wall_gradient = lax.psum(gradient, 'cond')  10.7 us
    ppermute x2, starting transfers between devices, extended_2(): lax.ppermute(tail, axis, [(i, (i + 1) % count) for i in range(ends)])  10.1 us
    scatter-add x1, other arithmetic, inject(): return shaped.at[row_index].add(source, mode='drop').reshape(state.shape)  2.96 us
    ppermute x2, starting transfers between devices, extended_2(): lax.ppermute(head, axis, [((i + 1) % count, i) for i in range(ends)])  2.57 us
    mul x2, other arithmetic, adjoint_step(): return updated * within_grid(length - 4, first_row + 2, grid_rows)  2.42 us
    slice x2, local copies, waits for them, and re-layouts, extended_2(): lax.slice_in_dim(cells, cells.shape[dim] - width, cells.shape[dim], axis=...  2.25 us
  transfers between devices with their start and end apart: 4, of which 0 were waited for; matrix products, arithmetic and copies ran while one was open for 2% of the time, Pallas kernels for 0%

commit v1 on v0

v1 whole, which is shorter than its diff:
```python
import jax
import jax.numpy as jnp
from jax import lax
from jax.experimental import pallas as pl
from jax.experimental.pallas import tpu as pltpu
from jax.sharding import PartitionSpec as P

mobility_step = 0.02
stiffness_step = 0.01
transport_step = 0.125
wall_weight = 0.25

f32 = jnp.float32
bf16 = jnp.bfloat16
CHUNK = 64
PAD = 8
ANY = pl.BlockSpec(memory_space=pl.ANY)
VMEM = pl.BlockSpec(memory_space=pltpu.VMEM)
SMEM = pl.BlockSpec(memory_space=pltpu.SMEM)


def cost(flops, nbytes):
    return pl.CostEstimate(flops=flops, bytes_accessed=nbytes, transcendentals=0)


def call(kernel, outs, out_specs, in_specs, scratch, estimate, aliases=None):
    return pl.pallas_call(
        kernel,
        out_shape=outs,
        out_specs=out_specs,
        in_specs=in_specs,
        scratch_shapes=scratch,
        input_output_aliases=aliases or {},
        cost_estimate=estimate,
        compiler_params=pltpu.CompilerParams(vmem_limit_bytes=24 * 1024 * 1024),
    )


def starts(rows):
    return range(0, rows, CHUNK)


def read(ref, lead, y, shift=0):
    return ref[(*lead, pl.ds(PAD + y + shift, CHUNK), slice(None))]


def z_sum(v):
    depth = v.shape[1]
    lane = lax.broadcasted_iota(jnp.int32, v.shape, 1)
    below = jnp.where(lane == 0, 0.0, pltpu.roll(v, 1, 1))
    above = jnp.where(lane == depth - 1, 0.0, pltpu.roll(v, depth - 1, 1))
    return below + above


def plane_part(ref, lead, y):
    v = read(ref, lead, y)
    return read(ref, lead, y, 1) + read(ref, lead, y, -1) + z_sum(v) - 6.0 * v


def clear_margins(ref, lead, rows):
    zero = jnp.zeros((PAD, ref.shape[-1]), f32)
    ref[(*lead, pl.ds(0, PAD), slice(None))] = zero
    ref[(*lead, pl.ds(PAD + rows, PAD), slice(None))] = zero


def oriented(depth_from_a, layers):
    odd = lax.rem(lax.axis_index("slab"), 2)
    return jnp.where(odd == 1, depth_from_a, layers - 1 - depth_from_a)


def fetch(pairs, sems):
    copies = [pltpu.make_async_copy(s, d, sems.at[i]) for i, (s, d) in enumerate(pairs)]
    for c in copies:
        c.start()
    for c in copies:
        c.wait()


def write_message(near, far, missing, out):
    rows = far.shape[0] - 2 * PAD
    clear_margins(missing, (), rows)
    for y in starts(rows):
        v = read(near, (), y)
        rounded = v.astype(bf16)
        out[pl.ds(y, CHUNK), :] = rounded
        missing[pl.ds(PAD + y, CHUNK), :] = v - rounded.astype(f32)
    for y in starts(rows):
        out[pl.ds(rows + y, CHUNK), :] = (read(far, (), y) + 2.0 * plane_part(missing, (), y)).astype(bf16)


def first_message(side, adjoint, out, near, far, missing, sems):
    layers = adjoint.shape[0]
    rows = adjoint.shape[1]
    one, two = (0, 1) if side == 0 else (layers - 1, layers - 2)
    fetch(
        [
            (adjoint.at[oriented(one, layers)], near.at[pl.ds(PAD, rows)]),
            (adjoint.at[oriented(two, layers)], far.at[pl.ds(PAD, rows)]),
        ],
        sems,
    )
    write_message(near, far, missing, out)


def make_first_message(adjoint, side):
    layers, rows, depth = adjoint.shape
    padded = pltpu.VMEM((rows + 2 * PAD, depth), f32)
    return call(
        lambda *refs: first_message(side, *refs),
        jax.ShapeDtypeStruct((2 * rows, depth), bf16),
        VMEM,
        [ANY],
        [padded, padded, padded, pltpu.SemaphoreType.DMA((2,))],
        cost(20 * rows * depth, 12 * rows * depth),
    )(adjoint)


def local_step(state, first, phase, inflow, count, emit):
    layers = state.shape[0]
    rows = state.shape[1] - 2 * PAD
    depth = state.shape[2]
    position = lax.axis_index("slab")
    low = jnp.where(position > 0, 1.0, 0.0).astype(f32)
    high = jnp.where(position < count - 1, 1.0, 0.0).astype(f32)
    lane = lax.broadcasted_iota(jnp.int32, (1, depth), 1)
    height = (lane.astype(f32) + 0.5) / depth
    transport = (transport_step * inflow) * (4.0 * height * (1.0 - height))
    for l in range(layers):
        for y in starts(rows):
            lap = plane_part(state, (l,), y)
            if l > 0:
                lap = lap + read(state, (l - 1,), y)
            if l < layers - 1:
                lap = lap + read(state, (l + 1,), y)
            first[l, pl.ds(PAD + y, CHUNK), :] = lap
    for l in range(layers):
        for y in starts(rows):
            v = read(state, (l,), y)
            lap = read(first, (l,), y)
            second = plane_part(first, (l,), y)
            second = second + (read(first, (l - 1,), y) if l > 0 else low * v)
            second = second + (read(first, (l + 1,), y) if l < layers - 1 else high * v)
            p = phase[l, pl.ds(y, CHUNK), :].astype(f32)
            curvature = 3.0 * p * p - 1.0
            moved = read(state, (l,), y, 1) - read(state, (l,), y, -1)
            emit(l, y, v, v + mobility_step * curvature * lap - stiffness_step * second + transport * moved, p)


def load_state(source, state, first, sems):
    layers, rows, _ = source.shape
    copies = [
        pltpu.make_async_copy(source.at[l], state.at[l, pl.ds(PAD, rows)], sems.at[l]) for l in range(layers)
    ]
    for c in copies:
        c.start()
    for l in range(layers):
        clear_margins(state, (l,), rows)
        clear_margins(first, (l,), rows)
    for c in copies:
        c.wait()


def first_local(count, adjoint, phase, rates, choice, out, state, first, sems):
    load_state(adjoint, state, first, sems)

    def emit(l, y, v, stepped, p):
        out[l, pl.ds(y, CHUNK), :] = stepped

    local_step(state, first, phase, rates[choice[0]], count, emit)


def make_first_local(adjoint, phase, rates, choice, count):
    layers, rows, depth = adjoint.shape
    padded = pltpu.VMEM((layers, rows + 2 * PAD, depth), f32)
    return call(
        lambda *refs: first_local(count, *refs),
        jax.ShapeDtypeStruct(adjoint.shape, f32),
        VMEM,
        [ANY, VMEM, SMEM, SMEM],
        [padded, padded, pltpu.SemaphoreType.DMA((layers,))],
        cost(60 * layers * rows * depth, 10 * layers * rows * depth),
    )(adjoint, phase, rates, choice)


def add_halo(message, edge, inner, halo, phase, rows, put_edge, put_inner):
    clear_margins(halo, (), rows)
    for y in starts(rows):
        halo[pl.ds(PAD + y, CHUNK), :] = message[pl.ds(y, CHUNK), :].astype(f32)
    for y in starts(rows):
        near = read(halo, (), y)
        far = message[pl.ds(rows + y, CHUNK), :].astype(f32)
        p = phase[pl.ds(y, CHUNK), :].astype(f32)
        curvature = 3.0 * p * p - 1.0
        both = far + 2.0 * plane_part(halo, (), y)
        put_edge(y, edge(y) + mobility_step * curvature * near - stiffness_step * both)
        put_inner(y, inner(y) - stiffness_step * near)


def wall_rows(v, first_row):
    depth = v.shape[1]
    row = lax.broadcasted_iota(jnp.int32, (8, depth), 0) - first_row
    lane = lax.broadcasted_iota(jnp.int32, (8, depth), 1)
    pick = ((row == 0) & (lane == 0)) | ((row == 1) & (lane == depth - 1))
    pick = jnp.where(pick, 1.0, 0.0).astype(bf16)

    def part(w):
        return lax.dot_general(pick, w, (((1,), (1,)), ((), ())), preferred_element_type=f32)

    if v.dtype == bf16:
        return part(v)
    high = v.astype(bf16)
    rest = v - high.astype(f32)
    middle = rest.astype(bf16)
    low = (rest - middle.astype(f32)).astype(bf16)
    return part(high) + part(middle) + part(low)


def middle(side, message, pre, phase, out, sent, wall, edge, inner, halo, curved, missing, sems):
    layers, rows, depth = pre.shape
    one, two = (0, 1) if side == 0 else (layers - 1, layers - 2)
    fetch(
        [
            (pre.at[oriented(one, layers)], edge.at[pl.ds(PAD, rows)]),
            (pre.at[oriented(two, layers)], inner.at[pl.ds(PAD, rows)]),
            (phase.at[oriented(one, layers)], curved),
        ],
        sems,
    )
    clear_margins(edge, (), rows)

    def put_edge(y, v):
        edge[pl.ds(PAD + y, CHUNK), :] = v
        out[0, pl.ds(y, CHUNK), :] = v

    def put_inner(y, v):
        inner[pl.ds(PAD + y, CHUNK), :] = v
        out[1, pl.ds(y, CHUNK), :] = v

    add_halo(
        message, lambda y: read(edge, (), y), lambda y: read(inner, (), y), halo, curved, rows, put_edge, put_inner
    )
    write_message(edge, inner, missing, sent)
    for y in range(0, rows, 128):
        both = [read(inner, (), y + k) + 2.0 * plane_part(edge, (), y + k) for k in range(0, 128, CHUNK)]
        near = [read(edge, (), y + k) for k in range(0, 128, CHUNK)]
        wall[:, pl.ds(y, 128)] = wall_rows(jnp.concatenate(near), 0) + wall_rows(jnp.concatenate(both), 2)


def make_middle(message, pre, phase, side):
    layers, rows, depth = pre.shape
    padded = pltpu.VMEM((rows + 2 * PAD, depth), f32)
    return call(
        lambda *refs: middle(side, *refs),
        (
            jax.ShapeDtypeStruct((2, rows, depth), f32),
            jax.ShapeDtypeStruct((2 * rows, depth), bf16),
            jax.ShapeDtypeStruct((8, rows), f32),
        ),
        (VMEM, VMEM, VMEM),
        [VMEM, ANY, ANY],
        [padded, padded, padded, pltpu.VMEM((rows, depth), bf16), padded, pltpu.SemaphoreType.DMA((3,))],
        cost(60 * rows * depth, 30 * rows * depth),
    )(message, pre, phase)


def second_local(count, side_a, side_b, phase, rates, choice, index, listed, out, wall, phase_wall, state, first, sems):
    layers, rows, depth = out.shape
    pairs = []
    for i, ref in enumerate((side_a, side_b)):
        for j in range(2):
            depth_from_a = j if i == 0 else layers - 1 - j
            pairs.append((ref.at[j], state.at[oriented(depth_from_a, layers), pl.ds(PAD, rows)]))
    copies = [pltpu.make_async_copy(s, d, sems.at[i]) for i, (s, d) in enumerate(pairs)]
    for c in copies:
        c.start()
    for l in range(layers):
        clear_margins(state, (l,), rows)
        clear_margins(first, (l,), rows)
    total = index.shape[1]
    rhs = jnp.concatenate([jnp.ones((total, depth), bf16), listed[...]], axis=1)
    for l in range(layers):
        for y in range(0, rows, 128):
            cell = lax.broadcasted_iota(jnp.int32, (128, total), 0) + (l * rows + y)
            here = jnp.where(cell == index[...], 1.0, 0.0).astype(bf16)
            added = jnp.dot(here, rhs, preferred_element_type=f32)
            p = phase[l, pl.ds(y, 128), :].astype(f32)
            out[l, pl.ds(y, 128), :] = added[:, :depth] * p - added[:, depth:]
            phase_wall[l, :, pl.ds(y, 128)] = wall_rows(phase[l, pl.ds(y, 128), :], 0)
    for c in copies:
        c.wait()
    held = []

    def emit(l, y, v, stepped, p):
        out[l, pl.ds(y, CHUNK), :] += stepped
        held.append(v + stepped)
        if len(held) * CHUNK == 128:
            wall[l, :, pl.ds(y + CHUNK - 128, 128)] = wall_rows(jnp.concatenate(held), 0)
            held.clear()

    local_step(state, first, phase, rates[choice[0]], count, emit)


def make_second_local(side_a, side_b, phase, rates, choice, index, listed, count):
    layers, rows, depth = phase.shape
    padded = pltpu.VMEM((layers, rows + 2 * PAD, depth), f32)
    return call(
        lambda *refs: second_local(count, *refs),
        (
            jax.ShapeDtypeStruct((layers, rows, depth), f32),
            jax.ShapeDtypeStruct((layers, 8, rows), f32),
            jax.ShapeDtypeStruct((layers, 8, rows), f32),
        ),
        (VMEM, VMEM, VMEM),
        [ANY, ANY, VMEM, SMEM, SMEM, VMEM, VMEM],
        [padded, padded, pltpu.SemaphoreType.DMA((4,))],
        cost(120 * layers * rows * depth, 10 * layers * rows * depth),
    )(side_a, side_b, phase, rates, choice, index, listed)


def wall_kernel(wall, phase_wall, from_a, from_b, mask, out):
    layers = wall.shape[0]
    odd = lax.rem(lax.axis_index("slab"), 2) == 1
    low = jnp.where(odd, from_a[...], from_b[...])
    high = jnp.where(odd, from_b[...], from_a[...])
    for l in range(layers):
        p = phase_wall[l, :2, :]
        w = wall[l, :2, :]
        curvature = 3.0 * p * p - 1.0
        for halo, far_off in ((low, l), (high, layers - 1 - l)):
            if far_off == 0:
                w = w + mobility_step * curvature * halo[:2] - stiffness_step * halo[2:4]
            elif far_off == 1:
                w = w - stiffness_step * halo[:2]
        m = mask[:, l, :].astype(f32)
        out[:, l, :] = wall_weight * m * (1.0 - p * p) * w


def make_walls(wall, phase_wall, from_a, from_b, mask):
    return call(
        wall_kernel,
        jax.ShapeDtypeStruct(mask.shape, f32),
        VMEM,
        [VMEM] * 5,
        [],
        cost(40 * mask.size, 20 * mask.size),
    )(wall, phase_wall, from_a, from_b, mask)


def final(side, message, pre, phase, out, edge, inner, halo, curved, sems, out_sems):
    layers, rows, depth = pre.shape
    one, two = (0, 1) if side == 0 else (layers - 1, layers - 2)
    one, two = oriented(one, layers), oriented(two, layers)
    fetch([(pre.at[one], edge), (pre.at[two], inner), (phase.at[one], curved)], sems)

    def put_edge(y, v):
        edge[pl.ds(y, CHUNK), :] = v

    def put_inner(y, v):
        inner[pl.ds(y, CHUNK), :] = v

    add_halo(
        message,
        lambda y: edge[pl.ds(y, CHUNK), :],
        lambda y: inner[pl.ds(y, CHUNK), :],
        halo,
        curved,
        rows,
        put_edge,
        put_inner,
    )
    fetch([(edge, out.at[one]), (inner, out.at[two])], out_sems)


def make_final(message, pre, phase, side):
    layers, rows, depth = pre.shape
    plane = pltpu.VMEM((rows, depth), f32)
    return call(
        lambda *refs: final(side, *refs),
        jax.ShapeDtypeStruct(pre.shape, f32),
        ANY,
        [VMEM, ANY, ANY],
        [
            plane,
            plane,
            pltpu.VMEM((rows + 2 * PAD, depth), f32),
            pltpu.VMEM((rows, depth), bf16),
            pltpu.SemaphoreType.DMA((3,)),
            pltpu.SemaphoreType.DMA((2,)),
        ],
        cost(30 * rows * depth, 20 * rows * depth),
        aliases={1: 0},
    )(message, pre, phase)


def gather_rows(block, count):
    if count != 8:
        return lax.all_gather(block, "slab", axis=0)
    parts = block[None]
    for k in (1, 2, 4):
        parts = jnp.concatenate([parts, lax.ppermute(parts, "slab", [(i, i ^ k) for i in range(count)])])
    return parts


def total_over(g, axis):
    if lax.axis_size(axis) != 4:
        return lax.psum(g, axis)
    others = [lax.ppermute(g, axis, [(i, i ^ k) for i in range(4)]) for k in (1, 2, 3)]
    return (g + others[0]) + (others[1] + others[2])


def on_device(adjoint, phase, targets, owners, target_cell, rate_index, inflow_rates, wall_mask):
    state, phase = adjoint[0], phase[0]
    rows, depth = state.shape[1:]
    count = lax.axis_size("slab")
    position = lax.axis_index("slab")
    pairs = (
        [(i, i ^ 1) for i in range(count)],
        [(i, i + 1) for i in range(1, count - 1, 2)] + [(i + 1, i) for i in range(1, count - 1, 2)],
    )

    def send(v, side):
        return lax.ppermute(v, "slab", pairs[side])

    arrived = [send(make_first_message(state, side), side) for side in (0, 1)]

    cells = target_cell[0]
    digits = jnp.stack([owners[0, :, 0], cells // 256, cells % 256])
    digits = jnp.pad(digits, ((0, 13), (0, depth - digits.shape[1]))).astype(bf16)
    gathered = gather_rows(jnp.concatenate([targets[0], digits], axis=0), count)
    n = targets.shape[1]
    listed = gathered[:, :n].reshape(-1, depth)
    codes = gathered[:, n : n + 3, :n].astype(jnp.int32)
    index = jnp.where(codes[:, 0] == position, codes[:, 1] * 256 + codes[:, 2], -1).reshape(1, -1)

    pre = make_first_local(state, phase, inflow_rates, rate_index, count)
    halves, walls, later = [], [], []
    for side in (0, 1):
        half, message, wall = make_middle(arrived[side], pre, phase, side)
        halves.append(half)
        walls.append(send(wall, side))
        later.append(send(message, side))
    pre, wall, phase_wall = make_second_local(*halves, phase, inflow_rates, rate_index, index, listed, count)
    wall_gradient = total_over(make_walls(wall, phase_wall, *walls, wall_mask), "cond")
    for side in (0, 1):
        pre = make_final(later[side], pre, phase, side)
    return pre[None], wall_gradient


def solution(mesh):
    in_specs = (
        P("cond", "slab", None, None),
        P("cond", "slab", None, None),
        P("cond", "slab", None),
        P("cond", "slab", None),
        P("cond", "slab"),
        P("cond"),
        P(),
        P(None, "slab", None),
    )
    out_specs = (P("cond", "slab", None, None), P(None, "slab", None))
    return jax.shard_map(
        on_device, mesh=mesh, in_specs=in_specs, out_specs=out_specs, check_vma=False
    )
```

time: 108 us -> 47.5 us (0.44)
  the two profiles are of different devices: /device:TPU:0 before, /device:TPU:13 now
where the time goes in v1:
time: 47.5 us; the launch traced here: 47.2 us
  starting transfers between devices  17.2 us (36%)
  waiting for transfers between devices  12.9 us (27%)
  Pallas kernels  12.2 us (26%)
  local copies, waits for them, and re-layouts  1.95 us (4%)
  between operations  1.52 us (3%)
  other arithmetic  1.37 us (3%)
    ppermute x6, starting transfers between devices, send(): return lax.ppermute(v, 'slab', pairs[side])  12.1 us
    ppermute x3, waiting for transfers between devices, gather_rows(): lax.ppermute(parts, 'slab', [(i, i ^ k) for i in range(count)])  5.48 us
    ppermute x6, waiting for transfers between devices, send(): return lax.ppermute(v, 'slab', pairs[side])  4.78 us
    pallas_call x2, Pallas kernels, make_final(): call(lambda *refs: final(side, *refs), jax.ShapeDtypeStruct(pre.shape, f3...  4.17 us
    pallas_call x1, Pallas kernels, make_second_local(): call(lambda *refs: second_local(count, *refs), (jax.ShapeDtypeStruct((lay...  3.77 us
    ppermute x3, starting transfers between devices, gather_rows(): lax.ppermute(parts, 'slab', [(i, i ^ k) for i in range(count)])  2.95 us
    ppermute x3, waiting for transfers between devices, total_over(): lax.ppermute(g, axis, [(i, i ^ k) for i in range(4)])  2.63 us
    ppermute x3, starting transfers between devices, total_over(): lax.ppermute(g, axis, [(i, i ^ k) for i in range(4)])  2.19 us
  transfers between devices with their start and end apart: 12, of which 4 were waited for; matrix products, arithmetic and copies ran while one was open for 2% of the time, Pallas kernels for 22%

profile of v1, /device:TPU:13, one launch (start us, length us, event | category | flops | bytes accessed | tf_op | source)
XLA Modules:
  0.0 47.2 jit_solution(5459507608462128632)
XLA Ops:
  0.7 0.7 %fusion.13 = (bf16[1,32]{1,0:T(2,128)(2,1)S(1)}, bf16[1,32]{1,0:T(2,128)(2,1)S(1)}) fusion(s32[1,32]{1,0:T(1,128)} %param.12), kind=kLoop, calls=%fused_computation.33 | loop fusion | flops 672 | bytes 256 | tf_op jit(solution)/shard_map/convert.3
  1.4 0.3 collective-permute-start.4
  1.7 1.2 %copy-done.1 = f32[1,4,512,128]{3,2,1,0:T(8,128)S(1)} copy-done((f32[1,4,512,128]{3,2,1,0:T(8,128)S(1)}, f32[1,4,512,128]{3,2,1,0:T(8,128)}, u32[]{:S(2)}) %copy-start.1) | copy-done | bytes 1048600
  2.9 0.3 shard_map.95
  3.2 0.0 copy-start
  3.2 4.3 %collective-permute-start = (bf16[1024,128]{1,0:T(8,128)(2,1)S(1)}, bf16[1024,128]{1,0:T(8,128)(2,1)S(1)}, u32[]{:S(2)}, u32[]{:S(2)}) collective-permute-start(bf16[1024,128]{1,0:T(8,128)(2,1)S(1)} %shard_map.95), channel_id=1, source_target_pairs={{1,2},{3,4},{5,6},{2,1},{4,3},{6,5},{9,10},{11,12},{13,14},{10,9},... | collective-permute-start | bytes 786440 | tf_op jit(solution)/shard_map/ppermute | solution.py:422
  7.5 0.3 shard_map.98
  7.8 0.1 collective-permute-start.2
  7.9 0.0 collective-permute-done.4
  7.9 0.2 collective-permute-start.5
  8.1 5.5 %collective-permute-done.5 = bf16[2,48,128]{2,1,0:T(8,128)(2,1)S(1)} collective-permute-done((bf16[2,48,128]{2,1,0:T(8,128)(2,1)S(1)}, bf16[2,48,128]{2,1,0:T(8,128)(2,1)S(1)}, u32[]{:S(2)}, u32[]{:S(2)}) %collective-permute-start.5) | collective-permute-done | bytes 24608 | tf_op jit(solution)/shard_map/ppermute | solution.py:400
  13.6 2.4 %collective-permute-start.6 = (bf16[4,48,128]{2,1,0:T(8,128)(2,1)S(1)}, bf16[4,48,128]{2,1,0:T(8,128)(2,1)S(1)}, u32[]{:S(2)}, u32[]{:S(2)}) collective-permute-start(bf16[4,48,128]{2,1,0:T(8,128)(2,1)S(1)} %pad_maximum_fusion.3), channel_id=1, source_target_pairs={{0,4},{1,5},{2,6},{3,7},{4,0},{5,1},{6,2},{7,3},{8,12},{9,13},{10,... | collective-permute-start | bytes 147464 | tf_op jit(solution)/shard_map/ppermute | solution.py:400
  16.7 0.0 copy-start.4
  16.7 0.6 %copy-done.4 = f32[8]{0:T(128)S(1)} copy-done((f32[8]{0:T(128)S(1)}, f32[8]{0:T(128)}, u32[]{:S(2)}) %copy-start.4) | copy-done | bytes 56
  17.3 1.9 %shard_map.96.refs_1_ = f32[4,512,128]{2,1,0:T(8,128)S(1)} custom-call(f32[4,512,128]{2,1,0:T(8,128)S(1)} %bitcast.22, bf16[4,512,128]{2,1,0:T(8,128)(2,1)S(1)} %bitcast.14, f32[8]{0:T(128)S(1)} %copy-done.4, s32[1]{0:T(128)S(6)} %copy.14.refs_3_.refs_4_), custom_call_target="tpu_custom_call" | custom-call | flops 15728640 | bytes 2621440 | tf_op jit(solution)/shard_map/pallas_call | solution.py:175
  19.3 0.9 %shard_map.97 = (f32[2,512,128]{2,1,0:T(8,128)S(1)}, bf16[1024,128]{1,0:T(8,128)(2,1)S(1)}, f32[8,512]{1,0:T(8,128)S(1)}) custom-call(bf16[1024,128]{1,0:T(8,128)(2,1)S(1)} %collective-permute-done.refs_0_, f32[4,512,128]{2,1,0:T(8,128)S(1)} %shard_map.96.refs_1_, bf16[4,512,128]{2,1,0:T(8,128)(2,1)S(1)} %bitcast.15), custom_call_target="tpu_custom_call" | custom-call | flops 3932160 | bytes 1966080 | tf_op jit(solution)/shard_map/pallas_call | solution.py:252
  20.2 1.9 %collective-permute-start.1 = (bf16[1024,128]{1,0:T(8,128)(2,1)S(1)}, bf16[1024,128]{1,0:T(8,128)(2,1)S(1)}, u32[]{:S(2)}, u32[]{:S(2)}) collective-permute-start(bf16[1024,128]{1,0:T(8,128)(2,1)S(1)} %get-tuple-element.11), channel_id=1, source_target_pairs={{1,2},{3,4},{5,6},{2,1},{4,3},{6,5},{9,10},{11,12},{13,14},{10,9},... | collective-permute-start | bytes 786440 | tf_op jit(solution)/shard_map/ppermute | solution.py:422
  22.1 0.0 collective-permute-done.2.refs_0_
  22.1 0.9 %shard_map.99 = (f32[2,512,128]{2,1,0:T(8,128)S(1)}, bf16[1024,128]{1,0:T(8,128)(2,1)S(1)}, f32[8,512]{1,0:T(8,128)S(1)}) custom-call(bf16[1024,128]{1,0:T(8,128)(2,1)S(1)} %collective-permute-done.2.refs_0_, f32[4,512,128]{2,1,0:T(8,128)S(1)} %shard_map.96.refs_1_, bf16[4,512,128]{2,1,0:T(8,128)(2,1)S(1)} %bitcast.16), custom_call_target="tpu_custom_call" | custom-call | flops 3932160 | bytes 1966080 | tf_op jit(solution)/shard_map/pallas_call | solution.py:252
  23.0 0.4 collective-permute-start.3
  23.5 1.1 %collective-permute-start.7 = (f32[8,512]{1,0:T(8,128)S(1)}, f32[8,512]{1,0:T(8,128)S(1)}, u32[]{:S(2)}, u32[]{:S(2)}) collective-permute-start(f32[8,512]{1,0:T(8,128)S(1)} %get-tuple-element.18), channel_id=1, source_target_pairs={{0,1},{1,0},{2,3},{3,2},{4,5},{5,4},{6,7},{7,6},{8,9},{9,8},{10,11... | collective-permute-start | bytes 49160 | tf_op jit(solution)/shard_map/ppermute | solution.py:422
  24.6 4.2 %collective-permute-start.8 = (f32[8,512]{1,0:T(8,128)S(1)}, f32[8,512]{1,0:T(8,128)S(1)}, u32[]{:S(2)}, u32[]{:S(2)}) collective-permute-start(f32[8,512]{1,0:T(8,128)S(1)} %get-tuple-element.19), channel_id=1, source_target_pairs={{1,2},{3,4},{5,6},{2,1},{4,3},{6,5},{9,10},{11,12},{13,14},{10,9},... | collective-permute-start | bytes 49160 | tf_op jit(solution)/shard_map/ppermute | solution.py:422
  28.9 0.1 select_n.31.refs_5_
  29.0 3.8 %shard_map.100 = (f32[4,512,128]{2,1,0:T(8,128)}, f32[4,8,512]{2,1,0:T(8,128)S(1)}, f32[4,8,512]{2,1,0:T(8,128)S(1)}) custom-call(f32[2,512,128]{2,1,0:T(8,128)S(1)} %get-tuple-element.13.refs_0_, f32[2,512,128]{2,1,0:T(8,128)S(1)} %get-tuple-element.14.refs_1_, bf16[4,512,128]{2,1,0:T(8,128)(2,1)S(1)} %bitcast.17, f32[8]{0:T(128)S(1)} %copy-done.4, ...), custom_call_target="tpu_custom_call" | custom-call | flops 31457280 | bytes 2621440 | tf_op jit(solution)/shard_map/pallas_call | solution.py:306
  32.7 4.8 %collective-permute-done.7.from_a = f32[8,512]{1,0:T(8,128)S(1)} collective-permute-done((f32[8,512]{1,0:T(8,128)S(1)}, f32[8,512]{1,0:T(8,128)S(1)}, u32[]{:S(2)}, u32[]{:S(2)}) %collective-permute-start.7) | collective-permute-done | bytes 16416 | tf_op jit(solution)/shard_map/ppermute | solution.py:422
  37.6 1.3 %collective-permute-start.10 = (f32[2,4,512]{2,1,0:T(4,128)S(1)}, f32[2,4,512]{2,1,0:T(4,128)S(1)}, u32[]{:S(2)}, u32[]{:S(2)}) collective-permute-start(f32[2,4,512]{2,1,0:T(4,128)S(1)} %shard_map.103), channel_id=1, source_target_pairs={{0,16},{8,24},{16,0},{24,8},{1,17},{9,25},{17,1},{25,9},{2,18},{10... | collective-permute-start | bytes 49160 | tf_op jit(solution)/shard_map/ppermute | solution.py:407
  38.8 0.9 %collective-permute-start.11 = (f32[2,4,512]{2,1,0:T(4,128)S(1)}, f32[2,4,512]{2,1,0:T(4,128)S(1)}, u32[]{:S(2)}, u32[]{:S(2)}) collective-permute-start(f32[2,4,512]{2,1,0:T(4,128)S(1)} %shard_map.103), channel_id=1, source_target_pairs={{0,24},{8,16},{16,8},{24,0},{1,25},{9,17},{17,9},{25,1},{2,26},{10... | collective-permute-start | bytes 49160 | tf_op jit(solution)/shard_map/ppermute | solution.py:407
  39.8 0.5 collective-permute-done.10
  40.2 2.2 %collective-permute-done.11 = f32[2,4,512]{2,1,0:T(4,128)S(1)} collective-permute-done((f32[2,4,512]{2,1,0:T(4,128)S(1)}, f32[2,4,512]{2,1,0:T(4,128)S(1)}, u32[]{:S(2)}, u32[]{:S(2)}) %collective-permute-start.11) | collective-permute-done | bytes 16416 | tf_op jit(solution)/shard_map/ppermute | solution.py:407
  42.4 0.6 %add_add_fusion = f32[1,8,512]{2,1,0:T(8,128)} fusion(f32[1,8,512]{2,1,0:T(8,128)S(1)} %bitcast.27, f32[1,8,512]{2,1,0:T(8,128)S(1)} %bitcast.28, f32[1,8,512]{2,1,0:T(8,128)S(1)} %bitcast.24, f32[1,8,512]{2,1,0:T(8,128)S(1)} %bitcast.29), kind=kLoop, calls=%fused_computation.5 | loop fusion | flops 12288 | bytes 81920 | tf_op jit(solution)/shard_map/add | solution.py:408
  43.0 2.1 %shard_map.101.refs_1_ = f32[4,512,128]{2,1,0:T(8,128)} custom-call(bf16[1024,128]{1,0:T(8,128)(2,1)S(1)} %collective-permute-done.3.refs_0_, f32[4,512,128]{2,1,0:T(8,128)} %get-tuple-element.15.refs_1_, bf16[4,512,128]{2,1,0:T(8,128)(2,1)S(1)} %bitcast.18), custom_call_target="tpu_custom_call", output_to_operand_aliasing={{}: (1, {})} | custom-call | flops 1966080 | bytes 1310720 | tf_op jit(solution)/shard_map/pallas_call | solution.py:377
  45.1 2.1 %shard_map.102 = f32[4,512,128]{2,1,0:T(8,128)} custom-call(bf16[1024,128]{1,0:T(8,128)(2,1)S(1)} %collective-permute-done.1.refs_0_, f32[4,512,128]{2,1,0:T(8,128)} %shard_map.101.refs_1_, bf16[4,512,128]{2,1,0:T(8,128)(2,1)S(1)} %bitcast.19), custom_call_target="tpu_custom_call", output_to_operand_aliasing={{}: (1, {})} | custom-call | flops 1966080 | bytes 1310720 | tf_op jit(solution)/shard_map/pallas_call | solution.py:377
  (25 shorter events, 0.2 us)
Async XLA Ops:
  0.6 0.7 %copy-start.6 = (s32[1,32,1]{1,2,0:T(1,128)S(1)}, s32[1,32,1]{1,2,0:T(1,128)}, u32[]{:S(2)}) copy-start(s32[1,32,1]{1,2,0:T(1,128)} %param.11) | copy-start | bytes 388
  0.6 0.7 %copy-start.5 = (bf16[1,32,128]{2,1,0:T(8,128)(2,1)S(1)}, bf16[1,32,128]{2,1,0:T(8,128)(2,1)}, u32[]{:S(2)}) copy-start(bf16[1,32,128]{2,1,0:T(8,128)(2,1)} %param.10) | copy-start | bytes 24580
  1.4 6.5 %collective-permute-start.4 = (bf16[1,48,128]{2,1,0:T(8,128)(2,1)S(1)}, bf16[1,48,128]{2,1,0:T(8,128)(2,1)S(1)}, u32[]{:S(2)}, u32[]{:S(2)}) collective-permute-start(bf16[1,48,128]{2,1,0:T(8,128)(2,1)S(1)} %maximum_bitcast_fusion), channel_id=1, source_target_pairs={{0,1},{1,0},{2,3},{3,2},{4,5},{5,4},{6,7},{7,6},{8,9},{9,8},{10,11... | collective-permute-start | bytes 36872 | tf_op jit(solution)/shard_map/ppermute | solution.py:400
  1.7 1.2 %copy-start.1 = (f32[1,4,512,128]{3,2,1,0:T(8,128)S(1)}, f32[1,4,512,128]{3,2,1,0:T(8,128)}, u32[]{:S(2)}) copy-start(f32[1,4,512,128]{3,2,1,0:T(8,128)} %param.8) | copy-start | bytes 3145732
  2.9 13.8 %copy-start.2 = (f32[1,4,512,128]{3,2,1,0:T(8,128)S(1)}, f32[1,4,512,128]{3,2,1,0:T(8,128)}, u32[]{:S(2)}) copy-start(f32[1,4,512,128]{3,2,1,0:T(8,128)} %param.8) | copy-start | bytes 3145732
  3.2 13.5 %copy-start = (bf16[1,4,512,128]{3,2,1,0:T(8,128)(2,1)S(1)}, bf16[1,4,512,128]{3,2,1,0:T(8,128)(2,1)}, u32[]{:S(2)}) copy-start(bf16[1,4,512,128]{3,2,1,0:T(8,128)(2,1)} %param.9) | copy-start | bytes 1572868
  3.2 16.1 %collective-permute-start = (bf16[1024,128]{1,0:T(8,128)(2,1)S(1)}, bf16[1024,128]{1,0:T(8,128)(2,1)S(1)}, u32[]{:S(2)}, u32[]{:S(2)}) collective-permute-start(bf16[1024,128]{1,0:T(8,128)(2,1)S(1)} %shard_map.95), channel_id=1, source_target_pairs={{1,2},{3,4},{5,6},{2,1},{4,3},{6,5},{9,10},{11,12},{13,14},{10,9},... | collective-permute-start | bytes 786440 | tf_op jit(solution)/shard_map/ppermute | solution.py:422
  7.8 14.3 %collective-permute-start.2 = (bf16[1024,128]{1,0:T(8,128)(2,1)S(1)}, bf16[1024,128]{1,0:T(8,128)(2,1)S(1)}, u32[]{:S(2)}, u32[]{:S(2)}) collective-permute-start(bf16[1024,128]{1,0:T(8,128)(2,1)S(1)} %shard_map.98), channel_id=1, source_target_pairs={{0,1},{1,0},{2,3},{3,2},{4,5},{5,4},{6,7},{7,6},{8,9},{9,8},{10,11... | collective-permute-start | bytes 786440 | tf_op jit(solution)/shard_map/ppermute | solution.py:422
  7.9 5.7 %collective-permute-start.5 = (bf16[2,48,128]{2,1,0:T(8,128)(2,1)S(1)}, bf16[2,48,128]{2,1,0:T(8,128)(2,1)S(1)}, u32[]{:S(2)}, u32[]{:S(2)}) collective-permute-start(bf16[2,48,128]{2,1,0:T(8,128)(2,1)S(1)} %pad_maximum_fusion.4), channel_id=1, source_target_pairs={{0,2},{1,3},{2,0},{3,1},{4,6},{5,7},{6,4},{7,5},{8,10},{9,11},{10,... | collective-permute-start | bytes 73736 | tf_op jit(solution)/shard_map/ppermute | solution.py:400
  13.6 15.2 %collective-permute-start.6 = (bf16[4,48,128]{2,1,0:T(8,128)(2,1)S(1)}, bf16[4,48,128]{2,1,0:T(8,128)(2,1)S(1)}, u32[]{:S(2)}, u32[]{:S(2)}) collective-permute-start(bf16[4,48,128]{2,1,0:T(8,128)(2,1)S(1)} %pad_maximum_fusion.3), channel_id=1, source_target_pairs={{0,4},{1,5},{2,6},{3,7},{4,0},{5,1},{6,2},{7,3},{8,12},{9,13},{10,... | collective-permute-start | bytes 147464 | tf_op jit(solution)/shard_map/ppermute | solution.py:400
  16.7 0.7 %copy-start.4 = (f32[8]{0:T(128)S(1)}, f32[8]{0:T(128)}, u32[]{:S(2)}) copy-start(f32[8]{0:T(128)} %refs_3_.2) | copy-start | bytes 100
  20.2 24.9 %collective-permute-start.1 = (bf16[1024,128]{1,0:T(8,128)(2,1)S(1)}, bf16[1024,128]{1,0:T(8,128)(2,1)S(1)}, u32[]{:S(2)}, u32[]{:S(2)}) collective-permute-start(bf16[1024,128]{1,0:T(8,128)(2,1)S(1)} %get-tuple-element.11), channel_id=1, source_target_pairs={{1,2},{3,4},{5,6},{2,1},{4,3},{6,5},{9,10},{11,12},{13,14},{10,9},... | collective-permute-start | bytes 786440 | tf_op jit(solution)/shard_map/ppermute | solution.py:422
  23.0 20.0 %collective-permute-start.3 = (bf16[1024,128]{1,0:T(8,128)(2,1)S(1)}, bf16[1024,128]{1,0:T(8,128)(2,1)S(1)}, u32[]{:S(2)}, u32[]{:S(2)}) collective-permute-start(bf16[1024,128]{1,0:T(8,128)(2,1)S(1)} %get-tuple-element.12), channel_id=1, source_target_pairs={{0,1},{1,0},{2,3},{3,2},{4,5},{5,4},{6,7},{7,6},{8,9},{9,8},{10,11... | collective-permute-start | bytes 786440 | tf_op jit(solution)/shard_map/ppermute | solution.py:422
  23.5 14.1 %collective-permute-start.7 = (f32[8,512]{1,0:T(8,128)S(1)}, f32[8,512]{1,0:T(8,128)S(1)}, u32[]{:S(2)}, u32[]{:S(2)}) collective-permute-start(f32[8,512]{1,0:T(8,128)S(1)} %get-tuple-element.18), channel_id=1, source_target_pairs={{0,1},{1,0},{2,3},{3,2},{4,5},{5,4},{6,7},{7,6},{8,9},{9,8},{10,11... | collective-permute-start | bytes 49160 | tf_op jit(solution)/shard_map/ppermute | solution.py:422
  24.6 13.0 %collective-permute-start.8 = (f32[8,512]{1,0:T(8,128)S(1)}, f32[8,512]{1,0:T(8,128)S(1)}, u32[]{:S(2)}, u32[]{:S(2)}) collective-permute-start(f32[8,512]{1,0:T(8,128)S(1)} %get-tuple-element.19), channel_id=1, source_target_pairs={{1,2},{3,4},{5,6},{2,1},{4,3},{6,5},{9,10},{11,12},{13,14},{10,9},... | collective-permute-start | bytes 49160 | tf_op jit(solution)/shard_map/ppermute | solution.py:422
  29.0 8.6 %copy-start.3 = (s32[2,4,512]{2,1,0:T(4,128)S(1)}, s32[2,4,512]{2,1,0:T(4,128)}, u32[]{:S(2)}) copy-start(s32[2,4,512]{2,1,0:T(4,128)} %mask.1) | copy-start | bytes 49156
  37.6 2.7 %collective-permute-start.10 = (f32[2,4,512]{2,1,0:T(4,128)S(1)}, f32[2,4,512]{2,1,0:T(4,128)S(1)}, u32[]{:S(2)}, u32[]{:S(2)}) collective-permute-start(f32[2,4,512]{2,1,0:T(4,128)S(1)} %shard_map.103), channel_id=1, source_target_pairs={{0,16},{8,24},{16,0},{24,8},{1,17},{9,25},{17,1},{25,9},{2,18},{10... | collective-permute-start | bytes 49160 | tf_op jit(solution)/shard_map/ppermute | solution.py:407
  38.8 3.5 %collective-permute-start.11 = (f32[2,4,512]{2,1,0:T(4,128)S(1)}, f32[2,4,512]{2,1,0:T(4,128)S(1)}, u32[]{:S(2)}, u32[]{:S(2)}) collective-permute-start(f32[2,4,512]{2,1,0:T(4,128)S(1)} %shard_map.103), channel_id=1, source_target_pairs={{0,24},{8,16},{16,8},{24,0},{1,25},{9,17},{17,9},{25,1},{2,26},{10... | collective-permute-start | bytes 49160 | tf_op jit(solution)/shard_map/ppermute | solution.py:407
  39.8 2.6 %collective-permute-start.9 = (f32[2,4,512]{2,1,0:T(4,128)S(1)}, f32[2,4,512]{2,1,0:T(4,128)S(1)}, u32[]{:S(2)}, u32[]{:S(2)}) collective-permute-start(f32[2,4,512]{2,1,0:T(4,128)S(1)} %shard_map.103), channel_id=1, source_target_pairs={{0,8},{8,0},{16,24},{24,16},{1,9},{9,1},{17,25},{25,17},{2,10},{10... | collective-permute-start | bytes 49160 | tf_op jit(solution)/shard_map/ppermute | solution.py:407

commit v2 on v0

v2 whole, which is shorter than its diff:
```python
import jax
import jax.numpy as jnp
from jax import lax
from jax.experimental import pallas as pl
from jax.experimental.pallas import tpu as pltpu
from jax.sharding import PartitionSpec as P

mobility_step = 0.02
stiffness_step = 0.01
transport_step = 0.125
wall_weight = 0.25

f32 = jnp.float32
bf16 = jnp.bfloat16
CHUNK = 64
LARGE = 56
PAD = 8
ANY = pl.BlockSpec(memory_space=pl.ANY)
HBM = pl.BlockSpec(memory_space=pltpu.HBM)
VMEM = pl.BlockSpec(memory_space=pltpu.VMEM)
SMEM = pl.BlockSpec(memory_space=pltpu.SMEM)


def cost(flops, nbytes):
    return pl.CostEstimate(flops=10**10, bytes_accessed=10**8, transcendentals=0)


def call(kernel, outs, out_specs, in_specs, scratch, estimate, aliases=None, limit=12):
    return pl.pallas_call(
        kernel,
        out_shape=outs,
        out_specs=out_specs,
        in_specs=in_specs,
        scratch_shapes=scratch,
        input_output_aliases=aliases or {},
        cost_estimate=estimate,
        compiler_params=pltpu.CompilerParams(vmem_limit_bytes=limit * 1024 * 1024),
    )


def starts(rows):
    return range(0, rows, CHUNK)


def read(layer, y, shift=0):
    ref, lead = layer
    return ref[(*lead, pl.ds(PAD + y + shift, CHUNK), slice(None))]


def write(layer, y, v):
    ref, lead = layer
    ref[(*lead, pl.ds(PAD + y, CHUNK), slice(None))] = v


def z_sum(v):
    depth = v.shape[1]
    lane = lax.broadcasted_iota(jnp.int32, v.shape, 1)
    below = jnp.where(lane == 0, 0.0, pltpu.roll(v, 1, 1))
    above = jnp.where(lane == depth - 1, 0.0, pltpu.roll(v, depth - 1, 1))
    return below + above


def plane_part(layer, y):
    v = read(layer, y)
    return read(layer, y, 1) + read(layer, y, -1) + z_sum(v) - 6.0 * v


def clear_margins(layer):
    ref, lead = layer
    zero = jnp.zeros((PAD, ref.shape[-1]), f32)
    ref[(*lead, pl.ds(0, PAD), slice(None))] = zero
    ref[(*lead, pl.ds(ref.shape[-2] - PAD, PAD), slice(None))] = zero


def is_odd():
    return lax.rem(lax.axis_index("slab"), 2) == 1


def stored(d, layers):
    return jnp.where(is_odd(), d, layers - 1 - d)


def has_partner(count):
    position = lax.axis_index("slab")
    above = position < count - 1
    below = position > 0
    odd = is_odd()
    flags = jnp.where(odd, below, above), jnp.where(odd, above, below)
    return [jnp.where(f, 1.0, 0.0).astype(f32) for f in flags]


def copy_all(pairs, sems):
    copies = [pltpu.make_async_copy(s, d, sems.at[i]) for i, (s, d) in enumerate(pairs)]
    for c in copies:
        c.start()
    return copies


def write_message(near, far, missing, out, rows):
    clear_margins(missing)
    for y in starts(rows):
        v = read(near, y)
        rounded = v.astype(bf16)
        out[pl.ds(y, CHUNK), :] = rounded
        write(missing, y, v - rounded.astype(f32))
    for y in starts(rows):
        out[pl.ds(rows + y, CHUNK), :] = (read(far, y) + 2.0 * plane_part(missing, y)).astype(bf16)


def curvature_of(p):
    return 3.0 * p * p - 1.0


def local_step(state, first, phase, row, count, emit):
    layers = len(state)
    rows = phase.shape[1]
    depth = phase.shape[2]
    side_a, side_b = has_partner(count)
    transport = row[0:1, :]
    for d in range(layers):
        for y in starts(rows):
            lap = plane_part(state[d], y)
            if d > 0:
                lap = lap + read(state[d - 1], y)
            if d < layers - 1:
                lap = lap + read(state[d + 1], y)
            write(first[d], y, lap)
    for d in range(layers):
        at = stored(d, layers)
        for y in starts(rows):
            v = read(state[d], y)
            second = plane_part(first[d], y)
            second = second + (read(first[d - 1], y) if d > 0 else side_a * v)
            second = second + (read(first[d + 1], y) if d < layers - 1 else side_b * v)
            p = phase[at, pl.ds(y, CHUNK), :].astype(f32)
            moved = read(state[d], y, 1) - read(state[d], y, -1)
            stepped = (
                v
                + mobility_step * curvature_of(p) * read(first[d], y)
                - stiffness_step * second
                + transport * moved
            )
            emit(d, y, v, stepped)


def padded(rows, depth, layers=None):
    lead = () if layers is None else (layers,)
    return pltpu.VMEM((*lead, rows + 2 * PAD, depth), f32)


def layers_of(ref):
    return [(ref, (d,)) for d in range(ref.shape[0])]


def first_message(adjoint, targets, owners, cells, out, near, far, missing, digits, owner, cell, sems):
    layers, rows, depth = adjoint.shape
    n = targets.shape[0]
    pairs = [(adjoint.at[stored(d, layers)], ref.at[pl.ds(PAD, rows)]) for d, ref in ((0, near), (1, far))]
    if out.shape[0] > 2 * rows:
        pairs += [(targets, out.at[pl.ds(2 * rows, n)]), (owners, owner), (cells, cell)]
    copies = copy_all(pairs, sems)
    if out.shape[0] > 2 * rows:
        digits[...] = jnp.zeros(digits.shape, f32)
        for c in copies[3:]:
            c.wait()
        digits[0:1, 0:n] = owner[...].astype(f32)
        digits[1:2, 0:n] = (cell[...] >> 8).astype(f32)
        digits[2:3, 0:n] = (cell[...] & 255).astype(f32)
        out[pl.ds(2 * rows + n, 16), :] = digits[...].astype(bf16)
    for c in copies[:3]:
        c.wait()
    write_message((near, ()), (far, ()), (missing, ()), out, rows)


def make_first_message(adjoint, targets, owners, cells, extra):
    layers, rows, depth = adjoint.shape
    row = pltpu.VMEM(owners.shape, jnp.int32)
    return call(
        first_message,
        jax.ShapeDtypeStruct((2 * rows + extra, depth), bf16),
        VMEM,
        [ANY] * 4,
        [padded(rows, depth)] * 3 + [pltpu.VMEM((16, depth), f32), row, row, pltpu.SemaphoreType.DMA((5,))],
        cost(20 * rows * depth, 12 * rows * depth),
        limit=LARGE,
    )(adjoint, targets, owners, cells)


def transport_row(inflow, depth):
    lane = lax.broadcasted_iota(jnp.int32, (8, depth), 1)
    height = (lane.astype(f32) + 0.5) / depth
    return (transport_step * inflow) * (4.0 * height * (1.0 - height))


def first_local(count, adjoint, phase, rates, choice, mask, after, out, message, row, masked, state, first, missing, sems):
    layers, rows, depth = adjoint.shape
    copies = copy_all(
        [(adjoint.at[stored(d, layers)], state.at[d, pl.ds(PAD, rows)]) for d in range(layers)], sems
    )
    row[...] = transport_row(rates[choice[0]], depth)
    masked[...] = wall_weight * mask[...].astype(f32)
    for d in range(layers):
        clear_margins((state, (d,)))
        clear_margins((first, (d,)))
    own = layers_of(state)
    for c in copies:
        c.wait()
    write_message(own[-1], own[-2], (missing, ()), message, rows)

    def emit(d, y, v, stepped):
        out[d, pl.ds(y, CHUNK), :] = stepped

    local_step(own, layers_of(first), phase, row, count, emit)


def make_first_local(adjoint, phase, rates, choice, mask, after, count):
    layers, rows, depth = adjoint.shape
    return call(
        lambda *refs: first_local(count, *refs),
        (
            jax.ShapeDtypeStruct(adjoint.shape, f32),
            jax.ShapeDtypeStruct((2 * rows, depth), bf16),
            jax.ShapeDtypeStruct((8, depth), f32),
            jax.ShapeDtypeStruct(mask.shape, f32),
        ),
        (VMEM,) * 4,
        [ANY, VMEM, SMEM, SMEM, VMEM, ANY],
        [padded(rows, depth, layers)] * 2 + [padded(rows, depth), pltpu.SemaphoreType.DMA((layers,))],
        cost(80 * layers * rows * depth, 12 * layers * rows * depth),
    )(adjoint, phase, rates, choice, mask, after)


def add_halo(message, edge, inner, halo, phase, at, rows, put_edge, put_inner):
    clear_margins(halo)
    for y in starts(rows):
        near = message[pl.ds(y, CHUNK), :].astype(f32)
        write(halo, y, near)
        put_inner(y, inner(y) - stiffness_step * near)
    for y in starts(rows):
        near = read(halo, y)
        far = message[pl.ds(rows + y, CHUNK), :].astype(f32)
        curvature = curvature_of(phase[at, pl.ds(y, CHUNK), :].astype(f32))
        both = far + 2.0 * plane_part(halo, y)
        put_edge(y, edge(y) + mobility_step * curvature * near - stiffness_step * both)


def wall_rows(v, first_row):
    depth = v.shape[1]
    row = lax.broadcasted_iota(jnp.int32, (8, depth), 0) - first_row
    lane = lax.broadcasted_iota(jnp.int32, (8, depth), 1)
    pick = ((row == 0) & (lane == 0)) | ((row == 1) & (lane == depth - 1))
    pick = jnp.where(pick, 1.0, 0.0).astype(bf16)

    def part(w):
        return lax.dot_general(pick, w, (((1,), (1,)), ((), ())), preferred_element_type=f32)

    if v.dtype == bf16:
        return part(v)
    high = v.astype(bf16)
    rest = v - high.astype(f32)
    middle = rest.astype(bf16)
    low = (rest - middle.astype(f32)).astype(bf16)
    return part(high) + part(middle) + part(low)


def middle(side, message, pre, phase, *refs):
    blocks, refs = refs[: 1 + 2 * side], refs[1 + 2 * side :]
    layers, rows, depth = pre.shape
    one, two = (0, 1) if side == 0 else (layers - 1, layers - 2)
    if side == 0:
        out, sent, block, halo, missing = refs
        if message.shape[0] > 2 * rows:
            block[0] = blocks[0][pl.ds(2 * rows, block.shape[1]), :]
            block[1] = message[pl.ds(2 * rows, block.shape[1]), :]
    else:
        out, wall, block, halo = refs
        for i in range(4):
            block[i] = blocks[i // 2][i % 2]
    edge, inner = layers_of(out)
    clear_margins(edge)
    clear_margins(inner)
    add_halo(
        message,
        lambda y: pre[one, pl.ds(y, CHUNK), :],
        lambda y: pre[two, pl.ds(y, CHUNK), :],
        (halo, ()),
        phase,
        stored(one, layers),
        rows,
        lambda y, v: write(edge, y, v),
        lambda y, v: write(inner, y, v),
    )
    if side == 0:
        write_message(edge, inner, (missing, ()), sent, rows)
    for y in range(0, rows, 128):
        both = [read(inner, y + k) + 2.0 * plane_part(edge, y + k) for k in range(0, 128, CHUNK)]
        near = [read(edge, y + k) for k in range(0, 128, CHUNK)]
        wall_part = wall_rows(jnp.concatenate(near), 0) + wall_rows(jnp.concatenate(both), 2)
        if side == 0:
            high = wall_part.astype(bf16)
            low = (wall_part - high.astype(f32)).astype(bf16)
            sent[pl.ds(2 * rows + y // 8, 16), :] = jnp.concatenate([high.astype(f32), low.astype(f32)]).astype(bf16)
        else:
            wall[:, pl.ds(y, 128)] = wall_part


def make_middle(message, pre, phase, side, extra, *more):
    layers, rows, depth = pre.shape
    outs = [jax.ShapeDtypeStruct((2, rows + 2 * PAD, depth), f32)]
    scratch = [padded(rows, depth)]
    if side == 1:
        outs.append(jax.ShapeDtypeStruct((8, rows), f32))
        outs.append(jax.ShapeDtypeStruct((4, extra, depth), bf16))
    else:
        outs.append(jax.ShapeDtypeStruct((2 * rows + rows // 8, depth), bf16))
        outs.append(jax.ShapeDtypeStruct((2, extra, depth), bf16))
        scratch.append(padded(rows, depth))
    return call(
        lambda *refs: middle(side, *refs),
        tuple(outs),
        (VMEM,) * len(outs),
        [VMEM, VMEM, VMEM] + ([VMEM, VMEM, ANY] if side else [VMEM]),
        scratch,
        cost(60 * rows * depth, 30 * rows * depth),
    )(message, pre, phase, *more)


def second_local(count, side_a, side_b, phase, row, out, wall, phase_wall, message, first, missing):
    layers, rows, depth = out.shape
    own = layers_of(side_a) + layers_of(side_b)[::-1]
    for d in range(layers):
        clear_margins((first, (d,)))
    write_message(own[-1], own[-2], (missing, ()), message, rows)
    held = []

    def emit(d, y, v, stepped):
        out[d, pl.ds(y, CHUNK), :] = stepped
        held.append(v + stepped)
        if len(held) * CHUNK == 128:
            start = y + CHUNK - 128
            wall[d, :, pl.ds(start, 128)] = wall_rows(jnp.concatenate(held), 0)
            phase_wall[d, :, pl.ds(start, 128)] = wall_rows(phase[stored(d, layers), pl.ds(start, 128), :], 0)
            held.clear()

    local_step(own, layers_of(first), phase, row, count, emit)


def make_second_local(side_a, side_b, phase, row, count):
    layers, rows, depth = phase.shape
    return call(
        lambda *refs: second_local(count, *refs),
        (
            jax.ShapeDtypeStruct((layers, rows, depth), f32),
            jax.ShapeDtypeStruct((layers, 8, rows), f32),
            jax.ShapeDtypeStruct((layers, 8, rows), f32),
            jax.ShapeDtypeStruct((2 * rows, depth), bf16),
        ),
        (VMEM,) * 4,
        [VMEM] * 4,
        [padded(rows, depth, layers), padded(rows, depth)],
        cost(80 * layers * rows * depth, 12 * layers * rows * depth),
    )(side_a, side_b, phase, row)


def injection(phase, *refs):
    blocks, (out, index, rhs) = refs[:-3], refs[-3:]
    layers, rows, depth = out.shape
    n = blocks[0].shape[1] - 16
    position = lax.axis_index("slab").astype(f32)
    rhs[:, :depth] = jnp.ones((rhs.shape[0], depth), bf16)
    at = 0
    for block in blocks:
        for i in range(block.shape[0]):
            rhs[pl.ds(at, n), depth:] = block[i, pl.ds(0, n), :]
            digits = block[i, pl.ds(n, 16), :].astype(f32)
            cell = jnp.where(digits[0:1] == position, digits[1:2] * 256.0 + digits[2:3], -1.0)
            index[0:1, pl.ds(at, n)] = cell[:, :n].astype(jnp.int32)
            at += n
    for d in range(layers):
        at = stored(d, layers)
        for y in range(0, rows, 128):
            cell = lax.broadcasted_iota(jnp.int32, (128, index.shape[1]), 0) + (at * rows + y)
            here = jnp.where(cell == index[0:1, :], 1.0, 0.0).astype(bf16)
            added = jnp.dot(here, rhs[...], preferred_element_type=f32)
            p = phase[at, pl.ds(y, 128), :].astype(f32)
            out[d, pl.ds(y, 128), :] = added[:, :depth] * p - added[:, depth:]


def make_injection(phase, *blocks):
    layers, rows, depth = phase.shape
    total = sum(b.shape[0] * (b.shape[1] - 16) for b in blocks)
    return call(
        injection,
        jax.ShapeDtypeStruct((layers, rows, depth), f32),
        VMEM,
        [VMEM] * (1 + len(blocks)),
        [pltpu.VMEM((8, total), jnp.int32), pltpu.VMEM((total, 2 * depth), bf16)],
        cost(40 * layers * rows * depth, 6 * layers * rows * depth),
    )(phase, *blocks)


def wall_kernel(wall, phase_wall, message, from_b, mask, after, out, from_a):
    layers = wall.shape[0]
    rows = wall.shape[2]
    for y in range(0, rows, 128):
        both = message[pl.ds(2 * rows + y // 8, 16), :].astype(f32)
        from_a[:, pl.ds(y, 128)] = both[:8] + both[8:]
    odd = is_odd()
    terms = []
    for d in range(layers):
        p = phase_wall[d, :2, :]
        w = wall[d, :2, :]
        for halo, off in ((from_a, d), (from_b, layers - 1 - d)):
            if off == 0:
                w = w + mobility_step * curvature_of(p) * halo[:2] - stiffness_step * halo[2:4]
            elif off == 1:
                w = w - stiffness_step * halo[:2]
        terms.append((1.0 - p * p) * w)
    for l in range(layers):
        out[:, l, :] = mask[:, l, :] * jnp.where(odd, terms[l], terms[layers - 1 - l])


def make_walls(wall, phase_wall, message, from_b, mask, after):
    return call(
        wall_kernel,
        jax.ShapeDtypeStruct(mask.shape, f32),
        VMEM,
        [VMEM] * 5 + [ANY],
        [pltpu.VMEM(from_b.shape, f32)],
        cost(40 * mask.size, 20 * mask.size),
    )(wall, phase_wall, message, from_b, mask, after)


def final(side, message, pre, added, phase, *refs):
    if side == 0:
        out, edge, inner, halo, sems = refs
    else:
        walls = refs[1:-6]
        out, total, edge, inner, halo, sems = refs[-6:]
        if len(walls) == 4:
            total[...] = (walls[0][...] + walls[1][...]) + (walls[2][...] + walls[3][...])
        else:
            total[...] = walls[0][...]
    layers, rows, depth = pre.shape
    one, two = (0, 1) if side == 0 else (layers - 1, layers - 2)
    half = rows // 2
    copies = []

    def send(ref, layer, start, slot):
        c = pltpu.make_async_copy(
            ref.at[pl.ds(start, half)], out.at[stored(layer, layers), pl.ds(start, half)], sems.at[slot]
        )
        c.start()
        copies.append(c)

    def put_inner(y, v):
        inner[pl.ds(y, CHUNK), :] = v + added[two, pl.ds(y, CHUNK), :]
        if (y + CHUNK) % half == 0:
            send(inner, two, y + CHUNK - half, len(copies))

    def put_edge(y, v):
        edge[pl.ds(y, CHUNK), :] = v + added[one, pl.ds(y, CHUNK), :]
        if (y + CHUNK) % half == 0:
            send(edge, one, y + CHUNK - half, len(copies))

    add_halo(
        message,
        lambda y: pre[one, pl.ds(y, CHUNK), :],
        lambda y: pre[two, pl.ds(y, CHUNK), :],
        (halo, ()),
        phase,
        stored(one, layers),
        rows,
        put_edge,
        put_inner,
    )
    for c in copies:
        c.wait()


def make_final(message, pre, added, phase, side, out=None, walls=()):
    layers, rows, depth = pre.shape
    plane = pltpu.VMEM((rows, depth), f32)
    whole = jax.ShapeDtypeStruct(pre.shape, f32)
    more = [] if side == 0 else [out, *walls]
    return call(
        lambda *refs: final(side, *refs),
        whole if side == 0 else (whole, jax.ShapeDtypeStruct(walls[0].shape, f32)),
        ANY if side == 0 else (ANY, VMEM),
        [VMEM] * 4 + ([] if side == 0 else [ANY] + [VMEM] * len(walls)),
        [plane, plane, padded(rows, depth), pltpu.SemaphoreType.DMA((4,))],
        cost(30 * rows * depth, 20 * rows * depth),
        aliases={} if side == 0 else {4: 0},
    )(message, pre, added, phase, *more)


def parts_over(g, axis):
    if lax.axis_size(axis) != 4:
        return [lax.psum(g, axis)]
    return [g] + [lax.ppermute(g, axis, [(i, i ^ k) for i in range(4)]) for k in (1, 2, 3)]


def row_block(targets, owners, cells):
    n, depth = targets.shape
    digits = jnp.concatenate([owners, cells // 256, cells % 256])
    digits = jnp.pad(digits, ((0, 13), (0, depth - n))).astype(bf16)
    return jnp.concatenate([targets, digits], axis=0)


def on_device(adjoint, phase, targets, owners, target_cell, rate_index, inflow_rates, wall_mask):
    state, phase, targets = adjoint[0], phase[0], targets[0]
    owners = owners.reshape(target_cell.shape)
    layers, rows, depth = state.shape
    n = targets.shape[0]
    count = lax.axis_size("slab")
    pairs = (
        [(i, i ^ 1) for i in range(count) if i ^ 1 < count],
        [(i, i + 1) for i in range(1, count - 1, 2)] + [(i + 1, i) for i in range(1, count - 1, 2)],
    )
    doubling = count == 8

    def send(v, side):
        return lax.ppermute(v, "slab", pairs[side])

    message = make_first_message(state, targets, owners, target_cell, n + 16 if doubling else 0)
    from_a = send(message, 0)
    pre, message_b, row, mask = make_first_local(
        state, phase, inflow_rates, rate_index, wall_mask, message, count
    )
    from_b = send(message_b, 1)
    half_a, message_a, block = make_middle(from_a, pre, phase, 0, n + 16, message)
    later_a = send(message_a, 0)
    beside = lax.ppermute(block, "slab", [(i, i ^ 2) for i in range(count)]) if doubling else block
    half_b, wall_b, block = make_middle(from_b, pre, phase, 1, n + 16, block, beside, message_a)
    wall_b = send(wall_b, 1)
    if doubling:
        blocks = [block, lax.ppermute(block, "slab", [(i, i ^ 4) for i in range(count)])]
    else:
        blocks = [lax.all_gather(row_block(targets, owners, target_cell), "slab", axis=0)]
    pre, wall, phase_wall, message_b = make_second_local(half_a, half_b, phase, row, count)
    later_b = send(message_b, 1)
    walls = parts_over(make_walls(wall, phase_wall, later_a, wall_b, mask, blocks[-1]), "cond")
    added = make_injection(phase, *blocks)
    out = make_final(later_a, pre, added, phase, 0)
    out, wall_gradient = make_final(later_b, pre, added, phase, 1, out, walls)
    return out[None], wall_gradient


def solution(mesh):
    in_specs = (
        P("cond", "slab", None, None),
        P("cond", "slab", None, None),
        P("cond", "slab", None),
        P("cond", "slab", None),
        P("cond", "slab"),
        P("cond"),
        P(),
        P(None, "slab", None),
    )
    out_specs = (P("cond", "slab", None, None), P(None, "slab", None))
    return jax.shard_map(
        on_device, mesh=mesh, in_specs=in_specs, out_specs=out_specs, check_vma=False
    )
```

time: 108 us -> 39 us (0.36)
  the two profiles are of different devices: /device:TPU:0 before, /device:TPU:4 now
where the time goes in v2:
time: 39 us; the launch traced here: 38.7 us
  starting transfers between devices  18 us (46%)
  Pallas kernels  10.2 us (26%)
  waiting for transfers between devices  7.46 us (19%)
  local copies, waits for them, and re-layouts  1.59 us (4%)
  between operations  1.46 us (4%)
    ppermute x5, starting transfers between devices, send(): return lax.ppermute(v, 'slab', pairs[side])  11.9 us
    ppermute x5, waiting for transfers between devices, send(): return lax.ppermute(v, 'slab', pairs[side])  7.44 us
    ppermute x1, starting transfers between devices, on_device(): lax.ppermute(block, 'slab', [(i, i ^ 4) for i in range(count)])  2.65 us
    pallas_call x2, Pallas kernels, make_final(): call(lambda *refs: final(side, *refs), whole if side == 0 else (whole, ja...  2.5 us
    pallas_call x1, Pallas kernels, make_first_message(): call(first_message, jax.ShapeDtypeStruct((2 * rows + extra, depth), bf16)...  2.11 us
    pallas_call x1, Pallas kernels, make_first_local(): call(lambda *refs: first_local(count, *refs), (jax.ShapeDtypeStruct(adjoi...  2.05 us
    ppermute x3, starting transfers between devices, parts_over(): lax.ppermute(g, axis, [(i, i ^ k) for i in range(4)])  1.92 us
    pallas_call x1, Pallas kernels, make_second_local(): call(lambda *refs: second_local(count, *refs), (jax.ShapeDtypeStruct((lay...  1.67 us
  transfers between devices with their start and end apart: 10, of which 2 were waited for; matrix products, arithmetic and copies ran while one was open for 0% of the time, Pallas kernels for 17%

profile of v2, /device:TPU:4, one launch (start us, length us, event | category | flops | bytes accessed | tf_op | source)
XLA Modules:
  0.0 38.7 jit_solution(3851119007583921764)
XLA Ops:
  0.6 0.0 copy-start
  0.7 2.1 %shard_map.95.refs_5_.refs_3_ = bf16[1072,128]{1,0:T(8,128)(2,1)} custom-call(f32[4,512,128]{2,1,0:T(8,128)} %bitcast.5, bf16[32,128]{1,0:T(8,128)(2,1)} %bitcast.14, s32[1,32]{1,0:T(1,128)} %bitcast.15, s32[1,32]{1,0:T(1,128)} %cells.1), custom_call_target="tpu_custom_call" | custom-call | flops 10000000000 | bytes 100000000 | tf_op jit(solution)/shard_map/pallas_call | solution.py:178
  2.8 0.1 collective-permute-start
  3.5 0.0 copy-start.5
  3.6 0.6 %copy-done.5 = f32[8]{0:T(128)S(1)} copy-done((f32[8]{0:T(128)S(1)}, f32[8]{0:T(128)}, u32[]{:S(2)}) %copy-start.5) | copy-done | bytes 56
  4.2 1.0 %copy-done.2 = bf16[1072,128]{1,0:T(8,128)(2,1)S(1)} copy-done((bf16[1072,128]{1,0:T(8,128)(2,1)S(1)}, bf16[1072,128]{1,0:T(8,128)(2,1)}, u32[]{:S(2)}) %copy-start.2) | copy-done | bytes 274456
  5.1 2.0 %shard_map.96 = (f32[4,512,128]{2,1,0:T(8,128)S(1)}, bf16[1024,128]{1,0:T(8,128)(2,1)S(1)}, f32[8,128]{1,0:T(8,128)S(1)}, f32[2,4,512]{2,1,0:T(4,128)S(1)}) custom-call(f32[4,512,128]{2,1,0:T(8,128)S(1)} %bitcast.6, bf16[4,512,128]{2,1,0:T(8,128)(2,1)S(1)} %bitcast.7, f32[8]{0:T(128)S(1)} %copy-done.5, s32[1]{0:T(128)S(6)} %copy.12.refs_3_, ...), custom_call_target="tpu_custom_call" | custom-call | flops 10000000000 | bytes 100000000 | tf_op jit(solution)/shard_map/pallas_call | solution.py:218
  7.2 4.9 %collective-permute-start.1 = (bf16[1024,128]{1,0:T(8,128)(2,1)S(1)}, bf16[1024,128]{1,0:T(8,128)(2,1)S(1)}, u32[]{:S(2)}, u32[]{:S(2)}) collective-permute-start(bf16[1024,128]{1,0:T(8,128)(2,1)S(1)} %get-tuple-element.20), channel_id=1, source_target_pairs={{1,2},{3,4},{5,6},{2,1},{4,3},{6,5},{9,10},{11,12},{13,14},{10,9},... | collective-permute-start | bytes 786440 | tf_op jit(solution)/shard_map/ppermute | solution.py:523
  12.1 0.0 collective-permute-done.refs_0_
  12.1 0.7 %shard_map.97 = (f32[2,528,128]{2,1,0:T(8,128)S(1)}, bf16[1088,128]{1,0:T(8,128)(2,1)S(1)}, bf16[2,48,128]{2,1,0:T(8,128)(2,1)S(1)}) custom-call(bf16[1072,128]{1,0:T(8,128)(2,1)S(1)} %collective-permute-done.refs_0_, f32[4,512,128]{2,1,0:T(8,128)S(1)} %get-tuple-element.18.refs_1_, bf16[4,512,128]{2,1,0:T(8,128)(2,1)S(1)} %bitcast.8, ...), custom_call_target="tpu_custom_call" | custom-call | flops 10000000000 | bytes 100000000 | tf_op jit(solution)/shard_map/pallas_call | solution.py:318
  12.8 1.6 %collective-permute-start.2 = (bf16[2,48,128]{2,1,0:T(8,128)(2,1)S(1)}, bf16[2,48,128]{2,1,0:T(8,128)(2,1)S(1)}, u32[]{:S(2)}, u32[]{:S(2)}) collective-permute-start(bf16[2,48,128]{2,1,0:T(8,128)(2,1)S(1)} %get-tuple-element.21.refs_3_), channel_id=1, source_target_pairs={{0,2},{1,3},{2,0},{3,1},{4,6},{5,7},{6,4},{7,5},{8,10},{9,11},{10,... | collective-permute-start | bytes 73736 | tf_op jit(solution)/shard_map/ppermute | solution.py:533
  14.4 0.0 collective-permute-start.5
  14.4 4.1 %collective-permute-done.1.refs_0_ = bf16[1024,128]{1,0:T(8,128)(2,1)S(1)} collective-permute-done((bf16[1024,128]{1,0:T(8,128)(2,1)S(1)}, bf16[1024,128]{1,0:T(8,128)(2,1)S(1)}, u32[]{:S(2)}, u32[]{:S(2)}) %collective-permute-start.1) | collective-permute-done | bytes 262176 | tf_op jit(solution)/shard_map/ppermute | solution.py:523
  18.5 0.0 collective-permute-done.2.refs_4_
  18.5 0.6 %shard_map.98 = (f32[2,528,128]{2,1,0:T(8,128)S(1)}, f32[8,512]{1,0:T(8,128)S(1)}, bf16[4,48,128]{2,1,0:T(8,128)(2,1)S(1)}) custom-call(bf16[1024,128]{1,0:T(8,128)(2,1)S(1)} %collective-permute-done.1.refs_0_, f32[4,512,128]{2,1,0:T(8,128)S(1)} %get-tuple-element.18.refs_1_, bf16[4,512,128]{2,1,0:T(8,128)(2,1)S(1)} %bitcast.9, ...), custom_call_target="tpu_custom_call" | custom-call | flops 10000000000 | bytes 100000000 | tf_op jit(solution)/shard_map/pallas_call | solution.py:318
  19.1 4.6 %collective-permute-start.6 = (f32[8,512]{1,0:T(8,128)S(1)}, f32[8,512]{1,0:T(8,128)S(1)}, u32[]{:S(2)}, u32[]{:S(2)}) collective-permute-start(f32[8,512]{1,0:T(8,128)S(1)} %get-tuple-element.30), channel_id=1, source_target_pairs={{1,2},{3,4},{5,6},{2,1},{4,3},{6,5},{9,10},{11,12},{13,14},{10,9},... | collective-permute-start | bytes 49160 | tf_op jit(solution)/shard_map/ppermute | solution.py:523
  23.7 2.7 %collective-permute-start.4 = (bf16[4,48,128]{2,1,0:T(8,128)(2,1)S(1)}, bf16[4,48,128]{2,1,0:T(8,128)(2,1)S(1)}, u32[]{:S(2)}, u32[]{:S(2)}) collective-permute-start(bf16[4,48,128]{2,1,0:T(8,128)(2,1)S(1)} %get-tuple-element.27.refs_0_), channel_id=1, source_target_pairs={{0,4},{1,5},{2,6},{3,7},{4,0},{5,1},{6,2},{7,3},{8,12},{9,13},{10,... | collective-permute-start | bytes 147464 | tf_op jit(solution)/shard_map/ppermute | solution.py:537
  26.4 1.7 %shard_map.99 = (f32[4,512,128]{2,1,0:T(8,128)S(1)}, f32[4,8,512]{2,1,0:T(8,128)S(1)}, f32[4,8,512]{2,1,0:T(8,128)S(1)}, bf16[1024,128]{1,0:T(8,128)(2,1)S(1)}) custom-call(f32[2,528,128]{2,1,0:T(8,128)S(1)} %get-tuple-element.19.refs_0_, f32[2,528,128]{2,1,0:T(8,128)S(1)} %get-tuple-element.23.refs_1_, bf16[4,512,128]{2,1,0:T(8,128)(2,1)S(1)} %bitcast.10, ...), custom_call_target="tpu_custom_call" | custom-call | flops 10000000000 | bytes 100000000 | tf_op jit(solution)/shard_map/pallas_call | solution.py:350
  28.0 2.3 %collective-permute-start.3 = (bf16[1024,128]{1,0:T(8,128)(2,1)S(1)}, bf16[1024,128]{1,0:T(8,128)(2,1)S(1)}, u32[]{:S(2)}, u32[]{:S(2)}) collective-permute-start(bf16[1024,128]{1,0:T(8,128)(2,1)S(1)} %get-tuple-element.25), channel_id=1, source_target_pairs={{1,2},{3,4},{5,6},{2,1},{4,3},{6,5},{9,10},{11,12},{13,14},{10,9},... | collective-permute-start | bytes 786440 | tf_op jit(solution)/shard_map/ppermute | solution.py:523
  30.3 0.0 collective-permute-done.4.refs_1_.after
  30.3 0.5 %shard_map.100.refs_2_ = f32[4,512,128]{2,1,0:T(8,128)S(1)} custom-call(bf16[4,512,128]{2,1,0:T(8,128)(2,1)S(1)} %bitcast.11, bf16[4,48,128]{2,1,0:T(8,128)(2,1)S(1)} %get-tuple-element.27.refs_0_, bf16[4,48,128]{2,1,0:T(8,128)(2,1)S(1)} %collective-permute-done.4.refs_1_.after), custom_call_target="tpu_custom_call" | custom-call | flops 10000000000 | bytes 100000000 | tf_op jit(solution)/shard_map/pallas_call | solution.py:392
  30.9 0.0 collective-permute-done.6.from_b
  30.9 0.0 collective-permute-done.5.refs_0_.message
  30.9 0.1 collective-permute-start.9
  31.0 1.6 %collective-permute-start.8 = (f32[2,4,512]{2,1,0:T(4,128)S(1)}, f32[2,4,512]{2,1,0:T(4,128)S(1)}, u32[]{:S(2)}, u32[]{:S(2)}) collective-permute-start(f32[2,4,512]{2,1,0:T(4,128)S(1)} %shard_map.102.refs_5_), channel_id=1, source_target_pairs={{0,16},{8,24},{16,0},{24,8},{1,17},{9,25},{17,1},{25,9},{2,18},{10... | collective-permute-start | bytes 49160 | tf_op jit(solution)/shard_map/ppermute | solution.py:500
  32.6 0.3 collective-permute-start.7
  32.9 0.9 %shard_map.101.refs_4_ = f32[4,512,128]{2,1,0:T(8,128)} custom-call(bf16[1088,128]{1,0:T(8,128)(2,1)S(1)} %collective-permute-done.5.refs_0_.message, f32[4,512,128]{2,1,0:T(8,128)S(1)} %get-tuple-element.26.refs_1_, f32[4,512,128]{2,1,0:T(8,128)S(1)} %shard_map.100.refs_2_, bf16[4,512,128]{2,1,0:T(8,128)(2,1)S(1)} %bitcast.12), custom_call_target="tpu_custom_call" | custom-call | flops 10000000000 | bytes 100000000 | tf_op jit(solution)/shard_map/pallas_call | solution.py:486
  33.8 3.4 %collective-permute-done.3.refs_0_ = bf16[1024,128]{1,0:T(8,128)(2,1)S(1)} collective-permute-done((bf16[1024,128]{1,0:T(8,128)(2,1)S(1)}, bf16[1024,128]{1,0:T(8,128)(2,1)S(1)}, u32[]{:S(2)}, u32[]{:S(2)}) %collective-permute-start.3) | collective-permute-done | bytes 262176 | tf_op jit(solution)/shard_map/ppermute | solution.py:523
  37.2 0.0 collective-permute-done.9.refs_8_
  37.2 0.0 collective-permute-done.8.refs_7_
  37.2 0.0 collective-permute-done.7.refs_6_
  37.2 1.6 %shard_map.103 = (f32[4,512,128]{2,1,0:T(8,128)}, f32[2,4,512]{2,1,0:T(4,128)}) custom-call(bf16[1024,128]{1,0:T(8,128)(2,1)S(1)} %collective-permute-done.3.refs_0_, f32[4,512,128]{2,1,0:T(8,128)S(1)} %get-tuple-element.26.refs_1_, f32[4,512,128]{2,1,0:T(8,128)S(1)} %shard_map.100.refs_2_, ...), custom_call_target="tpu_custom_call", output_to_operand_aliasing={{0}: (4, {})} | custom-call | flops 10000000000 | bytes 100000000 | tf_op jit(solution)/shard_map/pallas_call | solution.py:486
  (9 shorter events, 0.1 us)
Async XLA Ops:
  0.6 2.9 %copy-start = (f32[1,4,512,128]{3,2,1,0:T(8,128)S(1)}, f32[1,4,512,128]{3,2,1,0:T(8,128)}, u32[]{:S(2)}) copy-start(f32[1,4,512,128]{3,2,1,0:T(8,128)} %param.8) | copy-start | bytes 3145732
  0.6 2.9 %copy-start.1 = (bf16[1,4,512,128]{3,2,1,0:T(8,128)(2,1)S(1)}, bf16[1,4,512,128]{3,2,1,0:T(8,128)(2,1)}, u32[]{:S(2)}) copy-start(bf16[1,4,512,128]{3,2,1,0:T(8,128)(2,1)} %param.9) | copy-start | bytes 1572868
  0.7 2.9 %copy-start.4 = (s32[2,4,512]{2,1,0:T(4,128)S(1)}, s32[2,4,512]{2,1,0:T(4,128)}, u32[]{:S(2)}) copy-start(s32[2,4,512]{2,1,0:T(4,128)} %refs_4_.1) | copy-start | bytes 49156
  2.8 9.3 %collective-permute-start = (bf16[1072,128]{1,0:T(8,128)(2,1)}, bf16[1072,128]{1,0:T(8,128)(2,1)S(1)}, u32[]{:S(2)}, u32[]{:S(2)}) collective-permute-start(bf16[1072,128]{1,0:T(8,128)(2,1)} %shard_map.95.refs_5_.refs_3_), channel_id=1, source_target_pairs={{0,1},{1,0},{2,3},{3,2},{4,5},{5,4},{6,7},{7,6},{8,9},{9,8},{10,11... | collective-permute-start | bytes 823304 | tf_op jit(solution)/shard_map/ppermute | solution.py:523
  3.5 0.7 %copy-start.5 = (f32[8]{0:T(128)S(1)}, f32[8]{0:T(128)}, u32[]{:S(2)}) copy-start(f32[8]{0:T(128)} %refs_2_.1) | copy-start | bytes 100
  4.2 1.0 %copy-start.2 = (bf16[1072,128]{1,0:T(8,128)(2,1)S(1)}, bf16[1072,128]{1,0:T(8,128)(2,1)}, u32[]{:S(2)}) copy-start(bf16[1072,128]{1,0:T(8,128)(2,1)} %shard_map.95.refs_5_.refs_3_) | copy-start | bytes 823300
  5.1 7.0 %copy-start.3 = (bf16[1072,128]{1,0:T(8,128)(2,1)S(1)}, bf16[1072,128]{1,0:T(8,128)(2,1)}, u32[]{:S(2)}) copy-start(bf16[1072,128]{1,0:T(8,128)(2,1)} %shard_map.95.refs_5_.refs_3_) | copy-start | bytes 823300
  7.2 11.3 %collective-permute-start.1 = (bf16[1024,128]{1,0:T(8,128)(2,1)S(1)}, bf16[1024,128]{1,0:T(8,128)(2,1)S(1)}, u32[]{:S(2)}, u32[]{:S(2)}) collective-permute-start(bf16[1024,128]{1,0:T(8,128)(2,1)S(1)} %get-tuple-element.20), channel_id=1, source_target_pairs={{1,2},{3,4},{5,6},{2,1},{4,3},{6,5},{9,10},{11,12},{13,14},{10,9},... | collective-permute-start | bytes 786440 | tf_op jit(solution)/shard_map/ppermute | solution.py:523
  12.8 5.6 %collective-permute-start.2 = (bf16[2,48,128]{2,1,0:T(8,128)(2,1)S(1)}, bf16[2,48,128]{2,1,0:T(8,128)(2,1)S(1)}, u32[]{:S(2)}, u32[]{:S(2)}) collective-permute-start(bf16[2,48,128]{2,1,0:T(8,128)(2,1)S(1)} %get-tuple-element.21.refs_3_), channel_id=1, source_target_pairs={{0,2},{1,3},{2,0},{3,1},{4,6},{5,7},{6,4},{7,5},{8,10},{9,11},{10,... | collective-permute-start | bytes 73736 | tf_op jit(solution)/shard_map/ppermute | solution.py:533
  14.4 16.5 %collective-permute-start.5 = (bf16[1088,128]{1,0:T(8,128)(2,1)S(1)}, bf16[1088,128]{1,0:T(8,128)(2,1)S(1)}, u32[]{:S(2)}, u32[]{:S(2)}) collective-permute-start(bf16[1088,128]{1,0:T(8,128)(2,1)S(1)} %get-tuple-element.22.refs_5_), channel_id=1, source_target_pairs={{0,1},{1,0},{2,3},{3,2},{4,5},{5,4},{6,7},{7,6},{8,9},{9,8},{10,11... | collective-permute-start | bytes 835592 | tf_op jit(solution)/shard_map/ppermute | solution.py:523
  19.1 11.8 %collective-permute-start.6 = (f32[8,512]{1,0:T(8,128)S(1)}, f32[8,512]{1,0:T(8,128)S(1)}, u32[]{:S(2)}, u32[]{:S(2)}) collective-permute-start(f32[8,512]{1,0:T(8,128)S(1)} %get-tuple-element.30), channel_id=1, source_target_pairs={{1,2},{3,4},{5,6},{2,1},{4,3},{6,5},{9,10},{11,12},{13,14},{10,9},... | collective-permute-start | bytes 49160 | tf_op jit(solution)/shard_map/ppermute | solution.py:523
  23.7 6.6 %collective-permute-start.4 = (bf16[4,48,128]{2,1,0:T(8,128)(2,1)S(1)}, bf16[4,48,128]{2,1,0:T(8,128)(2,1)S(1)}, u32[]{:S(2)}, u32[]{:S(2)}) collective-permute-start(bf16[4,48,128]{2,1,0:T(8,128)(2,1)S(1)} %get-tuple-element.27.refs_0_), channel_id=1, source_target_pairs={{0,4},{1,5},{2,6},{3,7},{4,0},{5,1},{6,2},{7,3},{8,12},{9,13},{10,... | collective-permute-start | bytes 147464 | tf_op jit(solution)/shard_map/ppermute | solution.py:537
  28.0 9.2 %collective-permute-start.3 = (bf16[1024,128]{1,0:T(8,128)(2,1)S(1)}, bf16[1024,128]{1,0:T(8,128)(2,1)S(1)}, u32[]{:S(2)}, u32[]{:S(2)}) collective-permute-start(bf16[1024,128]{1,0:T(8,128)(2,1)S(1)} %get-tuple-element.25), channel_id=1, source_target_pairs={{1,2},{3,4},{5,6},{2,1},{4,3},{6,5},{9,10},{11,12},{13,14},{10,9},... | collective-permute-start | bytes 786440 | tf_op jit(solution)/shard_map/ppermute | solution.py:523
  30.9 6.3 %collective-permute-start.9 = (f32[2,4,512]{2,1,0:T(4,128)S(1)}, f32[2,4,512]{2,1,0:T(4,128)S(1)}, u32[]{:S(2)}, u32[]{:S(2)}) collective-permute-start(f32[2,4,512]{2,1,0:T(4,128)S(1)} %shard_map.102.refs_5_), channel_id=1, source_target_pairs={{0,24},{8,16},{16,8},{24,0},{1,25},{9,17},{17,9},{25,1},{2,26},{10... | collective-permute-start | bytes 49160 | tf_op jit(solution)/shard_map/ppermute | solution.py:500
  31.0 6.2 %collective-permute-start.8 = (f32[2,4,512]{2,1,0:T(4,128)S(1)}, f32[2,4,512]{2,1,0:T(4,128)S(1)}, u32[]{:S(2)}, u32[]{:S(2)}) collective-permute-start(f32[2,4,512]{2,1,0:T(4,128)S(1)} %shard_map.102.refs_5_), channel_id=1, source_target_pairs={{0,16},{8,24},{16,0},{24,8},{1,17},{9,25},{17,1},{25,9},{2,18},{10... | collective-permute-start | bytes 49160 | tf_op jit(solution)/shard_map/ppermute | solution.py:500
  32.6 4.6 %collective-permute-start.7 = (f32[2,4,512]{2,1,0:T(4,128)S(1)}, f32[2,4,512]{2,1,0:T(4,128)S(1)}, u32[]{:S(2)}, u32[]{:S(2)}) collective-permute-start(f32[2,4,512]{2,1,0:T(4,128)S(1)} %shard_map.102.refs_5_), channel_id=1, source_target_pairs={{0,8},{8,0},{16,24},{24,16},{1,9},{9,1},{17,25},{25,17},{2,10},{10... | collective-permute-start | bytes 49160 | tf_op jit(solution)/shard_map/ppermute | solution.py:500

commit v3 on v2

v3 whole, which is shorter than its diff:
```python
import jax
import jax.numpy as jnp
from jax import lax
from jax.experimental import pallas as pl
from jax.experimental.pallas import tpu as pltpu
from jax.sharding import PartitionSpec as P

mobility_step = 0.02
stiffness_step = 0.01
transport_step = 0.125
wall_weight = 0.25

f32 = jnp.float32
bf16 = jnp.bfloat16
CHUNK = 64
LONG = 10**10
PAD = 8
ANY = pl.BlockSpec(memory_space=pl.ANY)
HBM = pl.BlockSpec(memory_space=pltpu.HBM)
VMEM = pl.BlockSpec(memory_space=pltpu.VMEM)
SMEM = pl.BlockSpec(memory_space=pltpu.SMEM)


def cost(flops):
    return pl.CostEstimate(flops=flops, bytes_accessed=1, transcendentals=0)


def call(kernel, outs, out_specs, in_specs, scratch, estimate, aliases=None, limit=12):
    return pl.pallas_call(
        kernel,
        out_shape=outs,
        out_specs=out_specs,
        in_specs=in_specs,
        scratch_shapes=scratch,
        input_output_aliases=aliases or {},
        cost_estimate=estimate,
        compiler_params=pltpu.CompilerParams(vmem_limit_bytes=limit * 1024 * 1024),
    )


def starts(rows):
    return range(0, rows, CHUNK)


def read(layer, y, shift=0):
    ref, lead = layer
    return ref[(*lead, pl.ds(PAD + y + shift, CHUNK), slice(None))]


def write(layer, y, v):
    ref, lead = layer
    ref[(*lead, pl.ds(PAD + y, CHUNK), slice(None))] = v


def z_sum(v):
    depth = v.shape[1]
    lane = lax.broadcasted_iota(jnp.int32, v.shape, 1)
    below = jnp.where(lane == 0, 0.0, pltpu.roll(v, 1, 1))
    above = jnp.where(lane == depth - 1, 0.0, pltpu.roll(v, depth - 1, 1))
    return below + above


def plane_part(layer, y):
    v = read(layer, y)
    return read(layer, y, 1) + read(layer, y, -1) + z_sum(v) - 6.0 * v


def clear_margins(layer):
    ref, lead = layer
    zero = jnp.zeros((PAD, ref.shape[-1]), f32)
    ref[(*lead, pl.ds(0, PAD), slice(None))] = zero
    ref[(*lead, pl.ds(ref.shape[-2] - PAD, PAD), slice(None))] = zero


def is_odd():
    return lax.rem(lax.axis_index("slab"), 2) == 1


def stored(d, layers):
    return jnp.where(is_odd(), d, layers - 1 - d)


def has_partner(count):
    position = lax.axis_index("slab")
    above = position < count - 1
    below = position > 0
    odd = is_odd()
    flags = jnp.where(odd, below, above), jnp.where(odd, above, below)
    return [jnp.where(f, 1.0, 0.0).astype(f32) for f in flags]


def copy_all(pairs, sems):
    copies = [pltpu.make_async_copy(s, d, sems.at[i]) for i, (s, d) in enumerate(pairs)]
    for c in copies:
        c.start()
    return copies


def write_message(near, far, missing, out, rows):
    clear_margins(missing)
    for y in starts(rows):
        v = read(near, y)
        rounded = v.astype(bf16)
        out[pl.ds(y, CHUNK), :] = rounded
        write(missing, y, v - rounded.astype(f32))
    for y in starts(rows):
        out[pl.ds(rows + y, CHUNK), :] = (read(far, y) + 2.0 * plane_part(missing, y)).astype(bf16)


def curvature_of(p):
    return 3.0 * p * p - 1.0


def local_step(state, first, phase, row, count, emit):
    layers = len(state)
    rows = phase.shape[1]
    depth = phase.shape[2]
    side_a, side_b = has_partner(count)
    transport = row[0:1, :]
    for d in range(layers):
        for y in starts(rows):
            lap = plane_part(state[d], y)
            if d > 0:
                lap = lap + read(state[d - 1], y)
            if d < layers - 1:
                lap = lap + read(state[d + 1], y)
            write(first[d], y, lap)
    for d in range(layers):
        at = stored(d, layers)
        for y in starts(rows):
            v = read(state[d], y)
            second = plane_part(first[d], y)
            second = second + (read(first[d - 1], y) if d > 0 else side_a * v)
            second = second + (read(first[d + 1], y) if d < layers - 1 else side_b * v)
            p = phase[at, pl.ds(y, CHUNK), :].astype(f32)
            moved = read(state[d], y, 1) - read(state[d], y, -1)
            stepped = (
                v
                + mobility_step * curvature_of(p) * read(first[d], y)
                - stiffness_step * second
                + transport * moved
            )
            emit(d, y, v, stepped)


def padded(rows, depth, layers=None):
    lead = () if layers is None else (layers,)
    return pltpu.VMEM((*lead, rows + 2 * PAD, depth), f32)


def layers_of(ref):
    return [(ref, (d,)) for d in range(ref.shape[0])]


def first_message(adjoint, targets, owners, cells, out, near, far, missing, digits, owner, cell, sems):
    layers, rows, depth = adjoint.shape
    n = targets.shape[0]
    pairs = [(adjoint.at[stored(d, layers)], ref.at[pl.ds(PAD, rows)]) for d, ref in ((0, near), (1, far))]
    pairs += [(targets, out.at[pl.ds(2 * rows, n)]), (owners, owner), (cells, cell)]
    copies = copy_all(pairs, sems)
    digits[...] = jnp.zeros(digits.shape, f32)
    for c in copies[3:]:
        c.wait()
    digits[0:1, 0:n] = owner[...].astype(f32)
    digits[1:2, 0:n] = (cell[...] >> 8).astype(f32)
    digits[2:3, 0:n] = (cell[...] & 255).astype(f32)
    out[pl.ds(2 * rows + n, 16), :] = digits[...].astype(bf16)
    for c in copies[:3]:
        c.wait()
    write_message((near, ()), (far, ()), (missing, ()), out, rows)


def make_first_message(adjoint, targets, owners, cells):
    layers, rows, depth = adjoint.shape
    extra = targets.shape[0] + 16
    row = pltpu.VMEM(owners.shape, jnp.int32)
    return call(
        first_message,
        jax.ShapeDtypeStruct((2 * rows + extra, depth), bf16),
        VMEM,
        [ANY] * 4,
        [padded(rows, depth)] * 3 + [pltpu.VMEM((16, depth), f32), row, row, pltpu.SemaphoreType.DMA((5,))],
        cost(LONG),
    )(*[pltpu.with_memory_space_constraint(v, pltpu.HBM) for v in (adjoint, targets, owners, cells)])


def transport_row(inflow, depth):
    lane = lax.broadcasted_iota(jnp.int32, (8, depth), 1)
    height = (lane.astype(f32) + 0.5) / depth
    return (transport_step * inflow) * (4.0 * height * (1.0 - height))


def first_local(
    count, adjoint, phase, rates, choice, mask, after, out, message, row, masked, state, first, missing, sems
):
    layers, rows, depth = adjoint.shape
    copies = copy_all(
        [(adjoint.at[stored(d, layers)], state.at[d, pl.ds(PAD, rows)]) for d in range(layers)], sems
    )
    row[...] = transport_row(rates[choice[0]], depth)
    masked[...] = wall_weight * mask[...].astype(f32)
    for d in range(layers):
        clear_margins((state, (d,)))
        clear_margins((first, (d,)))
    for c in copies:
        c.wait()
    own = layers_of(state)
    write_message(own[-1], own[-2], (missing, ()), message, rows)

    def emit(d, y, v, stepped):
        out[d, pl.ds(y, CHUNK), :] = stepped

    local_step(own, layers_of(first), phase, row, count, emit)


def make_first_local(adjoint, phase, rates, choice, mask, after, count):
    layers, rows, depth = adjoint.shape
    return call(
        lambda *refs: first_local(count, *refs),
        (
            jax.ShapeDtypeStruct(adjoint.shape, f32),
            jax.ShapeDtypeStruct((2 * rows, depth), bf16),
            jax.ShapeDtypeStruct((8, depth), f32),
            jax.ShapeDtypeStruct(mask.shape, f32),
        ),
        (VMEM,) * 4,
        [ANY, VMEM, SMEM, SMEM, VMEM, ANY],
        [padded(rows, depth, layers)] * 2 + [padded(rows, depth), pltpu.SemaphoreType.DMA((layers,))],
        cost(LONG),
    )(adjoint, phase, rates, choice, mask, after)


def add_halo(message, edge, inner, halo, phase, at, rows, put_edge, put_inner):
    clear_margins(halo)
    for y in starts(rows):
        near = message[pl.ds(y, CHUNK), :].astype(f32)
        write(halo, y, near)
        put_inner(y, inner(y) - stiffness_step * near)
    for y in starts(rows):
        near = read(halo, y)
        far = message[pl.ds(rows + y, CHUNK), :].astype(f32)
        curvature = curvature_of(phase[at, pl.ds(y, CHUNK), :].astype(f32))
        both = far + 2.0 * plane_part(halo, y)
        put_edge(y, edge(y) + mobility_step * curvature * near - stiffness_step * both)


def wall_rows(v, first_row):
    depth = v.shape[1]
    row = lax.broadcasted_iota(jnp.int32, (8, depth), 0) - first_row
    lane = lax.broadcasted_iota(jnp.int32, (8, depth), 1)
    pick = ((row == 0) & (lane == 0)) | ((row == 1) & (lane == depth - 1))
    pick = jnp.where(pick, 1.0, 0.0).astype(bf16)

    def part(w):
        return lax.dot_general(pick, w, (((1,), (1,)), ((), ())), preferred_element_type=f32)

    if v.dtype == bf16:
        return part(v)
    high = v.astype(bf16)
    rest = v - high.astype(f32)
    middle = rest.astype(bf16)
    low = (rest - middle.astype(f32)).astype(bf16)
    return part(high) + part(middle) + part(low)


def join_halo(side, message, pre, phase, out, halo):
    layers, rows, depth = pre.shape
    one, two = (0, 1) if side == 0 else (layers - 1, layers - 2)
    edge, inner = layers_of(out)
    clear_margins(edge)
    clear_margins(inner)
    add_halo(
        message,
        lambda y: pre[one, pl.ds(y, CHUNK), :],
        lambda y: pre[two, pl.ds(y, CHUNK), :],
        (halo, ()),
        phase,
        stored(one, layers),
        rows,
        lambda y, v: write(edge, y, v),
        lambda y, v: write(inner, y, v),
    )


def second_message(half, sent, missing, rows):
    edge, inner = layers_of(half)
    write_message(edge, inner, (missing, ()), sent, rows)
    for y in range(0, rows, 256):
        wall_part = 0.0
        for i in range(2):
            span = range(y + 128 * i, y + 128 * (i + 1), CHUNK)
            both = jnp.concatenate([read(inner, k) + 2.0 * plane_part(edge, k) for k in span])
            near = jnp.concatenate([read(edge, k) for k in span])
            wall_part = wall_part + wall_rows(near, 4 * i) + wall_rows(both, 4 * i + 2)
        high = wall_part.astype(bf16)
        low = (wall_part - high.astype(f32)).astype(bf16)
        sent[pl.ds(2 * rows + y // 16, 16), :] = jnp.concatenate([high.astype(f32), low.astype(f32)]).astype(bf16)


def middle_a(message, pre, phase, first, out, sent, block, halo, missing):
    rows, n = pre.shape[1], block.shape[0] // 2
    join_halo(0, message, pre, phase, out, halo)
    second_message(out, sent, missing, rows)
    block[pl.ds(0, n), :] = first[pl.ds(2 * rows, n), :]
    block[pl.ds(n, n), :] = message[pl.ds(2 * rows, n), :]


def make_middle_a(message, pre, phase, first):
    layers, rows, depth = pre.shape
    extra = first.shape[0] - 2 * rows
    return call(
        middle_a,
        (
            jax.ShapeDtypeStruct((2, rows + 2 * PAD, depth), f32),
            jax.ShapeDtypeStruct((2 * rows + rows // 16, depth), bf16),
            jax.ShapeDtypeStruct((2 * extra, depth), bf16),
        ),
        (VMEM,) * 3,
        [VMEM] * 4,
        [padded(rows, depth)] * 2,
        cost(LONG),
    )(message, pre, phase, first)


def middle_b(message, pre, phase, after, out, sent, halo, missing):
    join_halo(1, message, pre, phase, out, halo)
    second_message(out, sent, missing, pre.shape[1])


def make_middle_b(message, pre, phase, after):
    layers, rows, depth = pre.shape
    return call(
        middle_b,
        (
            jax.ShapeDtypeStruct((2, rows + 2 * PAD, depth), f32),
            jax.ShapeDtypeStruct((2 * rows + rows // 16, depth), bf16),
        ),
        (VMEM,) * 2,
        [VMEM, VMEM, VMEM, ANY],
        [padded(rows, depth)] * 2,
        cost(LONG),
    )(message, pre, phase, after)


def second_local(count, side_a, side_b, phase, row, own, other, out, wall, phase_wall, block, first):
    layers, rows, depth = out.shape
    n = own.shape[0]
    block[pl.ds(0, n), :] = own[...]
    block[pl.ds(n, n), :] = other[...]
    own = layers_of(side_a) + layers_of(side_b)[::-1]
    for d in range(layers):
        clear_margins((first, (d,)))
    held = []

    def emit(d, y, v, stepped):
        out[d, pl.ds(y, CHUNK), :] = stepped
        held.append(v + stepped)
        if len(held) * CHUNK == 128:
            start = y + CHUNK - 128
            wall[d, :, pl.ds(start, 128)] = wall_rows(jnp.concatenate(held), 0)
            phase_wall[d, :, pl.ds(start, 128)] = wall_rows(phase[stored(d, layers), pl.ds(start, 128), :], 0)
            held.clear()

    local_step(own, layers_of(first), phase, row, count, emit)


def make_second_local(side_a, side_b, phase, row, own, other, count):
    layers, rows, depth = phase.shape
    return call(
        lambda *refs: second_local(count, *refs),
        (
            jax.ShapeDtypeStruct((layers, rows, depth), f32),
            jax.ShapeDtypeStruct((layers, 8, rows), f32),
            jax.ShapeDtypeStruct((layers, 8, rows), f32),
            jax.ShapeDtypeStruct((2 * own.shape[0], depth), bf16),
        ),
        (VMEM,) * 4,
        [VMEM] * 6,
        [padded(rows, depth, layers)],
        cost(2 * 10**9),
    )(side_a, side_b, phase, row, own, other)


def injection(n, phase, *refs):
    sources, (out, index, rhs) = refs[:-3], refs[-3:]
    layers, rows, depth = out.shape
    position = lax.axis_index("slab").astype(f32)
    rhs[:, :depth] = jnp.ones((rhs.shape[0], depth), bf16)
    at = 0
    for source in sources:
        for first in range(0, source.shape[0], n + 16):
            rhs[pl.ds(at, n), depth:] = source[pl.ds(first, n), :]
            digits = source[pl.ds(first + n, 16), :].astype(f32)
            cell = jnp.where(digits[0:1] == position, digits[1:2] * 256.0 + digits[2:3], -1.0)
            index[0:1, pl.ds(at, n)] = cell[:, :n].astype(jnp.int32)
            at += n
    for d in range(layers):
        at = stored(d, layers)
        for y in range(0, rows, 128):
            cell = lax.broadcasted_iota(jnp.int32, (128, index.shape[1]), 0) + (at * rows + y)
            here = jnp.where(cell == index[0:1, :], 1.0, 0.0).astype(bf16)
            added = jnp.dot(here, rhs[...], preferred_element_type=f32)
            p = phase[at, pl.ds(y, 128), :].astype(f32)
            out[d, pl.ds(y, 128), :] = added[:, :depth] * p - added[:, depth:]


def make_injection(phase, n, sources):
    layers, rows, depth = phase.shape
    total = sum(r.shape[0] // (n + 16) * n for r in sources)
    return call(
        lambda *refs: injection(n, *refs),
        jax.ShapeDtypeStruct((layers, rows, depth), f32),
        VMEM,
        [VMEM] * (1 + len(sources)),
        [pltpu.VMEM((8, total), jnp.int32), pltpu.VMEM((total, 2 * depth), bf16)],
        cost(1),
    )(phase, *sources)


def unpack_walls(message, rows, out):
    for y in range(0, rows, 256):
        both = message[pl.ds(2 * rows + y // 16, 16), :].astype(f32)
        both = both[:8] + both[8:]
        for i in range(2):
            out[:4, pl.ds(y + 128 * i, 128)] = both[4 * i : 4 * i + 4]


def make_unpack(message, rows):
    return call(
        lambda message, out: unpack_walls(message, rows, out),
        jax.ShapeDtypeStruct((8, rows), f32),
        VMEM,
        [VMEM],
        [],
        cost(14 * 10**8),
    )(message)


def wall_kernel(wall, phase_wall, from_a, message_b, mask, out, from_b):
    layers = wall.shape[0]
    unpack_walls(message_b, wall.shape[2], from_b)
    odd = is_odd()
    terms = []
    for d in range(layers):
        p = phase_wall[d, :2, :]
        w = wall[d, :2, :]
        for halo, off in ((from_a, d), (from_b, layers - 1 - d)):
            if off == 0:
                w = w + mobility_step * curvature_of(p) * halo[:2] - stiffness_step * halo[2:4]
            elif off == 1:
                w = w - stiffness_step * halo[:2]
        terms.append((1.0 - p * p) * w)
    for l in range(layers):
        out[:, l, :] = mask[:, l, :] * jnp.where(odd, terms[l], terms[layers - 1 - l])


def make_walls(wall, phase_wall, from_a, message_b, mask):
    held = pltpu.VMEM(wall.shape[1:], f32)
    return call(
        wall_kernel,
        jax.ShapeDtypeStruct(mask.shape, f32),
        VMEM,
        [VMEM] * 5,
        [held],
        cost(LONG),
    )(wall, phase_wall, from_a, message_b, mask)


def final(message_a, message_b, pre, added, phase, out, token, planes, halo, sems):
    layers, rows, depth = pre.shape
    half = rows // 2
    copies = []
    token[...] = jnp.zeros(token.shape, f32)

    def put(d):
        def store(y, v):
            planes[d, pl.ds(y, CHUNK), :] = v + added[d, pl.ds(y, CHUNK), :]
            if (y + CHUNK) % half == 0:
                span = pl.ds(y + CHUNK - half, half)
                c = pltpu.make_async_copy(
                    planes.at[d, span], out.at[stored(d, layers), span], sems.at[len(copies)]
                )
                c.start()
                copies.append(c)

        return store

    def get(d):
        return lambda y: pre[d, pl.ds(y, CHUNK), :]

    for message, one, two in ((message_a, 0, 1), (message_b, layers - 1, layers - 2)):
        add_halo(message, get(one), get(two), (halo, ()), phase, stored(one, layers), rows, put(one), put(two))
    for c in copies:
        c.wait()


def make_final(message_a, message_b, pre, added, phase):
    layers, rows, depth = pre.shape
    return call(
        final,
        (jax.ShapeDtypeStruct(pre.shape, f32), jax.ShapeDtypeStruct((8, depth), f32)),
        (ANY, VMEM),
        [VMEM] * 5,
        [pltpu.VMEM(pre.shape, f32), padded(rows, depth), pltpu.SemaphoreType.DMA((2 * layers,))],
        cost(1),
    )(message_a, message_b, pre, added, phase)


def add_up(a, b, c, d, after, out):
    out[...] = (a[...] + b[...]) + (c[...] + d[...])


def make_sum(parts, after):
    return call(add_up, jax.ShapeDtypeStruct(parts[0].shape, f32), VMEM, [VMEM] * 4 + [ANY], [], cost(1))(
        *parts, after
    )


def on_device(adjoint, phase, targets, owners, target_cell, rate_index, inflow_rates, wall_mask):
    state, phase, targets = adjoint[0], phase[0], targets[0]
    owners = owners.reshape(target_cell.shape)
    count = lax.axis_size("slab")
    pairs = (
        [(i, i ^ 1) for i in range(count) if i ^ 1 < count],
        [(i, i + 1) for i in range(1, count - 1, 2)] + [(i + 1, i) for i in range(1, count - 1, 2)],
    )

    def send(v, side):
        return lax.ppermute(v, "slab", pairs[side])

    rows, n = state.shape[1], targets.shape[0]
    few = count == 8
    first = make_first_message(state, targets, owners, target_cell)
    from_a = send(first, 0)
    pre, message, row, mask = make_first_local(state, phase, inflow_rates, rate_index, wall_mask, first, count)
    from_b = send(message, 1)
    half_a, message, pair = make_middle_a(from_a, pre, phase, first)
    later_a = send(message, 0)
    beside = lax.ppermute(pair, "slab", [(i, i ^ 2) for i in range(count)]) if few else pair
    half_b, message = make_middle_b(from_b, pre, phase, message)
    later_b = send(message, 1)
    pre, wall, phase_wall, four = make_second_local(half_a, half_b, phase, row, pair, beside, count)
    if few:
        blocks = [four, lax.ppermute(four, "slab", [(i, i ^ 4) for i in range(count)])]
    else:
        blocks = [lax.all_gather(first[2 * state.shape[1] :], "slab", axis=0, tiled=True)]
    part = make_walls(wall, phase_wall, make_unpack(later_a, state.shape[1]), later_b, mask)
    conditions = lax.axis_size("cond")
    if conditions == 4:
        parts = [part] + [lax.ppermute(part, "cond", [(i, i ^ k) for i in range(4)]) for k in (1, 2, 3)]
    added = make_injection(phase, n, blocks)
    out, token = make_final(later_a, later_b, pre, added, phase)
    wall_gradient = make_sum(parts, token) if conditions == 4 else lax.psum(part, "cond")
    return out[None], wall_gradient


def solution(mesh):
    in_specs = (
        P("cond", "slab", None, None),
        P("cond", "slab", None, None),
        P("cond", "slab", None),
        P("cond", "slab", None),
        P("cond", "slab"),
        P("cond"),
        P(),
        P(None, "slab", None),
    )
    out_specs = (P("cond", "slab", None, None), P(None, "slab", None))
    return jax.shard_map(
        on_device, mesh=mesh, in_specs=in_specs, out_specs=out_specs, check_vma=False
    )
```

time: 39 us -> 35 us (0.90)
  the two profiles are of different devices: /device:TPU:4 before, /device:TPU:25 now
where the time goes in v3:
time: 35 us; the launch traced here: 34.3 us
  waiting for transfers between devices  13.3 us (38%)
  starting transfers between devices  9.6 us (27%)
  Pallas kernels  9.35 us (27%)
  between operations  1.41 us (4%)
  local copies, waits for them, and re-layouts  0.63 us (2%)
    ppermute x4, waiting for transfers between devices, send(): return lax.ppermute(v, 'slab', pairs[side])  13.1 us
    ppermute x4, starting transfers between devices, send(): return lax.ppermute(v, 'slab', pairs[side])  6.91 us
    ppermute x3, starting transfers between devices, on_device(): lax.ppermute(part, 'cond', [(i, i ^ k) for i in range(4)])  2.21 us
    pallas_call x1, Pallas kernels, make_first_local(): call(lambda *refs: first_local(count, *refs), (jax.ShapeDtypeStruct(adjoi...  2.09 us
    pallas_call x1, Pallas kernels, make_second_local(): call(lambda *refs: second_local(count, *refs), (jax.ShapeDtypeStruct((lay...  1.93 us
    pallas_call x1, Pallas kernels, make_first_message(): call(first_message, jax.ShapeDtypeStruct((2 * rows + extra, depth), bf16)...  1.41 us
    pallas_call x1, Pallas kernels, make_final(): call(final, (jax.ShapeDtypeStruct(pre.shape, f32), jax.ShapeDtypeStruct((...  1.31 us
    pallas_call x1, Pallas kernels, make_middle_b(): call(middle_b, (jax.ShapeDtypeStruct((2, rows + 2 * PAD, depth), f32), ja...  0.73 us
  transfers between devices with their start and end apart: 9, of which 4 were waited for; matrix products, arithmetic and copies ran while one was open for 0% of the time, Pallas kernels for 21%

profile of v3, /device:TPU:25, one launch (start us, length us, event | category | flops | bytes accessed | tf_op | source)
XLA Modules:
  0.0 34.3 jit_solution(10606724338503671473)
XLA Ops:
  0.6 0.0 copy-start
  0.6 0.0 copy-start.1
  0.7 0.0 copy-start.2
  0.7 1.4 %shard_map.95.refs_5_.first = bf16[1072,128]{1,0:T(8,128)(2,1)S(1)} custom-call(f32[4,512,128]{2,1,0:T(8,128)} %bitcast.11, bf16[32,128]{1,0:T(8,128)(2,1)} %bitcast.14, s32[1,32]{1,0:T(1,128)} %bitcast.15, s32[1,32]{1,0:T(1,128)} %cells.1), custom_call_target="tpu_custom_call" | custom-call | flops 10000000000 | bytes 1 | tf_op jit(solution)/shard_map/pallas_call | solution.py:177
  2.1 1.3 %collective-permute-start = (bf16[1072,128]{1,0:T(8,128)(2,1)S(1)}, bf16[1072,128]{1,0:T(8,128)(2,1)S(1)}, u32[]{:S(2)}, u32[]{:S(2)}) collective-permute-start(bf16[1072,128]{1,0:T(8,128)(2,1)S(1)} %shard_map.95.refs_5_.first), channel_id=1, source_target_pairs={{0,1},{1,0},{2,3},{3,2},{4,5},{5,4},{6,7},{7,6},{8,9},{9,8},{10,11... | collective-permute-start | bytes 823304 | tf_op jit(solution)/shard_map/ppermute | solution.py:529
  4.0 0.0 copy-start.3
  4.0 0.0 copy-done
  4.1 0.6 %copy-done.3 = f32[8]{0:T(128)S(1)} copy-done((f32[8]{0:T(128)S(1)}, f32[8]{0:T(128)}, u32[]{:S(2)}) %copy-start.3) | copy-done | bytes 56
  4.7 2.1 %shard_map.96 = (f32[4,512,128]{2,1,0:T(8,128)S(1)}, bf16[1024,128]{1,0:T(8,128)(2,1)S(1)}, f32[8,128]{1,0:T(8,128)S(1)}, f32[2,4,512]{2,1,0:T(4,128)S(1)}) custom-call(f32[4,512,128]{2,1,0:T(8,128)S(1)} %bitcast.12, bf16[4,512,128]{2,1,0:T(8,128)(2,1)S(1)} %bitcast.5, f32[8]{0:T(128)S(1)} %copy-done.3, s32[1]{0:T(128)S(6)} %copy.10.refs_3_, ...), custom_call_target="tpu_custom_call" | custom-call | flops 10000000000 | bytes 1 | tf_op jit(solution)/shard_map/pallas_call | solution.py:218
  6.8 2.0 %collective-permute-start.2 = (bf16[1024,128]{1,0:T(8,128)(2,1)S(1)}, bf16[1024,128]{1,0:T(8,128)(2,1)S(1)}, u32[]{:S(2)}, u32[]{:S(2)}) collective-permute-start(bf16[1024,128]{1,0:T(8,128)(2,1)S(1)} %get-tuple-element.19), channel_id=1, source_target_pairs={{1,2},{3,4},{5,6},{2,1},{4,3},{6,5},{9,10},{11,12},{13,14},{10,9},... | collective-permute-start | bytes 786440 | tf_op jit(solution)/shard_map/ppermute | solution.py:529
  8.8 0.8 %collective-permute-done.message = bf16[1072,128]{1,0:T(8,128)(2,1)S(1)} collective-permute-done((bf16[1072,128]{1,0:T(8,128)(2,1)S(1)}, bf16[1072,128]{1,0:T(8,128)(2,1)S(1)}, u32[]{:S(2)}, u32[]{:S(2)}) %collective-permute-start) | collective-permute-done | bytes 274464 | tf_op jit(solution)/shard_map/ppermute | solution.py:529
  9.6 0.7 %shard_map.97 = (f32[2,528,128]{2,1,0:T(8,128)S(1)}, bf16[1056,128]{1,0:T(8,128)(2,1)S(1)}, bf16[96,128]{1,0:T(8,128)(2,1)S(1)}) custom-call(bf16[1072,128]{1,0:T(8,128)(2,1)S(1)} %collective-permute-done.message, f32[4,512,128]{2,1,0:T(8,128)S(1)} %get-tuple-element.17.pre, bf16[4,512,128]{2,1,0:T(8,128)(2,1)S(1)} %bitcast.6, ...), custom_call_target="tpu_custom_call" | custom-call | flops 10000000000 | bytes 1 | tf_op jit(solution)/shard_map/pallas_call | solution.py:311
  10.3 0.2 collective-permute-start.4
  10.5 1.6 %collective-permute-start.1 = (bf16[1056,128]{1,0:T(8,128)(2,1)S(1)}, bf16[1056,128]{1,0:T(8,128)(2,1)S(1)}, u32[]{:S(2)}, u32[]{:S(2)}) collective-permute-start(bf16[1056,128]{1,0:T(8,128)(2,1)S(1)} %get-tuple-element.18.after), channel_id=1, source_target_pairs={{0,1},{1,0},{2,3},{3,2},{4,5},{5,4},{6,7},{7,6},{8,9},{9,8},{10,11... | collective-permute-start | bytes 811016 | tf_op jit(solution)/shard_map/ppermute | solution.py:529
  12.1 4.4 %collective-permute-done.2.message = bf16[1024,128]{1,0:T(8,128)(2,1)S(1)} collective-permute-done((bf16[1024,128]{1,0:T(8,128)(2,1)S(1)}, bf16[1024,128]{1,0:T(8,128)(2,1)S(1)}, u32[]{:S(2)}, u32[]{:S(2)}) %collective-permute-start.2) | collective-permute-done | bytes 262176 | tf_op jit(solution)/shard_map/ppermute | solution.py:529
  16.5 0.7 %shard_map.98 = (f32[2,528,128]{2,1,0:T(8,128)S(1)}, bf16[1056,128]{1,0:T(8,128)(2,1)S(1)}) custom-call(bf16[1024,128]{1,0:T(8,128)(2,1)S(1)} %collective-permute-done.2.message, f32[4,512,128]{2,1,0:T(8,128)S(1)} %get-tuple-element.17.pre, bf16[4,512,128]{2,1,0:T(8,128)(2,1)S(1)} %bitcast.7, bf16[1056,128]{1,0:T(8,128)(2,1)S(1)} %get-tuple-element.18.after), custom_call_target="tpu_custom_call" | custom-call | flops 10000000000 | bytes 1 | tf_op jit(solution)/shard_map/pallas_call | solution.py:332
  17.2 2.0 %collective-permute-start.3 = (bf16[1056,128]{1,0:T(8,128)(2,1)S(1)}, bf16[1056,128]{1,0:T(8,128)(2,1)S(1)}, u32[]{:S(2)}, u32[]{:S(2)}) collective-permute-start(bf16[1056,128]{1,0:T(8,128)(2,1)S(1)} %get-tuple-element.20), channel_id=1, source_target_pairs={{1,2},{3,4},{5,6},{2,1},{4,3},{6,5},{9,10},{11,12},{13,14},{10,9},... | collective-permute-start | bytes 811016 | tf_op jit(solution)/shard_map/ppermute | solution.py:529
  19.2 0.0 collective-permute-done.4.refs_5_
  19.2 1.9 %shard_map.99 = (f32[4,512,128]{2,1,0:T(8,128)S(1)}, f32[4,8,512]{2,1,0:T(8,128)S(1)}, f32[4,8,512]{2,1,0:T(8,128)S(1)}, bf16[192,128]{1,0:T(8,128)(2,1)S(1)}) custom-call(f32[2,528,128]{2,1,0:T(8,128)S(1)} %get-tuple-element.21.refs_0_, f32[2,528,128]{2,1,0:T(8,128)S(1)} %get-tuple-element.22.refs_1_, bf16[4,512,128]{2,1,0:T(8,128)(2,1)S(1)} %bitcast.8, ...), custom_call_target="tpu_custom_call" | custom-call | flops 2000000000 | bytes 1 | tf_op jit(solution)/shard_map/pallas_call | solution.py:369
  21.1 0.3 collective-permute-start.5
  21.4 7.9 %collective-permute-done.1.message_a.message = bf16[1056,128]{1,0:T(8,128)(2,1)S(1)} collective-permute-done((bf16[1056,128]{1,0:T(8,128)(2,1)S(1)}, bf16[1056,128]{1,0:T(8,128)(2,1)S(1)}, u32[]{:S(2)}, u32[]{:S(2)}) %collective-permute-start.1) | collective-permute-done | bytes 270368 | tf_op jit(solution)/shard_map/ppermute | solution.py:529
  29.4 0.0 collective-permute-done.3.message_b
  29.4 1.7 %collective-permute-start.8 = (f32[2,4,512]{2,1,0:T(4,128)S(1)}, f32[2,4,512]{2,1,0:T(4,128)S(1)}, u32[]{:S(2)}, u32[]{:S(2)}) collective-permute-start(f32[2,4,512]{2,1,0:T(4,128)S(1)} %shard_map.103.a), channel_id=1, source_target_pairs={{0,24},{8,16},{16,8},{24,0},{1,25},{9,17},{17,9},{25,1},{2,26},{10... | collective-permute-start | bytes 49160 | tf_op jit(solution)/shard_map/ppermute | solution.py:550
  31.1 0.3 collective-permute-start.7
  31.4 0.3 collective-permute-start.6
  31.7 0.0 collective-permute-done.5.refs_2_
  31.7 0.5 %shard_map.100.added = f32[4,512,128]{2,1,0:T(8,128)S(1)} custom-call(bf16[4,512,128]{2,1,0:T(8,128)(2,1)S(1)} %bitcast.9, bf16[192,128]{1,0:T(8,128)(2,1)S(1)} %get-tuple-element.26.refs_1_, bf16[192,128]{1,0:T(8,128)(2,1)S(1)} %collective-permute-done.5.refs_2_), custom_call_target="tpu_custom_call" | custom-call | flops 1 | bytes 1 | tf_op jit(solution)/shard_map/pallas_call | solution.py:410
  32.2 1.3 %shard_map.101 = (f32[4,512,128]{2,1,0:T(8,128)}, f32[8,128]{1,0:T(8,128)S(1)}) custom-call(bf16[1056,128]{1,0:T(8,128)(2,1)S(1)} %collective-permute-done.1.message_a.message, bf16[1056,128]{1,0:T(8,128)(2,1)S(1)} %collective-permute-done.3.message_b, f32[4,512,128]{2,1,0:T(8,128)S(1)} %get-tuple-element.25.pre, f32[4,512,128]{2,1,0:T(8,128)S(1)} %shard_map.100.added, ...), custom_call_target="tpu_custom_call" | custom-call | flops 1 | bytes 1 | tf_op jit(solution)/shard_map/pallas_call | solution.py:499
  33.5 0.0 collective-permute-done.8.d
  33.5 0.2 collective-permute-done.7.c
  33.7 0.0 collective-permute-done.6.b
  33.7 0.6 %shard_map.104 = f32[2,4,512]{2,1,0:T(4,128)} custom-call(f32[2,4,512]{2,1,0:T(4,128)S(1)} %shard_map.103.a, f32[2,4,512]{2,1,0:T(4,128)S(1)} %collective-permute-done.6.b, f32[2,4,512]{2,1,0:T(4,128)S(1)} %collective-permute-done.7.c, f32[2,4,512]{2,1,0:T(4,128)S(1)} %collective-permute-done.8.d, f32[8,128]{1,0:T(8,128)S(1)} %get-tuple-element.31.after), custom_call_target="tpu_custom_call" | custom-call | flops 1 | bytes 1 | tf_op jit(solution)/shard_map/pallas_call | solution.py:514
  (4 shorter events, 0.0 us)
Async XLA Ops:
  0.6 3.4 %copy-start = (bf16[1,4,512,128]{3,2,1,0:T(8,128)(2,1)S(1)}, bf16[1,4,512,128]{3,2,1,0:T(8,128)(2,1)}, u32[]{:S(2)}) copy-start(bf16[1,4,512,128]{3,2,1,0:T(8,128)(2,1)} %param.9) | copy-start | bytes 1572868
  0.6 3.4 %copy-start.1 = (f32[1,4,512,128]{3,2,1,0:T(8,128)S(1)}, f32[1,4,512,128]{3,2,1,0:T(8,128)}, u32[]{:S(2)}) copy-start(f32[1,4,512,128]{3,2,1,0:T(8,128)} %param.8) | copy-start | bytes 3145732
  0.7 3.4 %copy-start.2 = (s32[2,4,512]{2,1,0:T(4,128)S(1)}, s32[2,4,512]{2,1,0:T(4,128)}, u32[]{:S(2)}) copy-start(s32[2,4,512]{2,1,0:T(4,128)} %refs_4_.1) | copy-start | bytes 49156
  2.1 7.5 %collective-permute-start = (bf16[1072,128]{1,0:T(8,128)(2,1)S(1)}, bf16[1072,128]{1,0:T(8,128)(2,1)S(1)}, u32[]{:S(2)}, u32[]{:S(2)}) collective-permute-start(bf16[1072,128]{1,0:T(8,128)(2,1)S(1)} %shard_map.95.refs_5_.first), channel_id=1, source_target_pairs={{0,1},{1,0},{2,3},{3,2},{4,5},{5,4},{6,7},{7,6},{8,9},{9,8},{10,11... | collective-permute-start | bytes 823304 | tf_op jit(solution)/shard_map/ppermute | solution.py:529
  4.0 0.7 %copy-start.3 = (f32[8]{0:T(128)S(1)}, f32[8]{0:T(128)}, u32[]{:S(2)}) copy-start(f32[8]{0:T(128)} %refs_2_.1) | copy-start | bytes 100
  6.8 9.7 %collective-permute-start.2 = (bf16[1024,128]{1,0:T(8,128)(2,1)S(1)}, bf16[1024,128]{1,0:T(8,128)(2,1)S(1)}, u32[]{:S(2)}, u32[]{:S(2)}) collective-permute-start(bf16[1024,128]{1,0:T(8,128)(2,1)S(1)} %get-tuple-element.19), channel_id=1, source_target_pairs={{1,2},{3,4},{5,6},{2,1},{4,3},{6,5},{9,10},{11,12},{13,14},{10,9},... | collective-permute-start | bytes 786440 | tf_op jit(solution)/shard_map/ppermute | solution.py:529
  10.3 8.9 %collective-permute-start.4 = (bf16[96,128]{1,0:T(8,128)(2,1)S(1)}, bf16[96,128]{1,0:T(8,128)(2,1)S(1)}, u32[]{:S(2)}, u32[]{:S(2)}) collective-permute-start(bf16[96,128]{1,0:T(8,128)(2,1)S(1)} %get-tuple-element.24.refs_4_), channel_id=1, source_target_pairs={{0,2},{1,3},{2,0},{3,1},{4,6},{5,7},{6,4},{7,5},{8,10},{9,11},{10,... | collective-permute-start | bytes 73736 | tf_op jit(solution)/shard_map/ppermute | solution.py:539
  10.5 18.9 %collective-permute-start.1 = (bf16[1056,128]{1,0:T(8,128)(2,1)S(1)}, bf16[1056,128]{1,0:T(8,128)(2,1)S(1)}, u32[]{:S(2)}, u32[]{:S(2)}) collective-permute-start(bf16[1056,128]{1,0:T(8,128)(2,1)S(1)} %get-tuple-element.18.after), channel_id=1, source_target_pairs={{0,1},{1,0},{2,3},{3,2},{4,5},{5,4},{6,7},{7,6},{8,9},{9,8},{10,11... | collective-permute-start | bytes 811016 | tf_op jit(solution)/shard_map/ppermute | solution.py:529
  17.2 12.2 %collective-permute-start.3 = (bf16[1056,128]{1,0:T(8,128)(2,1)S(1)}, bf16[1056,128]{1,0:T(8,128)(2,1)S(1)}, u32[]{:S(2)}, u32[]{:S(2)}) collective-permute-start(bf16[1056,128]{1,0:T(8,128)(2,1)S(1)} %get-tuple-element.20), channel_id=1, source_target_pairs={{1,2},{3,4},{5,6},{2,1},{4,3},{6,5},{9,10},{11,12},{13,14},{10,9},... | collective-permute-start | bytes 811016 | tf_op jit(solution)/shard_map/ppermute | solution.py:529
  21.1 10.5 %collective-permute-start.5 = (bf16[192,128]{1,0:T(8,128)(2,1)S(1)}, bf16[192,128]{1,0:T(8,128)(2,1)S(1)}, u32[]{:S(2)}, u32[]{:S(2)}) collective-permute-start(bf16[192,128]{1,0:T(8,128)(2,1)S(1)} %get-tuple-element.26.refs_1_), channel_id=1, source_target_pairs={{0,4},{1,5},{2,6},{3,7},{4,0},{5,1},{6,2},{7,3},{8,12},{9,13},{10,... | collective-permute-start | bytes 147464 | tf_op jit(solution)/shard_map/ppermute | solution.py:544
  29.4 4.1 %collective-permute-start.8 = (f32[2,4,512]{2,1,0:T(4,128)S(1)}, f32[2,4,512]{2,1,0:T(4,128)S(1)}, u32[]{:S(2)}, u32[]{:S(2)}) collective-permute-start(f32[2,4,512]{2,1,0:T(4,128)S(1)} %shard_map.103.a), channel_id=1, source_target_pairs={{0,24},{8,16},{16,8},{24,0},{1,25},{9,17},{17,9},{25,1},{2,26},{10... | collective-permute-start | bytes 49160 | tf_op jit(solution)/shard_map/ppermute | solution.py:550
  31.1 2.6 %collective-permute-start.7 = (f32[2,4,512]{2,1,0:T(4,128)S(1)}, f32[2,4,512]{2,1,0:T(4,128)S(1)}, u32[]{:S(2)}, u32[]{:S(2)}) collective-permute-start(f32[2,4,512]{2,1,0:T(4,128)S(1)} %shard_map.103.a), channel_id=1, source_target_pairs={{0,16},{8,24},{16,0},{24,8},{1,17},{9,25},{17,1},{25,9},{2,18},{10... | collective-permute-start | bytes 49160 | tf_op jit(solution)/shard_map/ppermute | solution.py:550
  31.4 2.3 %collective-permute-start.6 = (f32[2,4,512]{2,1,0:T(4,128)S(1)}, f32[2,4,512]{2,1,0:T(4,128)S(1)}, u32[]{:S(2)}, u32[]{:S(2)}) collective-permute-start(f32[2,4,512]{2,1,0:T(4,128)S(1)} %shard_map.103.a), channel_id=1, source_target_pairs={{0,8},{8,0},{16,24},{24,16},{1,9},{9,1},{17,25},{25,17},{2,10},{10... | collective-permute-start | bytes 49160 | tf_op jit(solution)/shard_map/ppermute | solution.py:550

commit v4 on v3

--- a/solution.py
+++ b/solution.py
@@ -191,7 +191,7 @@
 
 
 def first_local(
-    count, adjoint, phase, rates, choice, mask, after, out, message, row, masked, state, first, missing, sems
+    count, adjoint, phase, rates, choice, mask, after, out, message, row, masked, near_walls, state, first, missing, sems
 ):
     layers, rows, depth = adjoint.shape
     copies = copy_all(
@@ -211,6 +211,20 @@
         out[d, pl.ds(y, CHUNK), :] = stepped
 
     local_step(own, layers_of(first), phase, row, count, emit)
+    four = (0, 1, depth - 1, depth - 2)
+    two = (0, depth - 1)
+    at = stored(layers - 1, layers)
+    for y in range(0, rows, 128):
+        span = pl.ds(y, 128)
+        high, low = split(out[layers - 1, span, :], 2)
+        high2, low2 = split(out[layers - 2, span, :], 2)
+        picked = pick_rows(high, four, 0, 16) + pick_rows(low, four, 4, 16) + pick_rows(phase[at, span, :], four, 12, 16)
+        picked = picked + pick_rows(high2, two, 8, 16) + pick_rows(low2, two, 10, 16)
+        message[pl.ds(2 * rows + y // 8, 16), :] = picked.astype(bf16)
+        steps = range(y, y + 128, CHUNK)
+        near = jnp.concatenate([read(own[-1], k) for k in steps])
+        both = jnp.concatenate([read(own[-2], k) + 2.0 * plane_part(own[-1], k) for k in steps])
+        near_walls[:, span] = pick_exact(near, four, 0) + pick_exact(both, four, 4)
 
 
 def make_first_local(adjoint, phase, rates, choice, mask, after, count):
@@ -219,11 +233,12 @@
         lambda *refs: first_local(count, *refs),
         (
             jax.ShapeDtypeStruct(adjoint.shape, f32),
-            jax.ShapeDtypeStruct((2 * rows, depth), bf16),
+            jax.ShapeDtypeStruct((2 * rows + rows // 8, depth), bf16),
             jax.ShapeDtypeStruct((8, depth), f32),
             jax.ShapeDtypeStruct(mask.shape, f32),
+            jax.ShapeDtypeStruct((8, rows), f32),
         ),
-        (VMEM,) * 4,
+        (VMEM,) * 5,
         [ANY, VMEM, SMEM, SMEM, VMEM, ANY],
         [padded(rows, depth, layers)] * 2 + [padded(rows, depth), pltpu.SemaphoreType.DMA((layers,))],
         cost(LONG),
@@ -244,23 +259,32 @@
         put_edge(y, edge(y) + mobility_step * curvature * near - stiffness_step * both)
 
 
+def pick_rows(v, heights, first_row, rows=8):
+    depth = v.shape[1]
+    row = lax.broadcasted_iota(jnp.int32, (rows, depth), 0) - first_row
+    lane = lax.broadcasted_iota(jnp.int32, (rows, depth), 1)
+    pick = jnp.zeros((rows, depth), f32)
+    for i, z in enumerate(heights):
+        pick = pick + jnp.where((row == i) & (lane == z), 1.0, 0.0)
+    return lax.dot_general(pick.astype(bf16), v, (((1,), (1,)), ((), ())), preferred_element_type=f32)
+
+
+def split(v, parts):
+    out = []
+    for _ in range(parts):
+        high = v.astype(bf16)
+        out.append(high)
+        v = v - high.astype(f32)
+    return out
+
+
+def pick_exact(v, heights, first_row):
+    return sum(pick_rows(part, heights, first_row) for part in split(v, 3))
+
+
 def wall_rows(v, first_row):
-    depth = v.shape[1]
-    row = lax.broadcasted_iota(jnp.int32, (8, depth), 0) - first_row
-    lane = lax.broadcasted_iota(jnp.int32, (8, depth), 1)
-    pick = ((row == 0) & (lane == 0)) | ((row == 1) & (lane == depth - 1))
-    pick = jnp.where(pick, 1.0, 0.0).astype(bf16)
-
-    def part(w):
-        return lax.dot_general(pick, w, (((1,), (1,)), ((), ())), preferred_element_type=f32)
-
-    if v.dtype == bf16:
-        return part(v)
-    high = v.astype(bf16)
-    rest = v - high.astype(f32)
-    middle = rest.astype(bf16)
-    low = (rest - middle.astype(f32)).astype(bf16)
-    return part(high) + part(middle) + part(low)
+    heights = (0, v.shape[1] - 1)
+    return pick_rows(v, heights, first_row) if v.dtype == bf16 else pick_exact(v, heights, first_row)
 
 
 def join_halo(side, message, pre, phase, out, halo):
@@ -282,25 +306,30 @@
     )
 
 
-def second_message(half, sent, missing, rows):
+def wall_parts(half, y):
     edge, inner = layers_of(half)
-    write_message(edge, inner, (missing, ()), sent, rows)
+    parts = 0.0
+    for i in range(2):
+        span = range(y + 128 * i, y + 128 * (i + 1), CHUNK)
+        both = jnp.concatenate([read(inner, k) + 2.0 * plane_part(edge, k) for k in span])
+        near = jnp.concatenate([read(edge, k) for k in span])
+        parts = parts + wall_rows(near, 4 * i) + wall_rows(both, 4 * i + 2)
+    return parts
+
+
+def put_walls(half, out, start):
+    rows = half.shape[1] - 2 * PAD
     for y in range(0, rows, 256):
-        wall_part = 0.0
-        for i in range(2):
-            span = range(y + 128 * i, y + 128 * (i + 1), CHUNK)
-            both = jnp.concatenate([read(inner, k) + 2.0 * plane_part(edge, k) for k in span])
-            near = jnp.concatenate([read(edge, k) for k in span])
-            wall_part = wall_part + wall_rows(near, 4 * i) + wall_rows(both, 4 * i + 2)
-        high = wall_part.astype(bf16)
-        low = (wall_part - high.astype(f32)).astype(bf16)
-        sent[pl.ds(2 * rows + y // 16, 16), :] = jnp.concatenate([high.astype(f32), low.astype(f32)]).astype(bf16)
-
-
-def middle_a(message, pre, phase, first, out, sent, block, halo, missing):
+        parts = wall_parts(half, y)
+        high = parts.astype(bf16).astype(f32)
+        out[pl.ds(start + y // 16, 16), :] = jnp.concatenate([high, parts - high]).astype(bf16)
+
+
+def middle_a(message, pre, phase, first, out, sent, early, block, halo, missing):
     rows, n = pre.shape[1], block.shape[0] // 2
     join_halo(0, message, pre, phase, out, halo)
-    second_message(out, sent, missing, rows)
+    write_message(*layers_of(out), (missing, ()), sent, rows)
+    put_walls(out, early, 0)
     block[pl.ds(0, n), :] = first[pl.ds(2 * rows, n), :]
     block[pl.ds(n, n), :] = message[pl.ds(2 * rows, n), :]
 
@@ -312,34 +341,58 @@
         middle_a,
         (
             jax.ShapeDtypeStruct((2, rows + 2 * PAD, depth), f32),
-            jax.ShapeDtypeStruct((2 * rows + rows // 16, depth), bf16),
+            jax.ShapeDtypeStruct((2 * rows, depth), bf16),
+            jax.ShapeDtypeStruct((rows // 16, depth), bf16),
             jax.ShapeDtypeStruct((2 * extra, depth), bf16),
         ),
-        (VMEM,) * 3,
+        (VMEM,) * 4,
         [VMEM] * 4,
         [padded(rows, depth)] * 2,
         cost(LONG),
     )(message, pre, phase, first)
 
 
-def middle_b(message, pre, phase, after, out, sent, halo, missing):
+def partner_walls(message, near_walls, rows, present):
+    sent = [message[pl.ds(2 * rows + y // 8, 16), :].astype(f32) for y in range(0, rows, 128)]
+    sent = jnp.concatenate(sent, axis=1)
+    here = near_walls[0:4, :]
+    near = sent[0:4] + sent[4:8] + mobility_step * curvature_of(sent[12:16]) * here
+    near = near - stiffness_step * near_walls[4:8, :]
+    far = sent[8:10] + sent[10:12]
+    lane = lax.broadcasted_iota(jnp.int32, (1, rows), 1)
+    out = []
+    for wall in range(2):
+        v = near[2 * wall : 2 * wall + 1]
+        along = jnp.where(lane == 0, 0.0, pltpu.roll(v, 1, 1)) + jnp.where(lane == rows - 1, 0.0, pltpu.roll(v, rows - 1, 1))
+        plane = along + near[2 * wall + 1 : 2 * wall + 2] - 6.0 * v
+        both = far[wall : wall + 1] - stiffness_step * here[2 * wall : 2 * wall + 1] + 2.0 * plane
+        out.append((present * v, present * both))
+    return [out[0][0], out[1][0], out[0][1], out[1][1]]
+
+
+def middle_b(count, message, pre, phase, near_walls, after, out, sent, walls, halo, missing):
+    rows = pre.shape[1]
     join_halo(1, message, pre, phase, out, halo)
-    second_message(out, sent, missing, pre.shape[1])
-
-
-def make_middle_b(message, pre, phase, after):
+    write_message(*layers_of(out), (missing, ()), sent, rows)
+    walls[...] = jnp.zeros(walls.shape, f32)
+    for i, v in enumerate(partner_walls(message, near_walls, rows, has_partner(count)[1])):
+        walls[i : i + 1, :] = v
+
+
+def make_middle_b(message, pre, phase, near_walls, after, count):
     layers, rows, depth = pre.shape
     return call(
-        middle_b,
+        lambda *refs: middle_b(count, *refs),
         (
             jax.ShapeDtypeStruct((2, rows + 2 * PAD, depth), f32),
-            jax.ShapeDtypeStruct((2 * rows + rows // 16, depth), bf16),
+            jax.ShapeDtypeStruct((2 * rows, depth), bf16),
+            jax.ShapeDtypeStruct((8, rows), f32),
         ),
-        (VMEM,) * 2,
-        [VMEM, VMEM, VMEM, ANY],
+        (VMEM,) * 3,
+        [VMEM] * 4 + [ANY],
         [padded(rows, depth)] * 2,
         cost(LONG),
-    )(message, pre, phase, after)
+    )(message, pre, phase, near_walls, after)
 
 
 def second_local(count, side_a, side_b, phase, row, own, other, out, wall, phase_wall, block, first):
@@ -377,7 +430,7 @@
         (VMEM,) * 4,
         [VMEM] * 6,
         [padded(rows, depth, layers)],
-        cost(2 * 10**9),
+        cost(13 * 10**8),
     )(side_a, side_b, phase, row, own, other)
 
 
@@ -411,34 +464,23 @@
         lambda *refs: injection(n, *refs),
         jax.ShapeDtypeStruct((layers, rows, depth), f32),
         VMEM,
-        [VMEM] * (1 + len(sources)),
+        [VMEM] + [VMEM] * len(sources),
         [pltpu.VMEM((8, total), jnp.int32), pltpu.VMEM((total, 2 * depth), bf16)],
-        cost(1),
+        cost(6 * 10**8),
     )(phase, *sources)
 
 
-def unpack_walls(message, rows, out):
-    for y in range(0, rows, 256):
-        both = message[pl.ds(2 * rows + y // 16, 16), :].astype(f32)
+def unpack_walls(message, out):
+    for y in range(0, out.shape[1], 256):
+        both = message[pl.ds(y // 16, 16), :].astype(f32)
         both = both[:8] + both[8:]
         for i in range(2):
             out[:4, pl.ds(y + 128 * i, 128)] = both[4 * i : 4 * i + 4]
 
 
-def make_unpack(message, rows):
-    return call(
-        lambda message, out: unpack_walls(message, rows, out),
-        jax.ShapeDtypeStruct((8, rows), f32),
-        VMEM,
-        [VMEM],
-        [],
-        cost(14 * 10**8),
-    )(message)
-
-
-def wall_kernel(wall, phase_wall, from_a, message_b, mask, out, from_b):
+def wall_kernel(wall, phase_wall, early_a, from_b, mask, out, from_a):
     layers = wall.shape[0]
-    unpack_walls(message_b, wall.shape[2], from_b)
+    unpack_walls(early_a, from_a)
     odd = is_odd()
     terms = []
     for d in range(layers):
@@ -454,23 +496,48 @@
         out[:, l, :] = mask[:, l, :] * jnp.where(odd, terms[l], terms[layers - 1 - l])
 
 
-def make_walls(wall, phase_wall, from_a, message_b, mask):
-    held = pltpu.VMEM(wall.shape[1:], f32)
+def make_walls(wall, phase_wall, early_a, from_b, mask):
     return call(
         wall_kernel,
         jax.ShapeDtypeStruct(mask.shape, f32),
         VMEM,
         [VMEM] * 5,
-        [held],
-        cost(LONG),
-    )(wall, phase_wall, from_a, message_b, mask)
-
-
-def final(message_a, message_b, pre, added, phase, out, token, planes, halo, sems):
+        [pltpu.VMEM(wall.shape[1:], f32)],
+        cost(55 * 10**7),
+    )(wall, phase_wall, early_a, from_b, mask)
+
+
+def halo_terms(layers, message, phase, after, out, halo):
+    def put(layer):
+        def store(y, v):
+            out[layer, pl.ds(y, CHUNK), :] = v
+
+        return store
+
+    def nothing(y):
+        return 0.0
+
+    add_halo(message, nothing, nothing, (halo, ()), phase, stored(0, layers), phase.shape[1], put(0), put(1))
+
+
+def make_halo_terms(message, phase, after):
+    layers, rows, depth = phase.shape
+    return call(
+        lambda *refs: halo_terms(layers, *refs),
+        jax.ShapeDtypeStruct((2, rows, depth), f32),
+        VMEM,
+        [VMEM, VMEM, ANY],
+        [padded(rows, depth)],
+        cost(6 * 10**8),
+    )(message, phase, after)
+
+
+def final(terms_a, message_b, pre, added, phase, *refs):
+    walls, (out, total, planes, halo, sems) = refs[:-5], refs[-5:]
     layers, rows, depth = pre.shape
     half = rows // 2
     copies = []
-    token[...] = jnp.zeros(token.shape, f32)
+    total[...] = (walls[0][...] + walls[1][...]) + (walls[2][...] + walls[3][...]) if len(walls) == 4 else walls[0][...]
 
     def put(d):
         def store(y, v):
@@ -488,32 +555,25 @@
     def get(d):
         return lambda y: pre[d, pl.ds(y, CHUNK), :]
 
-    for message, one, two in ((message_a, 0, 1), (message_b, layers - 1, layers - 2)):
-        add_halo(message, get(one), get(two), (halo, ()), phase, stored(one, layers), rows, put(one), put(two))
+    for d in range(2):
+        for y in starts(rows):
+            put(d)(y, get(d)(y) + terms_a[d, pl.ds(y, CHUNK), :])
+    one, two = layers - 1, layers - 2
+    add_halo(message_b, get(one), get(two), (halo, ()), phase, stored(one, layers), rows, put(one), put(two))
     for c in copies:
         c.wait()
 
 
-def make_final(message_a, message_b, pre, added, phase):
+def make_final(terms_a, message_b, pre, added, phase, walls):
     layers, rows, depth = pre.shape
     return call(
         final,
-        (jax.ShapeDtypeStruct(pre.shape, f32), jax.ShapeDtypeStruct((8, depth), f32)),
+        (jax.ShapeDtypeStruct(pre.shape, f32), jax.ShapeDtypeStruct(walls[0].shape, f32)),
         (ANY, VMEM),
-        [VMEM] * 5,
+        [VMEM] * (5 + len(walls)),
         [pltpu.VMEM(pre.shape, f32), padded(rows, depth), pltpu.SemaphoreType.DMA((2 * layers,))],
         cost(1),
-    )(message_a, message_b, pre, added, phase)
-
-
-def add_up(a, b, c, d, after, out):
-    out[...] = (a[...] + b[...]) + (c[...] + d[...])
-
-
-def make_sum(parts, after):
-    return call(add_up, jax.ShapeDtypeStruct(parts[0].shape, f32), VMEM, [VMEM] * 4 + [ANY], [], cost(1))(
-        *parts, after
-    )
+    )(terms_a, message_b, pre, added, phase, *walls)
 
 
 def on_device(adjoint, phase, targets, owners, target_cell, rate_index, inflow_rates, wall_mask):
@@ -532,25 +592,27 @@
     few = count == 8
     first = make_first_message(state, targets, owners, target_cell)
     from_a = send(first, 0)
-    pre, message, row, mask = make_first_local(state, phase, inflow_rates, rate_index, wall_mask, first, count)
+    pre, message, row, mask, near_walls = make_first_local(state, phase, inflow_rates, rate_index, wall_mask, first, count)
     from_b = send(message, 1)
-    half_a, message, pair = make_middle_a(from_a, pre, phase, first)
+    half_a, message, early, pair = make_middle_a(from_a, pre, phase, first)
+    early = send(early, 0)
     later_a = send(message, 0)
-    beside = lax.ppermute(pair, "slab", [(i, i ^ 2) for i in range(count)]) if few else pair
-    half_b, message = make_middle_b(from_b, pre, phase, message)
+    beside = lax.ppermute(pair, "slab", [(i, i ^ 4) for i in range(count)]) if few else pair
+    half_b, message, walls_b = make_middle_b(from_b, pre, phase, near_walls, message, count)
     later_b = send(message, 1)
     pre, wall, phase_wall, four = make_second_local(half_a, half_b, phase, row, pair, beside, count)
     if few:
-        blocks = [four, lax.ppermute(four, "slab", [(i, i ^ 4) for i in range(count)])]
+        blocks = [four, lax.ppermute(four, "slab", [(i, i ^ 2) for i in range(count)])]
     else:
         blocks = [lax.all_gather(first[2 * state.shape[1] :], "slab", axis=0, tiled=True)]
-    part = make_walls(wall, phase_wall, make_unpack(later_a, state.shape[1]), later_b, mask)
-    conditions = lax.axis_size("cond")
-    if conditions == 4:
-        parts = [part] + [lax.ppermute(part, "cond", [(i, i ^ k) for i in range(4)]) for k in (1, 2, 3)]
+    part = make_walls(wall, phase_wall, early, walls_b, mask)
+    if lax.axis_size("cond") == 4:
+        walls = [part] + [lax.ppermute(part, "cond", [(i, i ^ k) for i in range(4)]) for k in (1, 2, 3)]
+    else:
+        walls = [lax.psum(part, "cond")]
     added = make_injection(phase, n, blocks)
-    out, token = make_final(later_a, later_b, pre, added, phase)
-    wall_gradient = make_sum(parts, token) if conditions == 4 else lax.psum(part, "cond")
+    terms = make_halo_terms(later_a, phase, added)
+    out, wall_gradient = make_final(terms, later_b, pre, added, phase, walls)
     return out[None], wall_gradient
 
 

time: 35 us -> 33.2 us (0.949)
  the two profiles are of different devices: /device:TPU:25 before, /device:TPU:0 now
where the time goes in v4:
time: 33.2 us; the launch traced here: 33 us
  starting transfers between devices  14.6 us (44%)
  Pallas kernels  9.07 us (27%)
  waiting for transfers between devices  7.26 us (22%)
  between operations  1.43 us (4%)
  local copies, waits for them, and re-layouts  0.63 us (2%)
    ppermute x5, starting transfers between devices, send(): return lax.ppermute(v, 'slab', pairs[side])  6.64 us
    ppermute x1, starting transfers between devices, on_device(): lax.ppermute(four, 'slab', [(i, i ^ 2) for i in range(count)])  3.66 us
    ppermute x1, starting transfers between devices, on_device(): lax.ppermute(pair, 'slab', [(i, i ^ 4) for i in range(count)])  2.59 us
    ppermute x1, waiting for transfers between devices, on_device(): lax.ppermute(four, 'slab', [(i, i ^ 2) for i in range(count)])  2.31 us
    ppermute x5, waiting for transfers between devices, send(): return lax.ppermute(v, 'slab', pairs[side])  2.3 us
    pallas_call x1, Pallas kernels, make_first_local(): call(lambda *refs: first_local(count, *refs), (jax.ShapeDtypeStruct(adjoi...  2.28 us
    ppermute x1, waiting for transfers between devices, on_device(): lax.ppermute(pair, 'slab', [(i, i ^ 4) for i in range(count)])  2.23 us
    pallas_call x1, Pallas kernels, make_second_local(): call(lambda *refs: second_local(count, *refs), (jax.ShapeDtypeStruct((lay...  1.8 us
  transfers between devices with their start and end apart: 10, of which 4 were waited for; matrix products, arithmetic and copies ran while one was open for 0% of the time, Pallas kernels for 18%

profile of v4, /device:TPU:0, one launch (start us, length us, event | category | flops | bytes accessed | tf_op | source)
XLA Modules:
  0.0 33.0 jit_solution(13682024069976471727)
XLA Ops:
  0.6 0.0 copy-start
  0.6 0.0 copy-start.1
  0.7 1.4 %shard_map.95.refs_5_.first = bf16[1072,128]{1,0:T(8,128)(2,1)S(1)} custom-call(f32[4,512,128]{2,1,0:T(8,128)} %bitcast.12, bf16[32,128]{1,0:T(8,128)(2,1)} %bitcast.15, s32[1,32]{1,0:T(1,128)} %bitcast.16, s32[1,32]{1,0:T(1,128)} %cells.1), custom_call_target="tpu_custom_call" | custom-call | flops 10000000000 | bytes 1 | tf_op jit(solution)/shard_map/pallas_call | solution.py:177
  2.1 3.0 %collective-permute-start = (bf16[1072,128]{1,0:T(8,128)(2,1)S(1)}, bf16[1072,128]{1,0:T(8,128)(2,1)S(1)}, u32[]{:S(2)}, u32[]{:S(2)}) collective-permute-start(bf16[1072,128]{1,0:T(8,128)(2,1)S(1)} %shard_map.95.refs_5_.first), channel_id=1, source_target_pairs={{0,1},{1,0},{2,3},{3,2},{4,5},{5,4},{6,7},{7,6},{8,9},{9,8},{10,11... | collective-permute-start | bytes 823304 | tf_op jit(solution)/shard_map/ppermute | solution.py:589
  5.8 0.0 copy-start.3
  5.8 0.6 %copy-done.3 = f32[8]{0:T(128)S(1)} copy-done((f32[8]{0:T(128)S(1)}, f32[8]{0:T(128)}, u32[]{:S(2)}) %copy-start.3) | copy-done | bytes 56
  6.4 2.3 %shard_map.96 = (f32[4,512,128]{2,1,0:T(8,128)S(1)}, bf16[1088,128]{1,0:T(8,128)(2,1)S(1)}, f32[8,128]{1,0:T(8,128)S(1)}, f32[2,4,512]{2,1,0:T(4,128)S(1)}, f32[8,512]{1,0:T(8,128)S(1)}) custom-call(f32[4,512,128]{2,1,0:T(8,128)S(1)} %bitcast.13, bf16[4,512,128]{2,1,0:T(8,128)(2,1)S(1)} %bitcast.5, f32[8]{0:T(128)S(1)} %copy-done.3, s32[1]{0:T(128)S(6)} %copy.10.refs_3_, ...), custom_call_target="tpu_custom_call" | custom-call | flops 10000000000 | bytes 1 | tf_op jit(solution)/shard_map/pallas_call | solution.py:232
  8.7 0.7 %collective-permute-start.2 = (bf16[1088,128]{1,0:T(8,128)(2,1)S(1)}, bf16[1088,128]{1,0:T(8,128)(2,1)S(1)}, u32[]{:S(2)}, u32[]{:S(2)}) collective-permute-start(bf16[1088,128]{1,0:T(8,128)(2,1)S(1)} %get-tuple-element.23), channel_id=1, source_target_pairs={{1,2},{3,4},{5,6},{2,1},{4,3},{6,5},{9,10},{11,12},{13,14},{10,9},... | collective-permute-start | bytes 835592 | tf_op jit(solution)/shard_map/ppermute | solution.py:589
  9.4 2.3 %collective-permute-done.message = bf16[1072,128]{1,0:T(8,128)(2,1)S(1)} collective-permute-done((bf16[1072,128]{1,0:T(8,128)(2,1)S(1)}, bf16[1072,128]{1,0:T(8,128)(2,1)S(1)}, u32[]{:S(2)}, u32[]{:S(2)}) %collective-permute-start) | collective-permute-done | bytes 274464 | tf_op jit(solution)/shard_map/ppermute | solution.py:589
  11.7 0.7 %shard_map.97 = (f32[2,528,128]{2,1,0:T(8,128)S(1)}, bf16[1024,128]{1,0:T(8,128)(2,1)S(1)}, bf16[32,128]{1,0:T(8,128)(2,1)S(1)}, bf16[96,128]{1,0:T(8,128)(2,1)S(1)}) custom-call(bf16[1072,128]{1,0:T(8,128)(2,1)S(1)} %collective-permute-done.message, f32[4,512,128]{2,1,0:T(8,128)S(1)} %get-tuple-element.20.pre.refs_1_, bf16[4,512,128]{2,1,0:T(8,128)(2,1)S(1)} %bitcast.6, ...), custom_call_target="tpu_custom_call" | custom-call | flops 10000000000 | bytes 1 | tf_op jit(solution)/shard_map/pallas_call | solution.py:340
  12.3 2.0 %collective-permute-start.6 = (bf16[32,128]{1,0:T(8,128)(2,1)S(1)}, bf16[32,128]{1,0:T(8,128)(2,1)S(1)}, u32[]{:S(2)}, u32[]{:S(2)}) collective-permute-start(bf16[32,128]{1,0:T(8,128)(2,1)S(1)} %get-tuple-element.33), channel_id=1, source_target_pairs={{0,1},{1,0},{2,3},{3,2},{4,5},{5,4},{6,7},{7,6},{8,9},{9,8},{10,11... | collective-permute-start | bytes 24584 | tf_op jit(solution)/shard_map/ppermute | solution.py:589
  14.3 2.6 %collective-permute-start.3 = (bf16[96,128]{1,0:T(8,128)(2,1)S(1)}, bf16[96,128]{1,0:T(8,128)(2,1)S(1)}, u32[]{:S(2)}, u32[]{:S(2)}) collective-permute-start(bf16[96,128]{1,0:T(8,128)(2,1)S(1)} %get-tuple-element.27.refs_4_), channel_id=1, source_target_pairs={{0,4},{1,5},{2,6},{3,7},{4,0},{5,1},{6,2},{7,3},{8,12},{9,13},{10,... | collective-permute-start | bytes 73736 | tf_op jit(solution)/shard_map/ppermute | solution.py:600
  16.9 0.3 collective-permute-start.1
  17.2 0.0 collective-permute-done.2.refs_0_
  17.2 0.4 %shard_map.98 = (f32[2,528,128]{2,1,0:T(8,128)S(1)}, bf16[1024,128]{1,0:T(8,128)(2,1)S(1)}, f32[8,512]{1,0:T(8,128)S(1)}) custom-call(bf16[1088,128]{1,0:T(8,128)(2,1)S(1)} %collective-permute-done.2.refs_0_, f32[4,512,128]{2,1,0:T(8,128)S(1)} %get-tuple-element.20.pre.refs_1_, bf16[4,512,128]{2,1,0:T(8,128)(2,1)S(1)} %bitcast.7, ...), custom_call_target="tpu_custom_call" | custom-call | flops 10000000000 | bytes 1 | tf_op jit(solution)/shard_map/pallas_call | solution.py:384
  17.6 0.7 %collective-permute-start.5 = (bf16[1024,128]{1,0:T(8,128)(2,1)S(1)}, bf16[1024,128]{1,0:T(8,128)(2,1)S(1)}, u32[]{:S(2)}, u32[]{:S(2)}) collective-permute-start(bf16[1024,128]{1,0:T(8,128)(2,1)S(1)} %get-tuple-element.29), channel_id=1, source_target_pairs={{1,2},{3,4},{5,6},{2,1},{4,3},{6,5},{9,10},{11,12},{13,14},{10,9},... | collective-permute-start | bytes 786440 | tf_op jit(solution)/shard_map/ppermute | solution.py:589
  18.3 2.2 %collective-permute-done.3.refs_5_ = bf16[96,128]{1,0:T(8,128)(2,1)S(1)} collective-permute-done((bf16[96,128]{1,0:T(8,128)(2,1)S(1)}, bf16[96,128]{1,0:T(8,128)(2,1)S(1)}, u32[]{:S(2)}, u32[]{:S(2)}) %collective-permute-start.3) | collective-permute-done | bytes 24608 | tf_op jit(solution)/shard_map/ppermute | solution.py:600
  20.5 1.8 %shard_map.99 = (f32[4,512,128]{2,1,0:T(8,128)S(1)}, f32[4,8,512]{2,1,0:T(8,128)S(1)}, f32[4,8,512]{2,1,0:T(8,128)S(1)}, bf16[192,128]{1,0:T(8,128)(2,1)S(1)}) custom-call(f32[2,528,128]{2,1,0:T(8,128)S(1)} %get-tuple-element.22.refs_0_, f32[2,528,128]{2,1,0:T(8,128)S(1)} %get-tuple-element.25.refs_1_, bf16[4,512,128]{2,1,0:T(8,128)(2,1)S(1)} %bitcast.8, ...), custom_call_target="tpu_custom_call" | custom-call | flops 1300000000 | bytes 1 | tf_op jit(solution)/shard_map/pallas_call | solution.py:422
  22.3 3.7 %collective-permute-start.4 = (bf16[192,128]{1,0:T(8,128)(2,1)S(1)}, bf16[192,128]{1,0:T(8,128)(2,1)S(1)}, u32[]{:S(2)}, u32[]{:S(2)}) collective-permute-start(bf16[192,128]{1,0:T(8,128)(2,1)S(1)} %get-tuple-element.28.refs_1_), channel_id=1, source_target_pairs={{0,2},{1,3},{2,0},{3,1},{4,6},{5,7},{6,4},{7,5},{8,10},{9,11},{10,... | collective-permute-start | bytes 147464 | tf_op jit(solution)/shard_map/ppermute | solution.py:605
  26.0 0.0 collective-permute-done.6.early_a
  26.0 0.1 collective-permute-start.9
  26.1 1.7 %collective-permute-start.8 = (f32[2,4,512]{2,1,0:T(4,128)S(1)}, f32[2,4,512]{2,1,0:T(4,128)S(1)}, u32[]{:S(2)}, u32[]{:S(2)}) collective-permute-start(f32[2,4,512]{2,1,0:T(4,128)S(1)} %shard_map.102.refs_0_), channel_id=1, source_target_pairs={{0,16},{8,24},{16,0},{24,8},{1,17},{9,25},{17,1},{25,9},{2,18},{10... | collective-permute-start | bytes 49160 | tf_op jit(solution)/shard_map/ppermute | solution.py:610
  27.8 2.3 %collective-permute-done.4.refs_2_ = bf16[192,128]{1,0:T(8,128)(2,1)S(1)} collective-permute-done((bf16[192,128]{1,0:T(8,128)(2,1)S(1)}, bf16[192,128]{1,0:T(8,128)(2,1)S(1)}, u32[]{:S(2)}, u32[]{:S(2)}) %collective-permute-start.4) | collective-permute-done | bytes 49184 | tf_op jit(solution)/shard_map/ppermute | solution.py:605
  30.1 0.0 collective-permute-start.7
  30.1 0.5 %shard_map.100.refs_2_.added = f32[4,512,128]{2,1,0:T(8,128)S(1)} custom-call(bf16[4,512,128]{2,1,0:T(8,128)(2,1)S(1)} %bitcast.9, bf16[192,128]{1,0:T(8,128)(2,1)S(1)} %get-tuple-element.28.refs_1_, bf16[192,128]{1,0:T(8,128)(2,1)S(1)} %collective-permute-done.4.refs_2_), custom_call_target="tpu_custom_call" | custom-call | flops 600000000 | bytes 1 | tf_op jit(solution)/shard_map/pallas_call | solution.py:463
  30.6 0.0 collective-permute-done.1.refs_0_
  30.6 0.2 shard_map.101.terms_a
  30.8 0.0 collective-permute-done.9.refs_3_
  30.8 0.0 collective-permute-done.8.refs_2_
  30.8 0.4 %collective-permute-done.7.refs_1_ = f32[2,4,512]{2,1,0:T(4,128)S(1)} collective-permute-done((f32[2,4,512]{2,1,0:T(4,128)S(1)}, f32[2,4,512]{2,1,0:T(4,128)S(1)}, u32[]{:S(2)}, u32[]{:S(2)}) %collective-permute-start.7) | collective-permute-done | bytes 16416 | tf_op jit(solution)/shard_map/ppermute | solution.py:610
  31.2 0.0 collective-permute-done.5.message_b
  31.3 1.8 %shard_map.103 = (f32[4,512,128]{2,1,0:T(8,128)}, f32[2,4,512]{2,1,0:T(4,128)}) custom-call(f32[2,512,128]{2,1,0:T(8,128)S(1)} %shard_map.101.terms_a, bf16[1024,128]{1,0:T(8,128)(2,1)S(1)} %collective-permute-done.5.message_b, f32[4,512,128]{2,1,0:T(8,128)S(1)} %get-tuple-element.30.pre, f32[4,512,128]{2,1,0:T(8,128)S(1)} %shard_map.100.refs_2_.added, ...), custom_call_target="tpu_custom_call" | custom-call | flops 1 | bytes 1 | tf_op jit(solution)/shard_map/pallas_call | solution.py:569
  (5 shorter events, 0.1 us)
Async XLA Ops:
  0.6 5.1 %copy-start = (bf16[1,4,512,128]{3,2,1,0:T(8,128)(2,1)S(1)}, bf16[1,4,512,128]{3,2,1,0:T(8,128)(2,1)}, u32[]{:S(2)}) copy-start(bf16[1,4,512,128]{3,2,1,0:T(8,128)(2,1)} %param.9) | copy-start | bytes 1572868
  0.6 5.1 %copy-start.1 = (f32[1,4,512,128]{3,2,1,0:T(8,128)S(1)}, f32[1,4,512,128]{3,2,1,0:T(8,128)}, u32[]{:S(2)}) copy-start(f32[1,4,512,128]{3,2,1,0:T(8,128)} %param.8) | copy-start | bytes 3145732
  0.7 5.1 %copy-start.2 = (s32[2,4,512]{2,1,0:T(4,128)S(1)}, s32[2,4,512]{2,1,0:T(4,128)}, u32[]{:S(2)}) copy-start(s32[2,4,512]{2,1,0:T(4,128)} %refs_4_.1) | copy-start | bytes 49156
  2.1 9.6 %collective-permute-start = (bf16[1072,128]{1,0:T(8,128)(2,1)S(1)}, bf16[1072,128]{1,0:T(8,128)(2,1)S(1)}, u32[]{:S(2)}, u32[]{:S(2)}) collective-permute-start(bf16[1072,128]{1,0:T(8,128)(2,1)S(1)} %shard_map.95.refs_5_.first), channel_id=1, source_target_pairs={{0,1},{1,0},{2,3},{3,2},{4,5},{5,4},{6,7},{7,6},{8,9},{9,8},{10,11... | collective-permute-start | bytes 823304 | tf_op jit(solution)/shard_map/ppermute | solution.py:589
  5.8 0.7 %copy-start.3 = (f32[8]{0:T(128)S(1)}, f32[8]{0:T(128)}, u32[]{:S(2)}) copy-start(f32[8]{0:T(128)} %refs_2_.1) | copy-start | bytes 100
  8.7 8.5 %collective-permute-start.2 = (bf16[1088,128]{1,0:T(8,128)(2,1)S(1)}, bf16[1088,128]{1,0:T(8,128)(2,1)S(1)}, u32[]{:S(2)}, u32[]{:S(2)}) collective-permute-start(bf16[1088,128]{1,0:T(8,128)(2,1)S(1)} %get-tuple-element.23), channel_id=1, source_target_pairs={{1,2},{3,4},{5,6},{2,1},{4,3},{6,5},{9,10},{11,12},{13,14},{10,9},... | collective-permute-start | bytes 835592 | tf_op jit(solution)/shard_map/ppermute | solution.py:589
  12.3 13.6 %collective-permute-start.6 = (bf16[32,128]{1,0:T(8,128)(2,1)S(1)}, bf16[32,128]{1,0:T(8,128)(2,1)S(1)}, u32[]{:S(2)}, u32[]{:S(2)}) collective-permute-start(bf16[32,128]{1,0:T(8,128)(2,1)S(1)} %get-tuple-element.33), channel_id=1, source_target_pairs={{0,1},{1,0},{2,3},{3,2},{4,5},{5,4},{6,7},{7,6},{8,9},{9,8},{10,11... | collective-permute-start | bytes 24584 | tf_op jit(solution)/shard_map/ppermute | solution.py:589
  14.3 6.2 %collective-permute-start.3 = (bf16[96,128]{1,0:T(8,128)(2,1)S(1)}, bf16[96,128]{1,0:T(8,128)(2,1)S(1)}, u32[]{:S(2)}, u32[]{:S(2)}) collective-permute-start(bf16[96,128]{1,0:T(8,128)(2,1)S(1)} %get-tuple-element.27.refs_4_), channel_id=1, source_target_pairs={{0,4},{1,5},{2,6},{3,7},{4,0},{5,1},{6,2},{7,3},{8,12},{9,13},{10,... | collective-permute-start | bytes 73736 | tf_op jit(solution)/shard_map/ppermute | solution.py:600
  16.9 13.7 %collective-permute-start.1 = (bf16[1024,128]{1,0:T(8,128)(2,1)S(1)}, bf16[1024,128]{1,0:T(8,128)(2,1)S(1)}, u32[]{:S(2)}, u32[]{:S(2)}) collective-permute-start(bf16[1024,128]{1,0:T(8,128)(2,1)S(1)} %get-tuple-element.21.refs_4_), channel_id=1, source_target_pairs={{0,1},{1,0},{2,3},{3,2},{4,5},{5,4},{6,7},{7,6},{8,9},{9,8},{10,11... | collective-permute-start | bytes 786440 | tf_op jit(solution)/shard_map/ppermute | solution.py:589
  17.6 13.7 %collective-permute-start.5 = (bf16[1024,128]{1,0:T(8,128)(2,1)S(1)}, bf16[1024,128]{1,0:T(8,128)(2,1)S(1)}, u32[]{:S(2)}, u32[]{:S(2)}) collective-permute-start(bf16[1024,128]{1,0:T(8,128)(2,1)S(1)} %get-tuple-element.29), channel_id=1, source_target_pairs={{1,2},{3,4},{5,6},{2,1},{4,3},{6,5},{9,10},{11,12},{13,14},{10,9},... | collective-permute-start | bytes 786440 | tf_op jit(solution)/shard_map/ppermute | solution.py:589
  22.3 7.8 %collective-permute-start.4 = (bf16[192,128]{1,0:T(8,128)(2,1)S(1)}, bf16[192,128]{1,0:T(8,128)(2,1)S(1)}, u32[]{:S(2)}, u32[]{:S(2)}) collective-permute-start(bf16[192,128]{1,0:T(8,128)(2,1)S(1)} %get-tuple-element.28.refs_1_), channel_id=1, source_target_pairs={{0,2},{1,3},{2,0},{3,1},{4,6},{5,7},{6,4},{7,5},{8,10},{9,11},{10,... | collective-permute-start | bytes 147464 | tf_op jit(solution)/shard_map/ppermute | solution.py:605
  26.0 4.8 %collective-permute-start.9 = (f32[2,4,512]{2,1,0:T(4,128)S(1)}, f32[2,4,512]{2,1,0:T(4,128)S(1)}, u32[]{:S(2)}, u32[]{:S(2)}) collective-permute-start(f32[2,4,512]{2,1,0:T(4,128)S(1)} %shard_map.102.refs_0_), channel_id=1, source_target_pairs={{0,24},{8,16},{16,8},{24,0},{1,25},{9,17},{17,9},{25,1},{2,26},{10... | collective-permute-start | bytes 49160 | tf_op jit(solution)/shard_map/ppermute | solution.py:610
  26.1 4.7 %collective-permute-start.8 = (f32[2,4,512]{2,1,0:T(4,128)S(1)}, f32[2,4,512]{2,1,0:T(4,128)S(1)}, u32[]{:S(2)}, u32[]{:S(2)}) collective-permute-start(f32[2,4,512]{2,1,0:T(4,128)S(1)} %shard_map.102.refs_0_), channel_id=1, source_target_pairs={{0,16},{8,24},{16,0},{24,8},{1,17},{9,25},{17,1},{25,9},{2,18},{10... | collective-permute-start | bytes 49160 | tf_op jit(solution)/shard_map/ppermute | solution.py:610
  30.1 1.2 %collective-permute-start.7 = (f32[2,4,512]{2,1,0:T(4,128)S(1)}, f32[2,4,512]{2,1,0:T(4,128)S(1)}, u32[]{:S(2)}, u32[]{:S(2)}) collective-permute-start(f32[2,4,512]{2,1,0:T(4,128)S(1)} %shard_map.102.refs_0_), channel_id=1, source_target_pairs={{0,8},{8,0},{16,24},{24,16},{1,9},{9,1},{17,25},{25,17},{2,10},{10... | collective-permute-start | bytes 49160 | tf_op jit(solution)/shard_map/ppermute | solution.py:610

commit v5 on v4

--- a/solution.py
+++ b/solution.py
@@ -391,8 +391,25 @@
         (VMEM,) * 3,
         [VMEM] * 4 + [ANY],
         [padded(rows, depth)] * 2,
-        cost(LONG),
+        cost(6 * 10**8),
     )(message, pre, phase, near_walls, after)
+
+
+def join(one, two, out):
+    n = one.shape[0]
+    out[pl.ds(0, n), :] = one[...]
+    out[pl.ds(n, n), :] = two[...]
+
+
+def make_join(one, two):
+    return call(
+        join,
+        jax.ShapeDtypeStruct((2 * one.shape[0], one.shape[1]), bf16),
+        VMEM,
+        [VMEM, VMEM],
+        [],
+        cost(15 * 10**8),
+    )(one, two)
 
 
 def second_local(count, side_a, side_b, phase, row, own, other, out, wall, phase_wall, block, first):
@@ -434,7 +451,7 @@
     )(side_a, side_b, phase, row, own, other)
 
 
-def injection(n, phase, *refs):
+def injection(n, phase, pre, *refs):
     sources, (out, index, rhs) = refs[:-3], refs[-3:]
     layers, rows, depth = out.shape
     position = lax.axis_index("slab").astype(f32)
@@ -454,20 +471,20 @@
             here = jnp.where(cell == index[0:1, :], 1.0, 0.0).astype(bf16)
             added = jnp.dot(here, rhs[...], preferred_element_type=f32)
             p = phase[at, pl.ds(y, 128), :].astype(f32)
-            out[d, pl.ds(y, 128), :] = added[:, :depth] * p - added[:, depth:]
-
-
-def make_injection(phase, n, sources):
+            out[d, pl.ds(y, 128), :] = pre[d, pl.ds(y, 128), :] + (added[:, :depth] * p - added[:, depth:])
+
+
+def make_injection(phase, n, pre, sources):
     layers, rows, depth = phase.shape
     total = sum(r.shape[0] // (n + 16) * n for r in sources)
     return call(
         lambda *refs: injection(n, *refs),
         jax.ShapeDtypeStruct((layers, rows, depth), f32),
         VMEM,
-        [VMEM] + [VMEM] * len(sources),
+        [VMEM, VMEM] + [VMEM] * len(sources),
         [pltpu.VMEM((8, total), jnp.int32), pltpu.VMEM((total, 2 * depth), bf16)],
-        cost(6 * 10**8),
-    )(phase, *sources)
+        cost(1),
+    )(phase, pre, *sources)
 
 
 def unpack_walls(message, out):
@@ -503,77 +520,89 @@
         VMEM,
         [VMEM] * 5,
         [pltpu.VMEM(wall.shape[1:], f32)],
-        cost(55 * 10**7),
+        cost(3 * 10**8),
     )(wall, phase_wall, early_a, from_b, mask)
 
 
-def halo_terms(layers, message, phase, after, out, halo):
-    def put(layer):
+def layers_at_a(message, phase, state, out, halo):
+    layers = state.shape[0]
+
+    def put(d):
         def store(y, v):
-            out[layer, pl.ds(y, CHUNK), :] = v
+            out[d, pl.ds(y, CHUNK), :] = v
 
         return store
 
-    def nothing(y):
-        return 0.0
-
-    add_halo(message, nothing, nothing, (halo, ()), phase, stored(0, layers), phase.shape[1], put(0), put(1))
-
-
-def make_halo_terms(message, phase, after):
+    def get(d):
+        return lambda y: state[d, pl.ds(y, CHUNK), :]
+
+    add_halo(message, get(0), get(1), (halo, ()), phase, stored(0, layers), phase.shape[1], put(0), put(1))
+
+
+def make_layers_at_a(message, phase, state):
     layers, rows, depth = phase.shape
     return call(
-        lambda *refs: halo_terms(layers, *refs),
+        layers_at_a,
         jax.ShapeDtypeStruct((2, rows, depth), f32),
         VMEM,
-        [VMEM, VMEM, ANY],
+        [VMEM] * 3,
         [padded(rows, depth)],
-        cost(6 * 10**8),
-    )(message, phase, after)
-
-
-def final(terms_a, message_b, pre, added, phase, *refs):
-    walls, (out, total, planes, halo, sems) = refs[:-5], refs[-5:]
-    layers, rows, depth = pre.shape
+        cost(15 * 10**8),
+    )(message, phase, state)
+
+
+def final(at_a, message_b, state, phase, *refs):
+    walls, (out, total, planes, summed, halo, sems) = refs[:-6], refs[-6:]
+    layers, rows, depth = state.shape
     half = rows // 2
     copies = []
-    total[...] = (walls[0][...] + walls[1][...]) + (walls[2][...] + walls[3][...]) if len(walls) == 4 else walls[0][...]
-
-    def put(d):
+
+    def send(source, target):
+        c = pltpu.make_async_copy(source, target, sems.at[len(copies)])
+        c.start()
+        copies.append(c)
+
+    for d in range(2):
+        send(at_a.at[d], out.at[stored(d, layers)])
+    if len(walls) == 4:
+        summed[...] = (walls[0][...] + walls[3][...]) + (walls[1][...] + walls[2][...])
+    else:
+        summed[...] = walls[0][...]
+    send(summed, total)
+
+    def put(i):
         def store(y, v):
-            planes[d, pl.ds(y, CHUNK), :] = v + added[d, pl.ds(y, CHUNK), :]
+            planes[i, pl.ds(y, CHUNK), :] = v
             if (y + CHUNK) % half == 0:
                 span = pl.ds(y + CHUNK - half, half)
-                c = pltpu.make_async_copy(
-                    planes.at[d, span], out.at[stored(d, layers), span], sems.at[len(copies)]
-                )
-                c.start()
-                copies.append(c)
+                send(planes.at[i, span], out.at[stored(layers - 1 - i, layers), span])
 
         return store
 
     def get(d):
-        return lambda y: pre[d, pl.ds(y, CHUNK), :]
-
-    for d in range(2):
-        for y in starts(rows):
-            put(d)(y, get(d)(y) + terms_a[d, pl.ds(y, CHUNK), :])
+        return lambda y: state[d, pl.ds(y, CHUNK), :]
+
     one, two = layers - 1, layers - 2
-    add_halo(message_b, get(one), get(two), (halo, ()), phase, stored(one, layers), rows, put(one), put(two))
+    add_halo(message_b, get(one), get(two), (halo, ()), phase, stored(one, layers), rows, put(0), put(1))
     for c in copies:
         c.wait()
 
 
-def make_final(terms_a, message_b, pre, added, phase, walls):
-    layers, rows, depth = pre.shape
+def make_final(at_a, message_b, state, phase, walls):
+    layers, rows, depth = state.shape
     return call(
         final,
-        (jax.ShapeDtypeStruct(pre.shape, f32), jax.ShapeDtypeStruct(walls[0].shape, f32)),
-        (ANY, VMEM),
-        [VMEM] * (5 + len(walls)),
-        [pltpu.VMEM(pre.shape, f32), padded(rows, depth), pltpu.SemaphoreType.DMA((2 * layers,))],
+        (jax.ShapeDtypeStruct(state.shape, f32), jax.ShapeDtypeStruct(walls[0].shape, f32)),
+        (ANY, ANY),
+        [VMEM] * (4 + len(walls)),
+        [
+            pltpu.VMEM((2, rows, depth), f32),
+            pltpu.VMEM(walls[0].shape, f32),
+            padded(rows, depth),
+            pltpu.SemaphoreType.DMA((7,)),
+        ],
         cost(1),
-    )(terms_a, message_b, pre, added, phase, *walls)
+    )(at_a, message_b, state, phase, *walls)
 
 
 def on_device(adjoint, phase, targets, owners, target_cell, rate_index, inflow_rates, wall_mask):
@@ -597,22 +626,23 @@
     half_a, message, early, pair = make_middle_a(from_a, pre, phase, first)
     early = send(early, 0)
     later_a = send(message, 0)
-    beside = lax.ppermute(pair, "slab", [(i, i ^ 4) for i in range(count)]) if few else pair
-    half_b, message, walls_b = make_middle_b(from_b, pre, phase, near_walls, message, count)
+    four = far = pair
+    if few:
+        four = make_join(pair, lax.ppermute(pair, "slab", [(i, i ^ 4) for i in range(count)]))
+        far = lax.ppermute(four, "slab", [(i, i ^ 2) for i in range(count)])
+    half_b, message, walls_b = make_middle_b(from_b, pre, phase, near_walls, four, count)
     later_b = send(message, 1)
-    pre, wall, phase_wall, four = make_second_local(half_a, half_b, phase, row, pair, beside, count)
-    if few:
-        blocks = [four, lax.ppermute(four, "slab", [(i, i ^ 2) for i in range(count)])]
-    else:
-        blocks = [lax.all_gather(first[2 * state.shape[1] :], "slab", axis=0, tiled=True)]
+    pre, wall, phase_wall, block = make_second_local(half_a, half_b, phase, row, four, far, count)
+    if not few:
+        block = lax.all_gather(first[2 * state.shape[1] :], "slab", axis=0, tiled=True)
     part = make_walls(wall, phase_wall, early, walls_b, mask)
     if lax.axis_size("cond") == 4:
-        walls = [part] + [lax.ppermute(part, "cond", [(i, i ^ k) for i in range(4)]) for k in (1, 2, 3)]
+        walls = [part] + [lax.ppermute(part, "cond", [(i, i ^ k) for i in range(4)]) for k in (3, 2, 1)]
     else:
         walls = [lax.psum(part, "cond")]
-    added = make_injection(phase, n, blocks)
-    terms = make_halo_terms(later_a, phase, added)
-    out, wall_gradient = make_final(terms, later_b, pre, added, phase, walls)
+    state = make_injection(phase, n, pre, [block])
+    at_a = make_layers_at_a(later_a, phase, state)
+    out, wall_gradient = make_final(at_a, later_b, state, phase, walls)
     return out[None], wall_gradient
 
 

time: 33.2 us -> 31.8 us (0.958)
  starting transfers between devices: 14.6 us -> 13 us
  waiting for transfers between devices: 7.26 us -> 8.15 us
  Pallas kernels: 9.07 us -> 8.42 us
    ppermute x1, starting transfers between devices: 3.66 us -> 1.88 us  [on_device(): far = lax.ppermute(four, 'slab', [(i, i ^ 2) for i in range(count)])]
    ppermute x1, waiting for transfers between devices: 2.23 us -> 3.24 us  [on_device(): lax.ppermute(pair, 'slab', [(i, i ^ 4) for i in range(count)])]
    ppermute x1, waiting for transfers between devices: 2.31 us -> 1.41 us  [on_device(): far = lax.ppermute(four, 'slab', [(i, i ^ 2) for i in range(count)])]
    ppermute x3, waiting for transfers between devices: 0.42 us -> 1.21 us  [on_device(): lax.ppermute(part, 'cond', [(i, i ^ k) for i in range(4)])]
    pallas_call x2 -> x3, Pallas kernels: 1.98 us -> 1.26 us  [the longest x1 1.04 us: make_final(): call(final, (jax.ShapeDtypeStruct(state.shape, f32), jax.ShapeDtypeStruct...]
  transfers between devices with their start and end apart: 10 -> 10, of which waited for: 4 -> 5; matrix products, arithmetic and copies ran while one was open for 0% -> 0% of each run, Pallas kernels for 18% -> 19%
where the time goes in v5:
time: 31.8 us; the launch traced here: 31.6 us
  starting transfers between devices  13 us (41%)
  Pallas kernels  8.42 us (26%)
  waiting for transfers between devices  8.15 us (26%)
  between operations  1.42 us (4%)
  local copies, waits for them, and re-layouts  0.63 us (2%)
    ppermute x5, starting transfers between devices, send(): return lax.ppermute(v, 'slab', pairs[side])  6.41 us
    ppermute x1, waiting for transfers between devices, on_device(): lax.ppermute(pair, 'slab', [(i, i ^ 4) for i in range(count)])  3.24 us
    ppermute x1, starting transfers between devices, on_device(): lax.ppermute(pair, 'slab', [(i, i ^ 4) for i in range(count)])  2.81 us
    ppermute x5, waiting for transfers between devices, send(): return lax.ppermute(v, 'slab', pairs[side])  2.29 us
    pallas_call x1, Pallas kernels, make_first_local(): call(lambda *refs: first_local(count, *refs), (jax.ShapeDtypeStruct(adjoi...  2.28 us
    ppermute x3, starting transfers between devices, on_device(): lax.ppermute(part, 'cond', [(i, i ^ k) for i in range(4)])  1.92 us
    ppermute x1, starting transfers between devices, on_device(): far = lax.ppermute(four, 'slab', [(i, i ^ 2) for i in range(count)])  1.88 us
    pallas_call x1, Pallas kernels, make_second_local(): call(lambda *refs: second_local(count, *refs), (jax.ShapeDtypeStruct((lay...  1.77 us
  transfers between devices with their start and end apart: 10, of which 5 were waited for; matrix products, arithmetic and copies ran while one was open for 0% of the time, Pallas kernels for 19%

profile of v5, /device:TPU:0, one launch (start us, length us, event | category | flops | bytes accessed | tf_op | source)
XLA Modules:
  0.0 31.6 jit_solution(185278607943853237)
XLA Ops:
  0.6 0.0 copy-start
  0.7 1.4 %shard_map.95.refs_5_.first = bf16[1072,128]{1,0:T(8,128)(2,1)S(1)} custom-call(f32[4,512,128]{2,1,0:T(8,128)} %bitcast.12, bf16[32,128]{1,0:T(8,128)(2,1)} %bitcast.15, s32[1,32]{1,0:T(1,128)} %bitcast.16, s32[1,32]{1,0:T(1,128)} %cells.1), custom_call_target="tpu_custom_call" | custom-call | flops 10000000000 | bytes 1 | tf_op jit(solution)/shard_map/pallas_call | solution.py:177
  2.1 3.0 %collective-permute-start = (bf16[1072,128]{1,0:T(8,128)(2,1)S(1)}, bf16[1072,128]{1,0:T(8,128)(2,1)S(1)}, u32[]{:S(2)}, u32[]{:S(2)}) collective-permute-start(bf16[1072,128]{1,0:T(8,128)(2,1)S(1)} %shard_map.95.refs_5_.first), channel_id=1, source_target_pairs={{0,1},{1,0},{2,3},{3,2},{4,5},{5,4},{6,7},{7,6},{8,9},{9,8},{10,11... | collective-permute-start | bytes 823304 | tf_op jit(solution)/shard_map/ppermute | solution.py:618
  5.8 0.0 copy-start.3
  5.8 0.6 %copy-done.3 = f32[8]{0:T(128)S(1)} copy-done((f32[8]{0:T(128)S(1)}, f32[8]{0:T(128)}, u32[]{:S(2)}) %copy-start.3) | copy-done | bytes 56
  6.4 2.3 %shard_map.96 = (f32[4,512,128]{2,1,0:T(8,128)S(1)}, bf16[1088,128]{1,0:T(8,128)(2,1)S(1)}, f32[8,128]{1,0:T(8,128)S(1)}, f32[2,4,512]{2,1,0:T(4,128)S(1)}, f32[8,512]{1,0:T(8,128)S(1)}) custom-call(f32[4,512,128]{2,1,0:T(8,128)S(1)} %bitcast.13, bf16[4,512,128]{2,1,0:T(8,128)(2,1)S(1)} %bitcast.5, f32[8]{0:T(128)S(1)} %copy-done.3, s32[1]{0:T(128)S(6)} %copy.10.refs_3_, ...), custom_call_target="tpu_custom_call" | custom-call | flops 10000000000 | bytes 1 | tf_op jit(solution)/shard_map/pallas_call | solution.py:232
  8.7 0.7 %collective-permute-start.2 = (bf16[1088,128]{1,0:T(8,128)(2,1)S(1)}, bf16[1088,128]{1,0:T(8,128)(2,1)S(1)}, u32[]{:S(2)}, u32[]{:S(2)}) collective-permute-start(bf16[1088,128]{1,0:T(8,128)(2,1)S(1)} %get-tuple-element.23), channel_id=1, source_target_pairs={{1,2},{3,4},{5,6},{2,1},{4,3},{6,5},{9,10},{11,12},{13,14},{10,9},... | collective-permute-start | bytes 835592 | tf_op jit(solution)/shard_map/ppermute | solution.py:618
  9.4 2.3 %collective-permute-done.message = bf16[1072,128]{1,0:T(8,128)(2,1)S(1)} collective-permute-done((bf16[1072,128]{1,0:T(8,128)(2,1)S(1)}, bf16[1072,128]{1,0:T(8,128)(2,1)S(1)}, u32[]{:S(2)}, u32[]{:S(2)}) %collective-permute-start) | collective-permute-done | bytes 274464 | tf_op jit(solution)/shard_map/ppermute | solution.py:618
  11.7 0.7 %shard_map.97 = (f32[2,528,128]{2,1,0:T(8,128)S(1)}, bf16[1024,128]{1,0:T(8,128)(2,1)S(1)}, bf16[32,128]{1,0:T(8,128)(2,1)S(1)}, bf16[96,128]{1,0:T(8,128)(2,1)S(1)}) custom-call(bf16[1072,128]{1,0:T(8,128)(2,1)S(1)} %collective-permute-done.message, f32[4,512,128]{2,1,0:T(8,128)S(1)} %get-tuple-element.20.pre.refs_1_, bf16[4,512,128]{2,1,0:T(8,128)(2,1)S(1)} %bitcast.6, ...), custom_call_target="tpu_custom_call" | custom-call | flops 10000000000 | bytes 1 | tf_op jit(solution)/shard_map/pallas_call | solution.py:340
  12.4 2.8 %collective-permute-start.3 = (bf16[96,128]{1,0:T(8,128)(2,1)S(1)}, bf16[96,128]{1,0:T(8,128)(2,1)S(1)}, u32[]{:S(2)}, u32[]{:S(2)}) collective-permute-start(bf16[96,128]{1,0:T(8,128)(2,1)S(1)} %get-tuple-element.25.one), channel_id=1, source_target_pairs={{0,4},{1,5},{2,6},{3,7},{4,0},{5,1},{6,2},{7,3},{8,12},{9,13},{10,... | collective-permute-start | bytes 73736 | tf_op jit(solution)/shard_map/ppermute | solution.py:631
  15.2 1.8 %collective-permute-start.6 = (bf16[32,128]{1,0:T(8,128)(2,1)S(1)}, bf16[32,128]{1,0:T(8,128)(2,1)S(1)}, u32[]{:S(2)}, u32[]{:S(2)}) collective-permute-start(bf16[32,128]{1,0:T(8,128)(2,1)S(1)} %get-tuple-element.33), channel_id=1, source_target_pairs={{0,1},{1,0},{2,3},{3,2},{4,5},{5,4},{6,7},{7,6},{8,9},{9,8},{10,11... | collective-permute-start | bytes 24584 | tf_op jit(solution)/shard_map/ppermute | solution.py:618
  17.0 0.2 collective-permute-start.1
  17.2 3.2 %collective-permute-done.3.two = bf16[96,128]{1,0:T(8,128)(2,1)S(1)} collective-permute-done((bf16[96,128]{1,0:T(8,128)(2,1)S(1)}, bf16[96,128]{1,0:T(8,128)(2,1)S(1)}, u32[]{:S(2)}, u32[]{:S(2)}) %collective-permute-start.3) | collective-permute-done | bytes 24608 | tf_op jit(solution)/shard_map/ppermute | solution.py:631
  20.5 1.9 %collective-permute-start.4 = (bf16[192,128]{1,0:T(8,128)(2,1)S(1)}, bf16[192,128]{1,0:T(8,128)(2,1)S(1)}, u32[]{:S(2)}, u32[]{:S(2)}) collective-permute-start(bf16[192,128]{1,0:T(8,128)(2,1)S(1)} %shard_map.98.refs_4_), channel_id=1, source_target_pairs={{0,2},{1,3},{2,0},{3,1},{4,6},{5,7},{6,4},{7,5},{8,10},{9,11},{10,... | collective-permute-start | bytes 147464 | tf_op jit(solution)/shard_map/ppermute | solution.py:632
  22.4 0.0 collective-permute-done.2.refs_0_
  22.4 0.4 %shard_map.99 = (f32[2,528,128]{2,1,0:T(8,128)S(1)}, bf16[1024,128]{1,0:T(8,128)(2,1)S(1)}, f32[8,512]{1,0:T(8,128)S(1)}) custom-call(bf16[1088,128]{1,0:T(8,128)(2,1)S(1)} %collective-permute-done.2.refs_0_, f32[4,512,128]{2,1,0:T(8,128)S(1)} %get-tuple-element.20.pre.refs_1_, bf16[4,512,128]{2,1,0:T(8,128)(2,1)S(1)} %bitcast.7, ...), custom_call_target="tpu_custom_call" | custom-call | flops 600000000 | bytes 1 | tf_op jit(solution)/shard_map/pallas_call | solution.py:384
  22.8 0.7 %collective-permute-start.5 = (bf16[1024,128]{1,0:T(8,128)(2,1)S(1)}, bf16[1024,128]{1,0:T(8,128)(2,1)S(1)}, u32[]{:S(2)}, u32[]{:S(2)}) collective-permute-start(bf16[1024,128]{1,0:T(8,128)(2,1)S(1)} %get-tuple-element.30), channel_id=1, source_target_pairs={{1,2},{3,4},{5,6},{2,1},{4,3},{6,5},{9,10},{11,12},{13,14},{10,9},... | collective-permute-start | bytes 786440 | tf_op jit(solution)/shard_map/ppermute | solution.py:618
  23.5 1.4 %collective-permute-done.4.refs_5_ = bf16[192,128]{1,0:T(8,128)(2,1)S(1)} collective-permute-done((bf16[192,128]{1,0:T(8,128)(2,1)S(1)}, bf16[192,128]{1,0:T(8,128)(2,1)S(1)}, u32[]{:S(2)}, u32[]{:S(2)}) %collective-permute-start.4) | collective-permute-done | bytes 49184 | tf_op jit(solution)/shard_map/ppermute | solution.py:632
  24.9 1.8 %shard_map.100 = (f32[4,512,128]{2,1,0:T(8,128)S(1)}, f32[4,8,512]{2,1,0:T(8,128)S(1)}, f32[4,8,512]{2,1,0:T(8,128)S(1)}, bf16[384,128]{1,0:T(8,128)(2,1)S(1)}) custom-call(f32[2,528,128]{2,1,0:T(8,128)S(1)} %get-tuple-element.22.refs_0_, f32[2,528,128]{2,1,0:T(8,128)S(1)} %get-tuple-element.26.refs_1_, bf16[4,512,128]{2,1,0:T(8,128)(2,1)S(1)} %bitcast.8, ...), custom_call_target="tpu_custom_call" | custom-call | flops 1300000000 | bytes 1 | tf_op jit(solution)/shard_map/pallas_call | solution.py:439
  26.6 0.0 collective-permute-done.6.early_a
  26.6 0.1 shard_map.103.refs_0_
  26.7 0.1 collective-permute-start.7
  26.8 1.6 %collective-permute-start.8 = (f32[2,4,512]{2,1,0:T(4,128)S(1)}, f32[2,4,512]{2,1,0:T(4,128)S(1)}, u32[]{:S(2)}, u32[]{:S(2)}) collective-permute-start(f32[2,4,512]{2,1,0:T(4,128)S(1)} %shard_map.103.refs_0_), channel_id=1, source_target_pairs={{0,16},{8,24},{16,0},{24,8},{1,17},{9,25},{17,1},{25,9},{2,18},{10... | collective-permute-start | bytes 49160 | tf_op jit(solution)/shard_map/ppermute | solution.py:640
  28.4 0.3 collective-permute-start.9
  28.6 0.5 %shard_map.101.state = f32[4,512,128]{2,1,0:T(8,128)S(1)} custom-call(bf16[4,512,128]{2,1,0:T(8,128)(2,1)S(1)} %bitcast.9, f32[4,512,128]{2,1,0:T(8,128)S(1)} %get-tuple-element.28.refs_1_, bf16[384,128]{1,0:T(8,128)(2,1)S(1)} %get-tuple-element.29.refs_2_), custom_call_target="tpu_custom_call" | custom-call | flops 1 | bytes 1 | tf_op jit(solution)/shard_map/pallas_call | solution.py:480
  29.2 0.0 collective-permute-done.1.message
  29.2 0.2 shard_map.102.at_a
  29.4 0.7 %collective-permute-done.7.refs_1_ = f32[2,4,512]{2,1,0:T(4,128)S(1)} collective-permute-done((f32[2,4,512]{2,1,0:T(4,128)S(1)}, f32[2,4,512]{2,1,0:T(4,128)S(1)}, u32[]{:S(2)}, u32[]{:S(2)}) %collective-permute-start.7) | collective-permute-done | bytes 16416 | tf_op jit(solution)/shard_map/ppermute | solution.py:640
  30.1 0.5 %collective-permute-done.8.refs_2_ = f32[2,4,512]{2,1,0:T(4,128)S(1)} collective-permute-done((f32[2,4,512]{2,1,0:T(4,128)S(1)}, f32[2,4,512]{2,1,0:T(4,128)S(1)}, u32[]{:S(2)}, u32[]{:S(2)}) %collective-permute-start.8) | collective-permute-done | bytes 16416 | tf_op jit(solution)/shard_map/ppermute | solution.py:640
  30.6 0.0 collective-permute-done.9.refs_3_
  30.6 0.0 collective-permute-done.5.message_b
  30.6 1.0 %shard_map.104 = (f32[4,512,128]{2,1,0:T(8,128)}, f32[2,4,512]{2,1,0:T(4,128)}) custom-call(f32[2,512,128]{2,1,0:T(8,128)S(1)} %shard_map.102.at_a, bf16[1024,128]{1,0:T(8,128)(2,1)S(1)} %collective-permute-done.5.message_b, f32[4,512,128]{2,1,0:T(8,128)S(1)} %shard_map.101.state, bf16[4,512,128]{2,1,0:T(8,128)(2,1)S(1)} %bitcast.11, ...), custom_call_target="tpu_custom_call" | custom-call | flops 1 | bytes 1 | tf_op jit(solution)/shard_map/pallas_call | solution.py:593
  (6 shorter events, 0.0 us)
Async XLA Ops:
  0.6 5.1 %copy-start = (bf16[1,4,512,128]{3,2,1,0:T(8,128)(2,1)S(1)}, bf16[1,4,512,128]{3,2,1,0:T(8,128)(2,1)}, u32[]{:S(2)}) copy-start(bf16[1,4,512,128]{3,2,1,0:T(8,128)(2,1)} %param.9) | copy-start | bytes 1572868
  0.6 5.1 %copy-start.1 = (f32[1,4,512,128]{3,2,1,0:T(8,128)S(1)}, f32[1,4,512,128]{3,2,1,0:T(8,128)}, u32[]{:S(2)}) copy-start(f32[1,4,512,128]{3,2,1,0:T(8,128)} %param.8) | copy-start | bytes 3145732
  0.7 5.1 %copy-start.2 = (s32[2,4,512]{2,1,0:T(4,128)S(1)}, s32[2,4,512]{2,1,0:T(4,128)}, u32[]{:S(2)}) copy-start(s32[2,4,512]{2,1,0:T(4,128)} %refs_4_.1) | copy-start | bytes 49156
  2.1 9.6 %collective-permute-start = (bf16[1072,128]{1,0:T(8,128)(2,1)S(1)}, bf16[1072,128]{1,0:T(8,128)(2,1)S(1)}, u32[]{:S(2)}, u32[]{:S(2)}) collective-permute-start(bf16[1072,128]{1,0:T(8,128)(2,1)S(1)} %shard_map.95.refs_5_.first), channel_id=1, source_target_pairs={{0,1},{1,0},{2,3},{3,2},{4,5},{5,4},{6,7},{7,6},{8,9},{9,8},{10,11... | collective-permute-start | bytes 823304 | tf_op jit(solution)/shard_map/ppermute | solution.py:618
  5.8 0.7 %copy-start.3 = (f32[8]{0:T(128)S(1)}, f32[8]{0:T(128)}, u32[]{:S(2)}) copy-start(f32[8]{0:T(128)} %refs_2_.1) | copy-start | bytes 100
  8.7 13.6 %collective-permute-start.2 = (bf16[1088,128]{1,0:T(8,128)(2,1)S(1)}, bf16[1088,128]{1,0:T(8,128)(2,1)S(1)}, u32[]{:S(2)}, u32[]{:S(2)}) collective-permute-start(bf16[1088,128]{1,0:T(8,128)(2,1)S(1)} %get-tuple-element.23), channel_id=1, source_target_pairs={{1,2},{3,4},{5,6},{2,1},{4,3},{6,5},{9,10},{11,12},{13,14},{10,9},... | collective-permute-start | bytes 835592 | tf_op jit(solution)/shard_map/ppermute | solution.py:618
  12.4 8.1 %collective-permute-start.3 = (bf16[96,128]{1,0:T(8,128)(2,1)S(1)}, bf16[96,128]{1,0:T(8,128)(2,1)S(1)}, u32[]{:S(2)}, u32[]{:S(2)}) collective-permute-start(bf16[96,128]{1,0:T(8,128)(2,1)S(1)} %get-tuple-element.25.one), channel_id=1, source_target_pairs={{0,4},{1,5},{2,6},{3,7},{4,0},{5,1},{6,2},{7,3},{8,12},{9,13},{10,... | collective-permute-start | bytes 73736 | tf_op jit(solution)/shard_map/ppermute | solution.py:631
  15.2 11.4 %collective-permute-start.6 = (bf16[32,128]{1,0:T(8,128)(2,1)S(1)}, bf16[32,128]{1,0:T(8,128)(2,1)S(1)}, u32[]{:S(2)}, u32[]{:S(2)}) collective-permute-start(bf16[32,128]{1,0:T(8,128)(2,1)S(1)} %get-tuple-element.33), channel_id=1, source_target_pairs={{0,1},{1,0},{2,3},{3,2},{4,5},{5,4},{6,7},{7,6},{8,9},{9,8},{10,11... | collective-permute-start | bytes 24584 | tf_op jit(solution)/shard_map/ppermute | solution.py:618
  17.0 12.2 %collective-permute-start.1 = (bf16[1024,128]{1,0:T(8,128)(2,1)S(1)}, bf16[1024,128]{1,0:T(8,128)(2,1)S(1)}, u32[]{:S(2)}, u32[]{:S(2)}) collective-permute-start(bf16[1024,128]{1,0:T(8,128)(2,1)S(1)} %get-tuple-element.21), channel_id=1, source_target_pairs={{0,1},{1,0},{2,3},{3,2},{4,5},{5,4},{6,7},{7,6},{8,9},{9,8},{10,11... | collective-permute-start | bytes 786440 | tf_op jit(solution)/shard_map/ppermute | solution.py:618
  20.5 4.4 %collective-permute-start.4 = (bf16[192,128]{1,0:T(8,128)(2,1)S(1)}, bf16[192,128]{1,0:T(8,128)(2,1)S(1)}, u32[]{:S(2)}, u32[]{:S(2)}) collective-permute-start(bf16[192,128]{1,0:T(8,128)(2,1)S(1)} %shard_map.98.refs_4_), channel_id=1, source_target_pairs={{0,2},{1,3},{2,0},{3,1},{4,6},{5,7},{6,4},{7,5},{8,10},{9,11},{10,... | collective-permute-start | bytes 147464 | tf_op jit(solution)/shard_map/ppermute | solution.py:632
  22.8 7.8 %collective-permute-start.5 = (bf16[1024,128]{1,0:T(8,128)(2,1)S(1)}, bf16[1024,128]{1,0:T(8,128)(2,1)S(1)}, u32[]{:S(2)}, u32[]{:S(2)}) collective-permute-start(bf16[1024,128]{1,0:T(8,128)(2,1)S(1)} %get-tuple-element.30), channel_id=1, source_target_pairs={{1,2},{3,4},{5,6},{2,1},{4,3},{6,5},{9,10},{11,12},{13,14},{10,9},... | collective-permute-start | bytes 786440 | tf_op jit(solution)/shard_map/ppermute | solution.py:618
  26.7 3.4 %collective-permute-start.7 = (f32[2,4,512]{2,1,0:T(4,128)S(1)}, f32[2,4,512]{2,1,0:T(4,128)S(1)}, u32[]{:S(2)}, u32[]{:S(2)}) collective-permute-start(f32[2,4,512]{2,1,0:T(4,128)S(1)} %shard_map.103.refs_0_), channel_id=1, source_target_pairs={{0,24},{8,16},{16,8},{24,0},{1,25},{9,17},{17,9},{25,1},{2,26},{10... | collective-permute-start | bytes 49160 | tf_op jit(solution)/shard_map/ppermute | solution.py:640
  26.8 3.8 %collective-permute-start.8 = (f32[2,4,512]{2,1,0:T(4,128)S(1)}, f32[2,4,512]{2,1,0:T(4,128)S(1)}, u32[]{:S(2)}, u32[]{:S(2)}) collective-permute-start(f32[2,4,512]{2,1,0:T(4,128)S(1)} %shard_map.103.refs_0_), channel_id=1, source_target_pairs={{0,16},{8,24},{16,0},{24,8},{1,17},{9,25},{17,1},{25,9},{2,18},{10... | collective-permute-start | bytes 49160 | tf_op jit(solution)/shard_map/ppermute | solution.py:640
  28.4 2.3 %collective-permute-start.9 = (f32[2,4,512]{2,1,0:T(4,128)S(1)}, f32[2,4,512]{2,1,0:T(4,128)S(1)}, u32[]{:S(2)}, u32[]{:S(2)}) collective-permute-start(f32[2,4,512]{2,1,0:T(4,128)S(1)} %shard_map.103.refs_0_), channel_id=1, source_target_pairs={{0,8},{8,0},{16,24},{24,16},{1,9},{9,1},{17,25},{25,17},{2,10},{10... | collective-permute-start | bytes 49160 | tf_op jit(solution)/shard_map/ppermute | solution.py:640

commit v6 on v5

--- a/solution.py
+++ b/solution.py
@@ -152,11 +152,11 @@
     return [(ref, (d,)) for d in range(ref.shape[0])]
 
 
-def first_message(adjoint, targets, owners, cells, out, near, far, missing, digits, owner, cell, sems):
+def first_message(adjoint, targets, owners, cells, rates, out, held, near, far, missing, digits, owner, cell, sems):
     layers, rows, depth = adjoint.shape
     n = targets.shape[0]
     pairs = [(adjoint.at[stored(d, layers)], ref.at[pl.ds(PAD, rows)]) for d, ref in ((0, near), (1, far))]
-    pairs += [(targets, out.at[pl.ds(2 * rows, n)]), (owners, owner), (cells, cell)]
+    pairs += [(targets, out.at[pl.ds(2 * rows, n)]), (owners, owner), (cells, cell), (rates, held)]
     copies = copy_all(pairs, sems)
     digits[...] = jnp.zeros(digits.shape, f32)
     for c in copies[3:]:
@@ -170,18 +170,18 @@
     write_message((near, ()), (far, ()), (missing, ()), out, rows)
 
 
-def make_first_message(adjoint, targets, owners, cells):
+def make_first_message(adjoint, targets, owners, cells, rates):
     layers, rows, depth = adjoint.shape
     extra = targets.shape[0] + 16
     row = pltpu.VMEM(owners.shape, jnp.int32)
     return call(
         first_message,
-        jax.ShapeDtypeStruct((2 * rows + extra, depth), bf16),
-        VMEM,
-        [ANY] * 4,
-        [padded(rows, depth)] * 3 + [pltpu.VMEM((16, depth), f32), row, row, pltpu.SemaphoreType.DMA((5,))],
+        (jax.ShapeDtypeStruct((2 * rows + extra, depth), bf16), jax.ShapeDtypeStruct(rates.shape, f32)),
+        (VMEM, VMEM),
+        [ANY] * 5,
+        [padded(rows, depth)] * 3 + [pltpu.VMEM((16, depth), f32), row, row, pltpu.SemaphoreType.DMA((6,))],
         cost(LONG),
-    )(*[pltpu.with_memory_space_constraint(v, pltpu.HBM) for v in (adjoint, targets, owners, cells)])
+    )(*[pltpu.with_memory_space_constraint(v, pltpu.HBM) for v in (adjoint, targets, owners, cells, rates)])
 
 
 def transport_row(inflow, depth):
@@ -197,7 +197,7 @@
     copies = copy_all(
         [(adjoint.at[stored(d, layers)], state.at[d, pl.ds(PAD, rows)]) for d in range(layers)], sems
     )
-    row[...] = transport_row(rates[choice[0]], depth)
+    row[...] = transport_row(rates[0, choice[0]], depth)
     masked[...] = wall_weight * mask[...].astype(f32)
     for d in range(layers):
         clear_margins((state, (d,)))
@@ -619,17 +619,17 @@
 
     rows, n = state.shape[1], targets.shape[0]
     few = count == 8
-    first = make_first_message(state, targets, owners, target_cell)
+    first, rates = make_first_message(state, targets, owners, target_cell, inflow_rates[None])
     from_a = send(first, 0)
-    pre, message, row, mask, near_walls = make_first_local(state, phase, inflow_rates, rate_index, wall_mask, first, count)
+    pre, message, row, mask, near_walls = make_first_local(state, phase, rates, rate_index, wall_mask, first, count)
     from_b = send(message, 1)
     half_a, message, early, pair = make_middle_a(from_a, pre, phase, first)
     early = send(early, 0)
     later_a = send(message, 0)
     four = far = pair
     if few:
-        four = make_join(pair, lax.ppermute(pair, "slab", [(i, i ^ 4) for i in range(count)]))
-        far = lax.ppermute(four, "slab", [(i, i ^ 2) for i in range(count)])
+        four = make_join(pair, lax.ppermute(pair, "slab", [(i, i ^ 2) for i in range(count)]))
+        far = lax.ppermute(four, "slab", [(i, i ^ 4) for i in range(count)])
     half_b, message, walls_b = make_middle_b(from_b, pre, phase, near_walls, four, count)
     later_b = send(message, 1)
     pre, wall, phase_wall, block = make_second_local(half_a, half_b, phase, row, four, far, count)

time: 31.8 us -> 31 us (0.975)
  the two profiles are of different devices: /device:TPU:0 before, /device:TPU:25 now
where the time goes in v6:
time: 31 us; the launch traced here: 30.4 us
  starting transfers between devices  11.8 us (38%)
  waiting for transfers between devices  8.75 us (28%)
  Pallas kernels  8.43 us (27%)
  between operations  1.43 us (5%)
    ppermute x5, waiting for transfers between devices, send(): return lax.ppermute(v, 'slab', pairs[side])  6.77 us
    ppermute x5, starting transfers between devices, send(): return lax.ppermute(v, 'slab', pairs[side])  6.77 us
    ppermute x3, starting transfers between devices, on_device(): lax.ppermute(part, 'cond', [(i, i ^ k) for i in range(4)])  4.57 us
    pallas_call x1, Pallas kernels, make_first_local(): call(lambda *refs: first_local(count, *refs), (jax.ShapeDtypeStruct(adjoi...  2.29 us
    ppermute x1, waiting for transfers between devices, on_device(): lax.ppermute(pair, 'slab', [(i, i ^ 2) for i in range(count)])  1.97 us
    pallas_call x1, Pallas kernels, make_second_local(): call(lambda *refs: second_local(count, *refs), (jax.ShapeDtypeStruct((lay...  1.78 us
    pallas_call x1, Pallas kernels, make_first_message(): call(first_message, (jax.ShapeDtypeStruct((2 * rows + extra, depth), bf16...  1.42 us
    pallas_call x1, Pallas kernels, make_final(): call(final, (jax.ShapeDtypeStruct(state.shape, f32), jax.ShapeDtypeStruct...  1.04 us
  transfers between devices with their start and end apart: 10, of which 4 were waited for; matrix products, arithmetic and copies ran while one was open for 0% of the time, Pallas kernels for 20%

profile of v6, /device:TPU:25, one launch (start us, length us, event | category | flops | bytes accessed | tf_op | source)
XLA Modules:
  0.0 30.4 jit_solution(77607088573584543)
XLA Ops:
  0.7 1.4 %shard_map.95 = (bf16[1072,128]{1,0:T(8,128)(2,1)S(1)}, f32[1,8]{1,0:T(1,128)S(1)}) custom-call(f32[4,512,128]{2,1,0:T(8,128)} %bitcast.13, bf16[32,128]{1,0:T(8,128)(2,1)} %bitcast.16, s32[1,32]{1,0:T(1,128)} %bitcast.17, s32[1,32]{1,0:T(1,128)} %cells.1, f32[1,8]{1,0:T(1,128)} %bitcast.18), custom_call_target="tpu_custom_call" | custom-call | flops 10000000000 | bytes 1 | tf_op jit(solution)/shard_map/pallas_call | solution.py:177
  2.1 1.3 %collective-permute-start = (bf16[1072,128]{1,0:T(8,128)(2,1)S(1)}, bf16[1072,128]{1,0:T(8,128)(2,1)S(1)}, u32[]{:S(2)}, u32[]{:S(2)}) collective-permute-start(bf16[1072,128]{1,0:T(8,128)(2,1)S(1)} %get-tuple-element.22.refs_5_.first), channel_id=1, source_target_pairs={{0,1},{1,0},{2,3},{3,2},{4,5},{5,4},{6,7},{7,6},{8,9},{9,8},{10,11... | collective-permute-start | bytes 823304 | tf_op jit(solution)/shard_map/ppermute | solution.py:618
  4.0 0.0 copy-done
  4.1 0.0 copy-done.1
  4.1 0.0 copy-done.2
  4.1 2.3 %shard_map.96 = (f32[4,512,128]{2,1,0:T(8,128)S(1)}, bf16[1088,128]{1,0:T(8,128)(2,1)S(1)}, f32[8,128]{1,0:T(8,128)S(1)}, f32[2,4,512]{2,1,0:T(4,128)S(1)}, f32[8,512]{1,0:T(8,128)S(1)}) custom-call(f32[4,512,128]{2,1,0:T(8,128)S(1)} %bitcast.14, bf16[4,512,128]{2,1,0:T(8,128)(2,1)S(1)} %bitcast.6, f32[1,8]{1,0:T(1,128)S(1)} %get-tuple-element.23.refs_2_, ...), custom_call_target="tpu_custom_call" | custom-call | flops 10000000000 | bytes 1 | tf_op jit(solution)/shard_map/pallas_call | solution.py:232
  6.4 2.0 %collective-permute-start.2 = (bf16[1088,128]{1,0:T(8,128)(2,1)S(1)}, bf16[1088,128]{1,0:T(8,128)(2,1)S(1)}, u32[]{:S(2)}, u32[]{:S(2)}) collective-permute-start(bf16[1088,128]{1,0:T(8,128)(2,1)S(1)} %get-tuple-element.27), channel_id=1, source_target_pairs={{1,2},{3,4},{5,6},{2,1},{4,3},{6,5},{9,10},{11,12},{13,14},{10,9},... | collective-permute-start | bytes 835592 | tf_op jit(solution)/shard_map/ppermute | solution.py:618
  8.4 1.2 %collective-permute-done.message = bf16[1072,128]{1,0:T(8,128)(2,1)S(1)} collective-permute-done((bf16[1072,128]{1,0:T(8,128)(2,1)S(1)}, bf16[1072,128]{1,0:T(8,128)(2,1)S(1)}, u32[]{:S(2)}, u32[]{:S(2)}) %collective-permute-start) | collective-permute-done | bytes 274464 | tf_op jit(solution)/shard_map/ppermute | solution.py:618
  9.6 0.7 %shard_map.97 = (f32[2,528,128]{2,1,0:T(8,128)S(1)}, bf16[1024,128]{1,0:T(8,128)(2,1)S(1)}, bf16[32,128]{1,0:T(8,128)(2,1)S(1)}, bf16[96,128]{1,0:T(8,128)(2,1)S(1)}) custom-call(bf16[1072,128]{1,0:T(8,128)(2,1)S(1)} %collective-permute-done.message, f32[4,512,128]{2,1,0:T(8,128)S(1)} %get-tuple-element.24.pre.refs_1_, bf16[4,512,128]{2,1,0:T(8,128)(2,1)S(1)} %bitcast.7, ...), custom_call_target="tpu_custom_call" | custom-call | flops 10000000000 | bytes 1 | tf_op jit(solution)/shard_map/pallas_call | solution.py:340
  10.3 0.2 collective-permute-start.3
  10.5 1.2 %collective-permute-start.6 = (bf16[32,128]{1,0:T(8,128)(2,1)S(1)}, bf16[32,128]{1,0:T(8,128)(2,1)S(1)}, u32[]{:S(2)}, u32[]{:S(2)}) collective-permute-start(bf16[32,128]{1,0:T(8,128)(2,1)S(1)} %get-tuple-element.37), channel_id=1, source_target_pairs={{0,1},{1,0},{2,3},{3,2},{4,5},{5,4},{6,7},{7,6},{8,9},{9,8},{10,11... | collective-permute-start | bytes 24584 | tf_op jit(solution)/shard_map/ppermute | solution.py:618
  11.7 0.2 collective-permute-start.1
  11.9 2.0 %collective-permute-done.3.two = bf16[96,128]{1,0:T(8,128)(2,1)S(1)} collective-permute-done((bf16[96,128]{1,0:T(8,128)(2,1)S(1)}, bf16[96,128]{1,0:T(8,128)(2,1)S(1)}, u32[]{:S(2)}, u32[]{:S(2)}) %collective-permute-start.3) | collective-permute-done | bytes 24608 | tf_op jit(solution)/shard_map/ppermute | solution.py:631
  13.9 0.3 collective-permute-start.4
  14.2 2.2 %collective-permute-done.2.refs_0_ = bf16[1088,128]{1,0:T(8,128)(2,1)S(1)} collective-permute-done((bf16[1088,128]{1,0:T(8,128)(2,1)S(1)}, bf16[1088,128]{1,0:T(8,128)(2,1)S(1)}, u32[]{:S(2)}, u32[]{:S(2)}) %collective-permute-start.2) | collective-permute-done | bytes 278560 | tf_op jit(solution)/shard_map/ppermute | solution.py:618
  16.4 0.4 %shard_map.99 = (f32[2,528,128]{2,1,0:T(8,128)S(1)}, bf16[1024,128]{1,0:T(8,128)(2,1)S(1)}, f32[8,512]{1,0:T(8,128)S(1)}) custom-call(bf16[1088,128]{1,0:T(8,128)(2,1)S(1)} %collective-permute-done.2.refs_0_, f32[4,512,128]{2,1,0:T(8,128)S(1)} %get-tuple-element.24.pre.refs_1_, bf16[4,512,128]{2,1,0:T(8,128)(2,1)S(1)} %bitcast.8, ...), custom_call_target="tpu_custom_call" | custom-call | flops 600000000 | bytes 1 | tf_op jit(solution)/shard_map/pallas_call | solution.py:384
  16.8 2.0 %collective-permute-start.5 = (bf16[1024,128]{1,0:T(8,128)(2,1)S(1)}, bf16[1024,128]{1,0:T(8,128)(2,1)S(1)}, u32[]{:S(2)}, u32[]{:S(2)}) collective-permute-start(bf16[1024,128]{1,0:T(8,128)(2,1)S(1)} %get-tuple-element.34), channel_id=1, source_target_pairs={{1,2},{3,4},{5,6},{2,1},{4,3},{6,5},{9,10},{11,12},{13,14},{10,9},... | collective-permute-start | bytes 786440 | tf_op jit(solution)/shard_map/ppermute | solution.py:618
  18.8 0.0 collective-permute-done.4.refs_5_
  18.8 1.8 %shard_map.100 = (f32[4,512,128]{2,1,0:T(8,128)S(1)}, f32[4,8,512]{2,1,0:T(8,128)S(1)}, f32[4,8,512]{2,1,0:T(8,128)S(1)}, bf16[384,128]{1,0:T(8,128)(2,1)S(1)}) custom-call(f32[2,528,128]{2,1,0:T(8,128)S(1)} %get-tuple-element.26.refs_0_, f32[2,528,128]{2,1,0:T(8,128)S(1)} %get-tuple-element.30.refs_1_, bf16[4,512,128]{2,1,0:T(8,128)(2,1)S(1)} %bitcast.9, ...), custom_call_target="tpu_custom_call" | custom-call | flops 1300000000 | bytes 1 | tf_op jit(solution)/shard_map/pallas_call | solution.py:439
  20.6 0.0 collective-permute-done.6.early_a
  20.6 0.1 shard_map.103.refs_0_
  20.7 4.1 %collective-permute-start.7 = (f32[2,4,512]{2,1,0:T(4,128)S(1)}, f32[2,4,512]{2,1,0:T(4,128)S(1)}, u32[]{:S(2)}, u32[]{:S(2)}) collective-permute-start(f32[2,4,512]{2,1,0:T(4,128)S(1)} %shard_map.103.refs_0_), channel_id=1, source_target_pairs={{0,24},{8,16},{16,8},{24,0},{1,25},{9,17},{17,9},{25,1},{2,26},{10... | collective-permute-start | bytes 49160 | tf_op jit(solution)/shard_map/ppermute | solution.py:640
  24.8 0.1 collective-permute-start.8
  24.9 0.4 %collective-permute-start.9 = (f32[2,4,512]{2,1,0:T(4,128)S(1)}, f32[2,4,512]{2,1,0:T(4,128)S(1)}, u32[]{:S(2)}, u32[]{:S(2)}) collective-permute-start(f32[2,4,512]{2,1,0:T(4,128)S(1)} %shard_map.103.refs_0_), channel_id=1, source_target_pairs={{0,8},{8,0},{16,24},{24,16},{1,9},{9,1},{17,25},{25,17},{2,10},{10... | collective-permute-start | bytes 49160 | tf_op jit(solution)/shard_map/ppermute | solution.py:640
  25.2 0.5 %shard_map.101.state = f32[4,512,128]{2,1,0:T(8,128)S(1)} custom-call(bf16[4,512,128]{2,1,0:T(8,128)(2,1)S(1)} %bitcast.10, f32[4,512,128]{2,1,0:T(8,128)S(1)} %get-tuple-element.32.refs_1_, bf16[384,128]{1,0:T(8,128)(2,1)S(1)} %get-tuple-element.33.refs_2_), custom_call_target="tpu_custom_call" | custom-call | flops 1 | bytes 1 | tf_op jit(solution)/shard_map/pallas_call | solution.py:480
  25.8 3.3 %collective-permute-done.1.message = bf16[1024,128]{1,0:T(8,128)(2,1)S(1)} collective-permute-done((bf16[1024,128]{1,0:T(8,128)(2,1)S(1)}, bf16[1024,128]{1,0:T(8,128)(2,1)S(1)}, u32[]{:S(2)}, u32[]{:S(2)}) %collective-permute-start.1) | collective-permute-done | bytes 262176 | tf_op jit(solution)/shard_map/ppermute | solution.py:618
  29.1 0.2 shard_map.102.at_a
  29.3 0.0 collective-permute-done.7.refs_1_
  29.3 0.0 collective-permute-done.8.refs_2_
  29.4 0.0 collective-permute-done.9.refs_3_
  29.4 0.0 collective-permute-done.5.message_b
  29.4 1.0 %shard_map.104 = (f32[4,512,128]{2,1,0:T(8,128)}, f32[2,4,512]{2,1,0:T(4,128)}) custom-call(f32[2,512,128]{2,1,0:T(8,128)S(1)} %shard_map.102.at_a, bf16[1024,128]{1,0:T(8,128)(2,1)S(1)} %collective-permute-done.5.message_b, f32[4,512,128]{2,1,0:T(8,128)S(1)} %shard_map.101.state, bf16[4,512,128]{2,1,0:T(8,128)(2,1)S(1)} %bitcast.12, ...), custom_call_target="tpu_custom_call" | custom-call | flops 1 | bytes 1 | tf_op jit(solution)/shard_map/pallas_call | solution.py:593
  (4 shorter events, 0.0 us)
Async XLA Ops:
  0.6 3.4 %copy-start = (bf16[1,4,512,128]{3,2,1,0:T(8,128)(2,1)S(1)}, bf16[1,4,512,128]{3,2,1,0:T(8,128)(2,1)}, u32[]{:S(2)}) copy-start(bf16[1,4,512,128]{3,2,1,0:T(8,128)(2,1)} %param.9) | copy-start | bytes 1572868
  0.6 3.4 %copy-start.1 = (f32[1,4,512,128]{3,2,1,0:T(8,128)S(1)}, f32[1,4,512,128]{3,2,1,0:T(8,128)}, u32[]{:S(2)}) copy-start(f32[1,4,512,128]{3,2,1,0:T(8,128)} %param.8) | copy-start | bytes 3145732
  0.7 3.4 %copy-start.2 = (s32[2,4,512]{2,1,0:T(4,128)S(1)}, s32[2,4,512]{2,1,0:T(4,128)}, u32[]{:S(2)}) copy-start(s32[2,4,512]{2,1,0:T(4,128)} %refs_4_.1) | copy-start | bytes 49156
  2.1 7.5 %collective-permute-start = (bf16[1072,128]{1,0:T(8,128)(2,1)S(1)}, bf16[1072,128]{1,0:T(8,128)(2,1)S(1)}, u32[]{:S(2)}, u32[]{:S(2)}) collective-permute-start(bf16[1072,128]{1,0:T(8,128)(2,1)S(1)} %get-tuple-element.22.refs_5_.first), channel_id=1, source_target_pairs={{0,1},{1,0},{2,3},{3,2},{4,5},{5,4},{6,7},{7,6},{8,9},{9,8},{10,11... | collective-permute-start | bytes 823304 | tf_op jit(solution)/shard_map/ppermute | solution.py:618
  6.4 10.0 %collective-permute-start.2 = (bf16[1088,128]{1,0:T(8,128)(2,1)S(1)}, bf16[1088,128]{1,0:T(8,128)(2,1)S(1)}, u32[]{:S(2)}, u32[]{:S(2)}) collective-permute-start(bf16[1088,128]{1,0:T(8,128)(2,1)S(1)} %get-tuple-element.27), channel_id=1, source_target_pairs={{1,2},{3,4},{5,6},{2,1},{4,3},{6,5},{9,10},{11,12},{13,14},{10,9},... | collective-permute-start | bytes 835592 | tf_op jit(solution)/shard_map/ppermute | solution.py:618
  10.3 3.6 %collective-permute-start.3 = (bf16[96,128]{1,0:T(8,128)(2,1)S(1)}, bf16[96,128]{1,0:T(8,128)(2,1)S(1)}, u32[]{:S(2)}, u32[]{:S(2)}) collective-permute-start(bf16[96,128]{1,0:T(8,128)(2,1)S(1)} %get-tuple-element.29.one), channel_id=1, source_target_pairs={{0,2},{1,3},{2,0},{3,1},{4,6},{5,7},{6,4},{7,5},{8,10},{9,11},{10,... | collective-permute-start | bytes 73736 | tf_op jit(solution)/shard_map/ppermute | solution.py:631
  10.5 10.1 %collective-permute-start.6 = (bf16[32,128]{1,0:T(8,128)(2,1)S(1)}, bf16[32,128]{1,0:T(8,128)(2,1)S(1)}, u32[]{:S(2)}, u32[]{:S(2)}) collective-permute-start(bf16[32,128]{1,0:T(8,128)(2,1)S(1)} %get-tuple-element.37), channel_id=1, source_target_pairs={{0,1},{1,0},{2,3},{3,2},{4,5},{5,4},{6,7},{7,6},{8,9},{9,8},{10,11... | collective-permute-start | bytes 24584 | tf_op jit(solution)/shard_map/ppermute | solution.py:618
  11.7 17.4 %collective-permute-start.1 = (bf16[1024,128]{1,0:T(8,128)(2,1)S(1)}, bf16[1024,128]{1,0:T(8,128)(2,1)S(1)}, u32[]{:S(2)}, u32[]{:S(2)}) collective-permute-start(bf16[1024,128]{1,0:T(8,128)(2,1)S(1)} %get-tuple-element.25), channel_id=1, source_target_pairs={{0,1},{1,0},{2,3},{3,2},{4,5},{5,4},{6,7},{7,6},{8,9},{9,8},{10,11... | collective-permute-start | bytes 786440 | tf_op jit(solution)/shard_map/ppermute | solution.py:618
  13.9 4.9 %collective-permute-start.4 = (bf16[192,128]{1,0:T(8,128)(2,1)S(1)}, bf16[192,128]{1,0:T(8,128)(2,1)S(1)}, u32[]{:S(2)}, u32[]{:S(2)}) collective-permute-start(bf16[192,128]{1,0:T(8,128)(2,1)S(1)} %shard_map.98.refs_4_), channel_id=1, source_target_pairs={{0,4},{1,5},{2,6},{3,7},{4,0},{5,1},{6,2},{7,3},{8,12},{9,13},{10,... | collective-permute-start | bytes 147464 | tf_op jit(solution)/shard_map/ppermute | solution.py:632
  16.8 12.5 %collective-permute-start.5 = (bf16[1024,128]{1,0:T(8,128)(2,1)S(1)}, bf16[1024,128]{1,0:T(8,128)(2,1)S(1)}, u32[]{:S(2)}, u32[]{:S(2)}) collective-permute-start(bf16[1024,128]{1,0:T(8,128)(2,1)S(1)} %get-tuple-element.34), channel_id=1, source_target_pairs={{1,2},{3,4},{5,6},{2,1},{4,3},{6,5},{9,10},{11,12},{13,14},{10,9},... | collective-permute-start | bytes 786440 | tf_op jit(solution)/shard_map/ppermute | solution.py:618
  20.7 8.7 %collective-permute-start.7 = (f32[2,4,512]{2,1,0:T(4,128)S(1)}, f32[2,4,512]{2,1,0:T(4,128)S(1)}, u32[]{:S(2)}, u32[]{:S(2)}) collective-permute-start(f32[2,4,512]{2,1,0:T(4,128)S(1)} %shard_map.103.refs_0_), channel_id=1, source_target_pairs={{0,24},{8,16},{16,8},{24,0},{1,25},{9,17},{17,9},{25,1},{2,26},{10... | collective-permute-start | bytes 49160 | tf_op jit(solution)/shard_map/ppermute | solution.py:640
  24.8 4.6 %collective-permute-start.8 = (f32[2,4,512]{2,1,0:T(4,128)S(1)}, f32[2,4,512]{2,1,0:T(4,128)S(1)}, u32[]{:S(2)}, u32[]{:S(2)}) collective-permute-start(f32[2,4,512]{2,1,0:T(4,128)S(1)} %shard_map.103.refs_0_), channel_id=1, source_target_pairs={{0,16},{8,24},{16,0},{24,8},{1,17},{9,25},{17,1},{25,9},{2,18},{10... | collective-permute-start | bytes 49160 | tf_op jit(solution)/shard_map/ppermute | solution.py:640
  24.9 4.5 %collective-permute-start.9 = (f32[2,4,512]{2,1,0:T(4,128)S(1)}, f32[2,4,512]{2,1,0:T(4,128)S(1)}, u32[]{:S(2)}, u32[]{:S(2)}) collective-permute-start(f32[2,4,512]{2,1,0:T(4,128)S(1)} %shard_map.103.refs_0_), channel_id=1, source_target_pairs={{0,8},{8,0},{16,24},{24,16},{1,9},{9,1},{17,25},{25,17},{2,10},{10... | collective-permute-start | bytes 49160 | tf_op jit(solution)/shard_map/ppermute | solution.py:640

commit v7 on v6

--- a/solution.py
+++ b/solution.py
@@ -395,28 +395,25 @@
     )(message, pre, phase, near_walls, after)
 
 
-def join(one, two, out):
+def join(one, two, after, out):
     n = one.shape[0]
     out[pl.ds(0, n), :] = one[...]
     out[pl.ds(n, n), :] = two[...]
 
 
-def make_join(one, two):
+def make_join(one, two, after, flops):
     return call(
         join,
         jax.ShapeDtypeStruct((2 * one.shape[0], one.shape[1]), bf16),
         VMEM,
-        [VMEM, VMEM],
+        [VMEM, VMEM, ANY],
         [],
-        cost(15 * 10**8),
-    )(one, two)
-
-
-def second_local(count, side_a, side_b, phase, row, own, other, out, wall, phase_wall, block, first):
+        cost(flops),
+    )(one, two, after)
+
+
+def second_local(count, side_a, side_b, phase, row, out, wall, phase_wall, first):
     layers, rows, depth = out.shape
-    n = own.shape[0]
-    block[pl.ds(0, n), :] = own[...]
-    block[pl.ds(n, n), :] = other[...]
     own = layers_of(side_a) + layers_of(side_b)[::-1]
     for d in range(layers):
         clear_margins((first, (d,)))
@@ -434,7 +431,7 @@
     local_step(own, layers_of(first), phase, row, count, emit)
 
 
-def make_second_local(side_a, side_b, phase, row, own, other, count):
+def make_second_local(side_a, side_b, phase, row, count):
     layers, rows, depth = phase.shape
     return call(
         lambda *refs: second_local(count, *refs),
@@ -442,13 +439,12 @@
             jax.ShapeDtypeStruct((layers, rows, depth), f32),
             jax.ShapeDtypeStruct((layers, 8, rows), f32),
             jax.ShapeDtypeStruct((layers, 8, rows), f32),
-            jax.ShapeDtypeStruct((2 * own.shape[0], depth), bf16),
         ),
-        (VMEM,) * 4,
-        [VMEM] * 6,
+        (VMEM,) * 3,
+        [VMEM] * 4,
         [padded(rows, depth, layers)],
         cost(13 * 10**8),
-    )(side_a, side_b, phase, row, own, other)
+    )(side_a, side_b, phase, row)
 
 
 def injection(n, phase, pre, *refs):
@@ -495,7 +491,7 @@
             out[:4, pl.ds(y + 128 * i, 128)] = both[4 * i : 4 * i + 4]
 
 
-def wall_kernel(wall, phase_wall, early_a, from_b, mask, out, from_a):
+def wall_kernel(wall, phase_wall, early_a, from_b, mask, after, out, from_a):
     layers = wall.shape[0]
     unpack_walls(early_a, from_a)
     odd = is_odd()
@@ -513,15 +509,15 @@
         out[:, l, :] = mask[:, l, :] * jnp.where(odd, terms[l], terms[layers - 1 - l])
 
 
-def make_walls(wall, phase_wall, early_a, from_b, mask):
+def make_walls(wall, phase_wall, early_a, from_b, mask, after):
     return call(
         wall_kernel,
         jax.ShapeDtypeStruct(mask.shape, f32),
         VMEM,
-        [VMEM] * 5,
+        [VMEM] * 5 + [ANY],
         [pltpu.VMEM(wall.shape[1:], f32)],
         cost(3 * 10**8),
-    )(wall, phase_wall, early_a, from_b, mask)
+    )(wall, phase_wall, early_a, from_b, mask, after)
 
 
 def layers_at_a(message, phase, state, out, halo):
@@ -628,14 +624,15 @@
     later_a = send(message, 0)
     four = far = pair
     if few:
-        four = make_join(pair, lax.ppermute(pair, "slab", [(i, i ^ 2) for i in range(count)]))
-        far = lax.ppermute(four, "slab", [(i, i ^ 4) for i in range(count)])
+        four = make_join(pair, lax.ppermute(pair, "slab", [(i, i ^ 4) for i in range(count)]), pair, 15 * 10**8)
+        far = lax.ppermute(four, "slab", [(i, i ^ 2) for i in range(count)])
     half_b, message, walls_b = make_middle_b(from_b, pre, phase, near_walls, four, count)
     later_b = send(message, 1)
-    pre, wall, phase_wall, block = make_second_local(half_a, half_b, phase, row, four, far, count)
+    pre, wall, phase_wall = make_second_local(half_a, half_b, phase, row, count)
+    block = make_join(four, far, wall, 1)
     if not few:
         block = lax.all_gather(first[2 * state.shape[1] :], "slab", axis=0, tiled=True)
-    part = make_walls(wall, phase_wall, early, walls_b, mask)
+    part = make_walls(wall, phase_wall, early, walls_b, mask, block)
     if lax.axis_size("cond") == 4:
         walls = [part] + [lax.ppermute(part, "cond", [(i, i ^ k) for i in range(4)]) for k in (3, 2, 1)]
     else:

time: 31 us -> 30.6 us (0.987); the launches traced: 30.4 us -> 30.4 us
  starting transfers between devices: 11.8 us -> 13.3 us
  waiting for transfers between devices: 8.75 us -> 7.32 us
    ppermute x5, waiting for transfers between devices: 6.77 us -> 4.82 us  [send(): return lax.ppermute(v, 'slab', pairs[side])]
    ppermute x5, starting transfers between devices: 6.77 us -> 8.57 us  [send(): return lax.ppermute(v, 'slab', pairs[side])]
    ppermute x2, waiting for transfers between devices: 1.97 us -> 2.49 us  [the longest x1 2.49 us: on_device(): lax.ppermute(pair, 'slab', [(i, i ^ 4) for i in range(count)])]
    ppermute x2, starting transfers between devices: 0.45 us -> 0.08 us  [the longest x1 0.06 us: on_device(): lax.ppermute(pair, 'slab', [(i, i ^ 4) for i in range(count)])]
where the time goes in v7:
time: 30.6 us; the launch traced here: 30.4 us
  starting transfers between devices  13.3 us (43%)
  Pallas kernels  8.42 us (28%)
  waiting for transfers between devices  7.32 us (24%)
  between operations  1.43 us (5%)
    ppermute x5, starting transfers between devices, send(): return lax.ppermute(v, 'slab', pairs[side])  8.57 us
    ppermute x5, waiting for transfers between devices, send(): return lax.ppermute(v, 'slab', pairs[side])  4.82 us
    ppermute x3, starting transfers between devices, on_device(): lax.ppermute(part, 'cond', [(i, i ^ k) for i in range(4)])  4.61 us
    ppermute x1, waiting for transfers between devices, on_device(): lax.ppermute(pair, 'slab', [(i, i ^ 4) for i in range(count)])  2.49 us
    pallas_call x1, Pallas kernels, make_first_local(): call(lambda *refs: first_local(count, *refs), (jax.ShapeDtypeStruct(adjoi...  2.28 us
    pallas_call x1, Pallas kernels, make_second_local(): call(lambda *refs: second_local(count, *refs), (jax.ShapeDtypeStruct((lay...  1.76 us
    pallas_call x1, Pallas kernels, make_first_message(): call(first_message, (jax.ShapeDtypeStruct((2 * rows + extra, depth), bf16...  1.42 us
    pallas_call x1, Pallas kernels, make_final(): call(final, (jax.ShapeDtypeStruct(state.shape, f32), jax.ShapeDtypeStruct...  1.04 us
  transfers between devices with their start and end apart: 10, of which 4 were waited for; matrix products, arithmetic and copies ran while one was open for 0% of the time, Pallas kernels for 20%

profile of v7, /device:TPU:25, one launch (start us, length us, event | category | flops | bytes accessed | tf_op | source)
XLA Modules:
  0.0 30.4 jit_solution(15611944875927485648)
XLA Ops:
  0.6 0.0 copy-start
  0.7 1.4 %shard_map.95 = (bf16[1072,128]{1,0:T(8,128)(2,1)S(1)}, f32[1,8]{1,0:T(1,128)S(1)}) custom-call(f32[4,512,128]{2,1,0:T(8,128)} %bitcast.13, bf16[32,128]{1,0:T(8,128)(2,1)} %bitcast.16, s32[1,32]{1,0:T(1,128)} %bitcast.17, s32[1,32]{1,0:T(1,128)} %cells.1, f32[1,8]{1,0:T(1,128)} %bitcast.18), custom_call_target="tpu_custom_call" | custom-call | flops 10000000000 | bytes 1 | tf_op jit(solution)/shard_map/pallas_call | solution.py:177
  2.1 1.3 %collective-permute-start = (bf16[1072,128]{1,0:T(8,128)(2,1)S(1)}, bf16[1072,128]{1,0:T(8,128)(2,1)S(1)}, u32[]{:S(2)}, u32[]{:S(2)}) collective-permute-start(bf16[1072,128]{1,0:T(8,128)(2,1)S(1)} %get-tuple-element.21.refs_5_.first), channel_id=1, source_target_pairs={{0,1},{1,0},{2,3},{3,2},{4,5},{5,4},{6,7},{7,6},{8,9},{9,8},{10,11... | collective-permute-start | bytes 823304 | tf_op jit(solution)/shard_map/ppermute | solution.py:614
  4.0 0.0 copy-done
  4.1 0.0 copy-done.1
  4.1 0.0 copy-done.2
  4.1 2.3 %shard_map.96 = (f32[4,512,128]{2,1,0:T(8,128)S(1)}, bf16[1088,128]{1,0:T(8,128)(2,1)S(1)}, f32[8,128]{1,0:T(8,128)S(1)}, f32[2,4,512]{2,1,0:T(4,128)S(1)}, f32[8,512]{1,0:T(8,128)S(1)}) custom-call(f32[4,512,128]{2,1,0:T(8,128)S(1)} %bitcast.14, bf16[4,512,128]{2,1,0:T(8,128)(2,1)S(1)} %bitcast.6, f32[1,8]{1,0:T(1,128)S(1)} %get-tuple-element.22.refs_2_, ...), custom_call_target="tpu_custom_call" | custom-call | flops 10000000000 | bytes 1 | tf_op jit(solution)/shard_map/pallas_call | solution.py:232
  6.4 2.0 %collective-permute-start.2 = (bf16[1088,128]{1,0:T(8,128)(2,1)S(1)}, bf16[1088,128]{1,0:T(8,128)(2,1)S(1)}, u32[]{:S(2)}, u32[]{:S(2)}) collective-permute-start(bf16[1088,128]{1,0:T(8,128)(2,1)S(1)} %get-tuple-element.26), channel_id=1, source_target_pairs={{1,2},{3,4},{5,6},{2,1},{4,3},{6,5},{9,10},{11,12},{13,14},{10,9},... | collective-permute-start | bytes 835592 | tf_op jit(solution)/shard_map/ppermute | solution.py:614
  8.4 1.2 %collective-permute-done.message = bf16[1072,128]{1,0:T(8,128)(2,1)S(1)} collective-permute-done((bf16[1072,128]{1,0:T(8,128)(2,1)S(1)}, bf16[1072,128]{1,0:T(8,128)(2,1)S(1)}, u32[]{:S(2)}, u32[]{:S(2)}) %collective-permute-start) | collective-permute-done | bytes 274464 | tf_op jit(solution)/shard_map/ppermute | solution.py:614
  9.6 0.7 %shard_map.97 = (f32[2,528,128]{2,1,0:T(8,128)S(1)}, bf16[1024,128]{1,0:T(8,128)(2,1)S(1)}, bf16[32,128]{1,0:T(8,128)(2,1)S(1)}, bf16[96,128]{1,0:T(8,128)(2,1)S(1)}) custom-call(bf16[1072,128]{1,0:T(8,128)(2,1)S(1)} %collective-permute-done.message, f32[4,512,128]{2,1,0:T(8,128)S(1)} %get-tuple-element.23.pre.refs_1_, bf16[4,512,128]{2,1,0:T(8,128)(2,1)S(1)} %bitcast.7, ...), custom_call_target="tpu_custom_call" | custom-call | flops 10000000000 | bytes 1 | tf_op jit(solution)/shard_map/pallas_call | solution.py:340
  10.3 0.1 collective-permute-start.3
  10.4 1.2 %collective-permute-start.6 = (bf16[32,128]{1,0:T(8,128)(2,1)S(1)}, bf16[32,128]{1,0:T(8,128)(2,1)S(1)}, u32[]{:S(2)}, u32[]{:S(2)}) collective-permute-start(bf16[32,128]{1,0:T(8,128)(2,1)S(1)} %get-tuple-element.35), channel_id=1, source_target_pairs={{0,1},{1,0},{2,3},{3,2},{4,5},{5,4},{6,7},{7,6},{8,9},{9,8},{10,11... | collective-permute-start | bytes 24584 | tf_op jit(solution)/shard_map/ppermute | solution.py:614
  11.6 0.2 collective-permute-start.1
  11.8 2.5 %collective-permute-done.3.two = bf16[96,128]{1,0:T(8,128)(2,1)S(1)} collective-permute-done((bf16[96,128]{1,0:T(8,128)(2,1)S(1)}, bf16[96,128]{1,0:T(8,128)(2,1)S(1)}, u32[]{:S(2)}, u32[]{:S(2)}) %collective-permute-start.3) | collective-permute-done | bytes 24608 | tf_op jit(solution)/shard_map/ppermute | solution.py:627
  14.3 0.0 collective-permute-start.4
  14.3 2.1 %collective-permute-done.2.refs_0_ = bf16[1088,128]{1,0:T(8,128)(2,1)S(1)} collective-permute-done((bf16[1088,128]{1,0:T(8,128)(2,1)S(1)}, bf16[1088,128]{1,0:T(8,128)(2,1)S(1)}, u32[]{:S(2)}, u32[]{:S(2)}) %collective-permute-start.2) | collective-permute-done | bytes 278560 | tf_op jit(solution)/shard_map/ppermute | solution.py:614
  16.4 0.4 %shard_map.99 = (f32[2,528,128]{2,1,0:T(8,128)S(1)}, bf16[1024,128]{1,0:T(8,128)(2,1)S(1)}, f32[8,512]{1,0:T(8,128)S(1)}) custom-call(bf16[1088,128]{1,0:T(8,128)(2,1)S(1)} %collective-permute-done.2.refs_0_, f32[4,512,128]{2,1,0:T(8,128)S(1)} %get-tuple-element.23.pre.refs_1_, bf16[4,512,128]{2,1,0:T(8,128)(2,1)S(1)} %bitcast.8, ...), custom_call_target="tpu_custom_call" | custom-call | flops 600000000 | bytes 1 | tf_op jit(solution)/shard_map/pallas_call | solution.py:384
  16.8 3.8 %collective-permute-start.5 = (bf16[1024,128]{1,0:T(8,128)(2,1)S(1)}, bf16[1024,128]{1,0:T(8,128)(2,1)S(1)}, u32[]{:S(2)}, u32[]{:S(2)}) collective-permute-start(bf16[1024,128]{1,0:T(8,128)(2,1)S(1)} %get-tuple-element.33), channel_id=1, source_target_pairs={{1,2},{3,4},{5,6},{2,1},{4,3},{6,5},{9,10},{11,12},{13,14},{10,9},... | collective-permute-start | bytes 786440 | tf_op jit(solution)/shard_map/ppermute | solution.py:614
  20.6 1.8 %shard_map.100 = (f32[4,512,128]{2,1,0:T(8,128)S(1)}, f32[4,8,512]{2,1,0:T(8,128)S(1)}, f32[4,8,512]{2,1,0:T(8,128)S(1)}) custom-call(f32[2,528,128]{2,1,0:T(8,128)S(1)} %get-tuple-element.25.refs_0_, f32[2,528,128]{2,1,0:T(8,128)S(1)} %get-tuple-element.29.refs_1_, bf16[4,512,128]{2,1,0:T(8,128)(2,1)S(1)} %bitcast.9, f32[8,128]{1,0:T(8,128)S(1)} %get-tuple-element.30.refs_3_), custom_call_target="tpu_custom_call" | custom-call | flops 1300000000 | bytes 1 | tf_op jit(solution)/shard_map/pallas_call | solution.py:436
  22.4 0.0 collective-permute-done.4.two
  22.4 0.0 collective-permute-done.6.early_a
  22.5 4.1 %collective-permute-start.7 = (f32[2,4,512]{2,1,0:T(4,128)S(1)}, f32[2,4,512]{2,1,0:T(4,128)S(1)}, u32[]{:S(2)}, u32[]{:S(2)}) collective-permute-start(f32[2,4,512]{2,1,0:T(4,128)S(1)} %shard_map.104.refs_0_), channel_id=1, source_target_pairs={{0,24},{8,16},{16,8},{24,0},{1,25},{9,17},{17,9},{25,1},{2,26},{10... | collective-permute-start | bytes 49160 | tf_op jit(solution)/shard_map/ppermute | solution.py:637
  26.6 0.3 collective-permute-start.8
  26.9 0.2 collective-permute-start.9
  27.1 0.5 %shard_map.102.state = f32[4,512,128]{2,1,0:T(8,128)S(1)} custom-call(bf16[4,512,128]{2,1,0:T(8,128)(2,1)S(1)} %bitcast.10, f32[4,512,128]{2,1,0:T(8,128)S(1)} %get-tuple-element.31.refs_1_, bf16[384,128]{1,0:T(8,128)(2,1)S(1)} %shard_map.101.refs_2_.after), custom_call_target="tpu_custom_call" | custom-call | flops 1 | bytes 1 | tf_op jit(solution)/shard_map/pallas_call | solution.py:476
  27.6 1.6 %collective-permute-done.1.message = bf16[1024,128]{1,0:T(8,128)(2,1)S(1)} collective-permute-done((bf16[1024,128]{1,0:T(8,128)(2,1)S(1)}, bf16[1024,128]{1,0:T(8,128)(2,1)S(1)}, u32[]{:S(2)}, u32[]{:S(2)}) %collective-permute-start.1) | collective-permute-done | bytes 262176 | tf_op jit(solution)/shard_map/ppermute | solution.py:614
  29.1 0.2 shard_map.103.at_a
  29.4 0.0 collective-permute-done.7.refs_1_
  29.4 0.0 collective-permute-done.8.refs_2_
  29.4 0.0 collective-permute-done.9.refs_3_
  29.4 0.0 collective-permute-done.5.message_b
  29.4 1.0 %shard_map.105 = (f32[4,512,128]{2,1,0:T(8,128)}, f32[2,4,512]{2,1,0:T(4,128)}) custom-call(f32[2,512,128]{2,1,0:T(8,128)S(1)} %shard_map.103.at_a, bf16[1024,128]{1,0:T(8,128)(2,1)S(1)} %collective-permute-done.5.message_b, f32[4,512,128]{2,1,0:T(8,128)S(1)} %shard_map.102.state, bf16[4,512,128]{2,1,0:T(8,128)(2,1)S(1)} %bitcast.12, ...), custom_call_target="tpu_custom_call" | custom-call | flops 1 | bytes 1 | tf_op jit(solution)/shard_map/pallas_call | solution.py:589
  (5 shorter events, 0.1 us)
Async XLA Ops:
  0.6 3.4 %copy-start = (bf16[1,4,512,128]{3,2,1,0:T(8,128)(2,1)S(1)}, bf16[1,4,512,128]{3,2,1,0:T(8,128)(2,1)}, u32[]{:S(2)}) copy-start(bf16[1,4,512,128]{3,2,1,0:T(8,128)(2,1)} %param.9) | copy-start | bytes 1572868
  0.6 3.4 %copy-start.1 = (f32[1,4,512,128]{3,2,1,0:T(8,128)S(1)}, f32[1,4,512,128]{3,2,1,0:T(8,128)}, u32[]{:S(2)}) copy-start(f32[1,4,512,128]{3,2,1,0:T(8,128)} %param.8) | copy-start | bytes 3145732
  0.7 3.4 %copy-start.2 = (s32[2,4,512]{2,1,0:T(4,128)S(1)}, s32[2,4,512]{2,1,0:T(4,128)}, u32[]{:S(2)}) copy-start(s32[2,4,512]{2,1,0:T(4,128)} %refs_4_.1) | copy-start | bytes 49156
  2.1 7.5 %collective-permute-start = (bf16[1072,128]{1,0:T(8,128)(2,1)S(1)}, bf16[1072,128]{1,0:T(8,128)(2,1)S(1)}, u32[]{:S(2)}, u32[]{:S(2)}) collective-permute-start(bf16[1072,128]{1,0:T(8,128)(2,1)S(1)} %get-tuple-element.21.refs_5_.first), channel_id=1, source_target_pairs={{0,1},{1,0},{2,3},{3,2},{4,5},{5,4},{6,7},{7,6},{8,9},{9,8},{10,11... | collective-permute-start | bytes 823304 | tf_op jit(solution)/shard_map/ppermute | solution.py:614
  6.4 10.0 %collective-permute-start.2 = (bf16[1088,128]{1,0:T(8,128)(2,1)S(1)}, bf16[1088,128]{1,0:T(8,128)(2,1)S(1)}, u32[]{:S(2)}, u32[]{:S(2)}) collective-permute-start(bf16[1088,128]{1,0:T(8,128)(2,1)S(1)} %get-tuple-element.26), channel_id=1, source_target_pairs={{1,2},{3,4},{5,6},{2,1},{4,3},{6,5},{9,10},{11,12},{13,14},{10,9},... | collective-permute-start | bytes 835592 | tf_op jit(solution)/shard_map/ppermute | solution.py:614
  10.3 4.0 %collective-permute-start.3 = (bf16[96,128]{1,0:T(8,128)(2,1)S(1)}, bf16[96,128]{1,0:T(8,128)(2,1)S(1)}, u32[]{:S(2)}, u32[]{:S(2)}) collective-permute-start(bf16[96,128]{1,0:T(8,128)(2,1)S(1)} %get-tuple-element.28.one.after), channel_id=1, source_target_pairs={{0,4},{1,5},{2,6},{3,7},{4,0},{5,1},{6,2},{7,3},{8,12},{9,13},{10,... | collective-permute-start | bytes 73736 | tf_op jit(solution)/shard_map/ppermute | solution.py:627
  10.4 12.0 %collective-permute-start.6 = (bf16[32,128]{1,0:T(8,128)(2,1)S(1)}, bf16[32,128]{1,0:T(8,128)(2,1)S(1)}, u32[]{:S(2)}, u32[]{:S(2)}) collective-permute-start(bf16[32,128]{1,0:T(8,128)(2,1)S(1)} %get-tuple-element.35), channel_id=1, source_target_pairs={{0,1},{1,0},{2,3},{3,2},{4,5},{5,4},{6,7},{7,6},{8,9},{9,8},{10,11... | collective-permute-start | bytes 24584 | tf_op jit(solution)/shard_map/ppermute | solution.py:614
  11.6 17.5 %collective-permute-start.1 = (bf16[1024,128]{1,0:T(8,128)(2,1)S(1)}, bf16[1024,128]{1,0:T(8,128)(2,1)S(1)}, u32[]{:S(2)}, u32[]{:S(2)}) collective-permute-start(bf16[1024,128]{1,0:T(8,128)(2,1)S(1)} %get-tuple-element.24), channel_id=1, source_target_pairs={{0,1},{1,0},{2,3},{3,2},{4,5},{5,4},{6,7},{7,6},{8,9},{9,8},{10,11... | collective-permute-start | bytes 786440 | tf_op jit(solution)/shard_map/ppermute | solution.py:614
  14.3 8.0 %collective-permute-start.4 = (bf16[192,128]{1,0:T(8,128)(2,1)S(1)}, bf16[192,128]{1,0:T(8,128)(2,1)S(1)}, u32[]{:S(2)}, u32[]{:S(2)}) collective-permute-start(bf16[192,128]{1,0:T(8,128)(2,1)S(1)} %shard_map.98.refs_4_.one), channel_id=1, source_target_pairs={{0,2},{1,3},{2,0},{3,1},{4,6},{5,7},{6,4},{7,5},{8,10},{9,11},{10,... | collective-permute-start | bytes 147464 | tf_op jit(solution)/shard_map/ppermute | solution.py:628
  16.8 12.6 %collective-permute-start.5 = (bf16[1024,128]{1,0:T(8,128)(2,1)S(1)}, bf16[1024,128]{1,0:T(8,128)(2,1)S(1)}, u32[]{:S(2)}, u32[]{:S(2)}) collective-permute-start(bf16[1024,128]{1,0:T(8,128)(2,1)S(1)} %get-tuple-element.33), channel_id=1, source_target_pairs={{1,2},{3,4},{5,6},{2,1},{4,3},{6,5},{9,10},{11,12},{13,14},{10,9},... | collective-permute-start | bytes 786440 | tf_op jit(solution)/shard_map/ppermute | solution.py:614
  22.5 6.9 %collective-permute-start.7 = (f32[2,4,512]{2,1,0:T(4,128)S(1)}, f32[2,4,512]{2,1,0:T(4,128)S(1)}, u32[]{:S(2)}, u32[]{:S(2)}) collective-permute-start(f32[2,4,512]{2,1,0:T(4,128)S(1)} %shard_map.104.refs_0_), channel_id=1, source_target_pairs={{0,24},{8,16},{16,8},{24,0},{1,25},{9,17},{17,9},{25,1},{2,26},{10... | collective-permute-start | bytes 49160 | tf_op jit(solution)/shard_map/ppermute | solution.py:637
  26.6 2.8 %collective-permute-start.8 = (f32[2,4,512]{2,1,0:T(4,128)S(1)}, f32[2,4,512]{2,1,0:T(4,128)S(1)}, u32[]{:S(2)}, u32[]{:S(2)}) collective-permute-start(f32[2,4,512]{2,1,0:T(4,128)S(1)} %shard_map.104.refs_0_), channel_id=1, source_target_pairs={{0,16},{8,24},{16,0},{24,8},{1,17},{9,25},{17,1},{25,9},{2,18},{10... | collective-permute-start | bytes 49160 | tf_op jit(solution)/shard_map/ppermute | solution.py:637
  26.9 2.5 %collective-permute-start.9 = (f32[2,4,512]{2,1,0:T(4,128)S(1)}, f32[2,4,512]{2,1,0:T(4,128)S(1)}, u32[]{:S(2)}, u32[]{:S(2)}) collective-permute-start(f32[2,4,512]{2,1,0:T(4,128)S(1)} %shard_map.104.refs_0_), channel_id=1, source_target_pairs={{0,8},{8,0},{16,24},{24,16},{1,9},{9,1},{17,25},{25,17},{2,10},{10... | collective-permute-start | bytes 49160 | tf_op jit(solution)/shard_map/ppermute | solution.py:637

commit v8 on v7

--- a/solution.py
+++ b/solution.py
@@ -550,7 +550,7 @@
 def final(at_a, message_b, state, phase, *refs):
     walls, (out, total, planes, summed, halo, sems) = refs[:-6], refs[-6:]
     layers, rows, depth = state.shape
-    half = rows // 2
+    half = rows // 4
     copies = []
 
     def send(source, target):
@@ -595,7 +595,7 @@
             pltpu.VMEM((2, rows, depth), f32),
             pltpu.VMEM(walls[0].shape, f32),
             padded(rows, depth),
-            pltpu.SemaphoreType.DMA((7,)),
+            pltpu.SemaphoreType.DMA((11,)),
         ],
         cost(1),
     )(at_a, message_b, state, phase, *walls)

time: 30.6 us -> 30.7 us (level)
  no operation moved by 1% of the time
where the time goes in v8:
time: 30.7 us; the launch traced here: 30.5 us
  starting transfers between devices  13.3 us (43%)
  Pallas kernels  8.45 us (28%)
  waiting for transfers between devices  7.32 us (24%)
  between operations  1.43 us (5%)
    ppermute x5, starting transfers between devices, send(): return lax.ppermute(v, 'slab', pairs[side])  8.57 us
    ppermute x5, waiting for transfers between devices, send(): return lax.ppermute(v, 'slab', pairs[side])  4.82 us
    ppermute x3, starting transfers between devices, on_device(): lax.ppermute(part, 'cond', [(i, i ^ k) for i in range(4)])  4.61 us
    ppermute x1, waiting for transfers between devices, on_device(): lax.ppermute(pair, 'slab', [(i, i ^ 4) for i in range(count)])  2.49 us
    pallas_call x1, Pallas kernels, make_first_local(): call(lambda *refs: first_local(count, *refs), (jax.ShapeDtypeStruct(adjoi...  2.28 us
    pallas_call x1, Pallas kernels, make_second_local(): call(lambda *refs: second_local(count, *refs), (jax.ShapeDtypeStruct((lay...  1.76 us
    pallas_call x1, Pallas kernels, make_first_message(): call(first_message, (jax.ShapeDtypeStruct((2 * rows + extra, depth), bf16...  1.42 us
    pallas_call x1, Pallas kernels, make_final(): call(final, (jax.ShapeDtypeStruct(state.shape, f32), jax.ShapeDtypeStruct...  1.07 us
  transfers between devices with their start and end apart: 10, of which 4 were waited for; matrix products, arithmetic and copies ran while one was open for 0% of the time, Pallas kernels for 20%

profile of v8, /device:TPU:25, one launch (start us, length us, event | category | flops | bytes accessed | tf_op | source)
XLA Modules:
  0.0 30.5 jit_solution(9104411414503122625)
XLA Ops:
  0.6 0.0 copy-start
  0.7 1.4 %shard_map.95 = (bf16[1072,128]{1,0:T(8,128)(2,1)S(1)}, f32[1,8]{1,0:T(1,128)S(1)}) custom-call(f32[4,512,128]{2,1,0:T(8,128)} %bitcast.13, bf16[32,128]{1,0:T(8,128)(2,1)} %bitcast.16, s32[1,32]{1,0:T(1,128)} %bitcast.17, s32[1,32]{1,0:T(1,128)} %cells.1, f32[1,8]{1,0:T(1,128)} %bitcast.18), custom_call_target="tpu_custom_call" | custom-call | flops 10000000000 | bytes 1 | tf_op jit(solution)/shard_map/pallas_call | solution.py:177
  2.1 1.3 %collective-permute-start = (bf16[1072,128]{1,0:T(8,128)(2,1)S(1)}, bf16[1072,128]{1,0:T(8,128)(2,1)S(1)}, u32[]{:S(2)}, u32[]{:S(2)}) collective-permute-start(bf16[1072,128]{1,0:T(8,128)(2,1)S(1)} %get-tuple-element.21.refs_5_.first), channel_id=1, source_target_pairs={{0,1},{1,0},{2,3},{3,2},{4,5},{5,4},{6,7},{7,6},{8,9},{9,8},{10,11... | collective-permute-start | bytes 823304 | tf_op jit(solution)/shard_map/ppermute | solution.py:614
  4.0 0.0 copy-done
  4.1 0.0 copy-done.1
  4.1 0.0 copy-done.2
  4.1 2.3 %shard_map.96 = (f32[4,512,128]{2,1,0:T(8,128)S(1)}, bf16[1088,128]{1,0:T(8,128)(2,1)S(1)}, f32[8,128]{1,0:T(8,128)S(1)}, f32[2,4,512]{2,1,0:T(4,128)S(1)}, f32[8,512]{1,0:T(8,128)S(1)}) custom-call(f32[4,512,128]{2,1,0:T(8,128)S(1)} %bitcast.14, bf16[4,512,128]{2,1,0:T(8,128)(2,1)S(1)} %bitcast.6, f32[1,8]{1,0:T(1,128)S(1)} %get-tuple-element.22.refs_2_, ...), custom_call_target="tpu_custom_call" | custom-call | flops 10000000000 | bytes 1 | tf_op jit(solution)/shard_map/pallas_call | solution.py:232
  6.4 2.0 %collective-permute-start.2 = (bf16[1088,128]{1,0:T(8,128)(2,1)S(1)}, bf16[1088,128]{1,0:T(8,128)(2,1)S(1)}, u32[]{:S(2)}, u32[]{:S(2)}) collective-permute-start(bf16[1088,128]{1,0:T(8,128)(2,1)S(1)} %get-tuple-element.26), channel_id=1, source_target_pairs={{1,2},{3,4},{5,6},{2,1},{4,3},{6,5},{9,10},{11,12},{13,14},{10,9},... | collective-permute-start | bytes 835592 | tf_op jit(solution)/shard_map/ppermute | solution.py:614
  8.4 1.2 %collective-permute-done.message = bf16[1072,128]{1,0:T(8,128)(2,1)S(1)} collective-permute-done((bf16[1072,128]{1,0:T(8,128)(2,1)S(1)}, bf16[1072,128]{1,0:T(8,128)(2,1)S(1)}, u32[]{:S(2)}, u32[]{:S(2)}) %collective-permute-start) | collective-permute-done | bytes 274464 | tf_op jit(solution)/shard_map/ppermute | solution.py:614
  9.6 0.7 %shard_map.97 = (f32[2,528,128]{2,1,0:T(8,128)S(1)}, bf16[1024,128]{1,0:T(8,128)(2,1)S(1)}, bf16[32,128]{1,0:T(8,128)(2,1)S(1)}, bf16[96,128]{1,0:T(8,128)(2,1)S(1)}) custom-call(bf16[1072,128]{1,0:T(8,128)(2,1)S(1)} %collective-permute-done.message, f32[4,512,128]{2,1,0:T(8,128)S(1)} %get-tuple-element.23.pre.refs_1_, bf16[4,512,128]{2,1,0:T(8,128)(2,1)S(1)} %bitcast.7, ...), custom_call_target="tpu_custom_call" | custom-call | flops 10000000000 | bytes 1 | tf_op jit(solution)/shard_map/pallas_call | solution.py:340
  10.3 0.1 collective-permute-start.3
  10.4 1.2 %collective-permute-start.6 = (bf16[32,128]{1,0:T(8,128)(2,1)S(1)}, bf16[32,128]{1,0:T(8,128)(2,1)S(1)}, u32[]{:S(2)}, u32[]{:S(2)}) collective-permute-start(bf16[32,128]{1,0:T(8,128)(2,1)S(1)} %get-tuple-element.35), channel_id=1, source_target_pairs={{0,1},{1,0},{2,3},{3,2},{4,5},{5,4},{6,7},{7,6},{8,9},{9,8},{10,11... | collective-permute-start | bytes 24584 | tf_op jit(solution)/shard_map/ppermute | solution.py:614
  11.6 0.2 collective-permute-start.1
  11.8 2.5 %collective-permute-done.3.two = bf16[96,128]{1,0:T(8,128)(2,1)S(1)} collective-permute-done((bf16[96,128]{1,0:T(8,128)(2,1)S(1)}, bf16[96,128]{1,0:T(8,128)(2,1)S(1)}, u32[]{:S(2)}, u32[]{:S(2)}) %collective-permute-start.3) | collective-permute-done | bytes 24608 | tf_op jit(solution)/shard_map/ppermute | solution.py:627
  14.3 0.0 collective-permute-start.4
  14.3 2.1 %collective-permute-done.2.refs_0_ = bf16[1088,128]{1,0:T(8,128)(2,1)S(1)} collective-permute-done((bf16[1088,128]{1,0:T(8,128)(2,1)S(1)}, bf16[1088,128]{1,0:T(8,128)(2,1)S(1)}, u32[]{:S(2)}, u32[]{:S(2)}) %collective-permute-start.2) | collective-permute-done | bytes 278560 | tf_op jit(solution)/shard_map/ppermute | solution.py:614
  16.4 0.4 %shard_map.99 = (f32[2,528,128]{2,1,0:T(8,128)S(1)}, bf16[1024,128]{1,0:T(8,128)(2,1)S(1)}, f32[8,512]{1,0:T(8,128)S(1)}) custom-call(bf16[1088,128]{1,0:T(8,128)(2,1)S(1)} %collective-permute-done.2.refs_0_, f32[4,512,128]{2,1,0:T(8,128)S(1)} %get-tuple-element.23.pre.refs_1_, bf16[4,512,128]{2,1,0:T(8,128)(2,1)S(1)} %bitcast.8, ...), custom_call_target="tpu_custom_call" | custom-call | flops 600000000 | bytes 1 | tf_op jit(solution)/shard_map/pallas_call | solution.py:384
  16.8 3.8 %collective-permute-start.5 = (bf16[1024,128]{1,0:T(8,128)(2,1)S(1)}, bf16[1024,128]{1,0:T(8,128)(2,1)S(1)}, u32[]{:S(2)}, u32[]{:S(2)}) collective-permute-start(bf16[1024,128]{1,0:T(8,128)(2,1)S(1)} %get-tuple-element.33), channel_id=1, source_target_pairs={{1,2},{3,4},{5,6},{2,1},{4,3},{6,5},{9,10},{11,12},{13,14},{10,9},... | collective-permute-start | bytes 786440 | tf_op jit(solution)/shard_map/ppermute | solution.py:614
  20.6 1.8 %shard_map.100 = (f32[4,512,128]{2,1,0:T(8,128)S(1)}, f32[4,8,512]{2,1,0:T(8,128)S(1)}, f32[4,8,512]{2,1,0:T(8,128)S(1)}) custom-call(f32[2,528,128]{2,1,0:T(8,128)S(1)} %get-tuple-element.25.refs_0_, f32[2,528,128]{2,1,0:T(8,128)S(1)} %get-tuple-element.29.refs_1_, bf16[4,512,128]{2,1,0:T(8,128)(2,1)S(1)} %bitcast.9, f32[8,128]{1,0:T(8,128)S(1)} %get-tuple-element.30.refs_3_), custom_call_target="tpu_custom_call" | custom-call | flops 1300000000 | bytes 1 | tf_op jit(solution)/shard_map/pallas_call | solution.py:436
  22.4 0.0 collective-permute-done.4.two
  22.4 0.0 collective-permute-done.6.early_a
  22.5 4.1 %collective-permute-start.7 = (f32[2,4,512]{2,1,0:T(4,128)S(1)}, f32[2,4,512]{2,1,0:T(4,128)S(1)}, u32[]{:S(2)}, u32[]{:S(2)}) collective-permute-start(f32[2,4,512]{2,1,0:T(4,128)S(1)} %shard_map.104.refs_0_), channel_id=1, source_target_pairs={{0,24},{8,16},{16,8},{24,0},{1,25},{9,17},{17,9},{25,1},{2,26},{10... | collective-permute-start | bytes 49160 | tf_op jit(solution)/shard_map/ppermute | solution.py:637
  26.6 0.3 collective-permute-start.8
  26.9 0.2 collective-permute-start.9
  27.1 0.5 %shard_map.102.state = f32[4,512,128]{2,1,0:T(8,128)S(1)} custom-call(bf16[4,512,128]{2,1,0:T(8,128)(2,1)S(1)} %bitcast.10, f32[4,512,128]{2,1,0:T(8,128)S(1)} %get-tuple-element.31.refs_1_, bf16[384,128]{1,0:T(8,128)(2,1)S(1)} %shard_map.101.refs_2_.after), custom_call_target="tpu_custom_call" | custom-call | flops 1 | bytes 1 | tf_op jit(solution)/shard_map/pallas_call | solution.py:476
  27.6 1.6 %collective-permute-done.1.message = bf16[1024,128]{1,0:T(8,128)(2,1)S(1)} collective-permute-done((bf16[1024,128]{1,0:T(8,128)(2,1)S(1)}, bf16[1024,128]{1,0:T(8,128)(2,1)S(1)}, u32[]{:S(2)}, u32[]{:S(2)}) %collective-permute-start.1) | collective-permute-done | bytes 262176 | tf_op jit(solution)/shard_map/ppermute | solution.py:614
  29.1 0.2 shard_map.103.at_a
  29.4 0.0 collective-permute-done.7.refs_1_
  29.4 0.0 collective-permute-done.8.refs_2_
  29.4 0.0 collective-permute-done.9.refs_3_
  29.4 0.0 collective-permute-done.5.message_b
  29.4 1.1 %shard_map.105 = (f32[4,512,128]{2,1,0:T(8,128)}, f32[2,4,512]{2,1,0:T(4,128)}) custom-call(f32[2,512,128]{2,1,0:T(8,128)S(1)} %shard_map.103.at_a, bf16[1024,128]{1,0:T(8,128)(2,1)S(1)} %collective-permute-done.5.message_b, f32[4,512,128]{2,1,0:T(8,128)S(1)} %shard_map.102.state, bf16[4,512,128]{2,1,0:T(8,128)(2,1)S(1)} %bitcast.12, ...), custom_call_target="tpu_custom_call" | custom-call | flops 1 | bytes 1 | tf_op jit(solution)/shard_map/pallas_call | solution.py:589
  (5 shorter events, 0.1 us)
Async XLA Ops:
  0.6 3.4 %copy-start = (bf16[1,4,512,128]{3,2,1,0:T(8,128)(2,1)S(1)}, bf16[1,4,512,128]{3,2,1,0:T(8,128)(2,1)}, u32[]{:S(2)}) copy-start(bf16[1,4,512,128]{3,2,1,0:T(8,128)(2,1)} %param.9) | copy-start | bytes 1572868
  0.6 3.4 %copy-start.1 = (f32[1,4,512,128]{3,2,1,0:T(8,128)S(1)}, f32[1,4,512,128]{3,2,1,0:T(8,128)}, u32[]{:S(2)}) copy-start(f32[1,4,512,128]{3,2,1,0:T(8,128)} %param.8) | copy-start | bytes 3145732
  0.7 3.4 %copy-start.2 = (s32[2,4,512]{2,1,0:T(4,128)S(1)}, s32[2,4,512]{2,1,0:T(4,128)}, u32[]{:S(2)}) copy-start(s32[2,4,512]{2,1,0:T(4,128)} %refs_4_.1) | copy-start | bytes 49156
  2.1 7.5 %collective-permute-start = (bf16[1072,128]{1,0:T(8,128)(2,1)S(1)}, bf16[1072,128]{1,0:T(8,128)(2,1)S(1)}, u32[]{:S(2)}, u32[]{:S(2)}) collective-permute-start(bf16[1072,128]{1,0:T(8,128)(2,1)S(1)} %get-tuple-element.21.refs_5_.first), channel_id=1, source_target_pairs={{0,1},{1,0},{2,3},{3,2},{4,5},{5,4},{6,7},{7,6},{8,9},{9,8},{10,11... | collective-permute-start | bytes 823304 | tf_op jit(solution)/shard_map/ppermute | solution.py:614
  6.4 10.0 %collective-permute-start.2 = (bf16[1088,128]{1,0:T(8,128)(2,1)S(1)}, bf16[1088,128]{1,0:T(8,128)(2,1)S(1)}, u32[]{:S(2)}, u32[]{:S(2)}) collective-permute-start(bf16[1088,128]{1,0:T(8,128)(2,1)S(1)} %get-tuple-element.26), channel_id=1, source_target_pairs={{1,2},{3,4},{5,6},{2,1},{4,3},{6,5},{9,10},{11,12},{13,14},{10,9},... | collective-permute-start | bytes 835592 | tf_op jit(solution)/shard_map/ppermute | solution.py:614
  10.3 4.0 %collective-permute-start.3 = (bf16[96,128]{1,0:T(8,128)(2,1)S(1)}, bf16[96,128]{1,0:T(8,128)(2,1)S(1)}, u32[]{:S(2)}, u32[]{:S(2)}) collective-permute-start(bf16[96,128]{1,0:T(8,128)(2,1)S(1)} %get-tuple-element.28.one.after), channel_id=1, source_target_pairs={{0,4},{1,5},{2,6},{3,7},{4,0},{5,1},{6,2},{7,3},{8,12},{9,13},{10,... | collective-permute-start | bytes 73736 | tf_op jit(solution)/shard_map/ppermute | solution.py:627
  10.4 12.0 %collective-permute-start.6 = (bf16[32,128]{1,0:T(8,128)(2,1)S(1)}, bf16[32,128]{1,0:T(8,128)(2,1)S(1)}, u32[]{:S(2)}, u32[]{:S(2)}) collective-permute-start(bf16[32,128]{1,0:T(8,128)(2,1)S(1)} %get-tuple-element.35), channel_id=1, source_target_pairs={{0,1},{1,0},{2,3},{3,2},{4,5},{5,4},{6,7},{7,6},{8,9},{9,8},{10,11... | collective-permute-start | bytes 24584 | tf_op jit(solution)/shard_map/ppermute | solution.py:614
  11.6 17.5 %collective-permute-start.1 = (bf16[1024,128]{1,0:T(8,128)(2,1)S(1)}, bf16[1024,128]{1,0:T(8,128)(2,1)S(1)}, u32[]{:S(2)}, u32[]{:S(2)}) collective-permute-start(bf16[1024,128]{1,0:T(8,128)(2,1)S(1)} %get-tuple-element.24), channel_id=1, source_target_pairs={{0,1},{1,0},{2,3},{3,2},{4,5},{5,4},{6,7},{7,6},{8,9},{9,8},{10,11... | collective-permute-start | bytes 786440 | tf_op jit(solution)/shard_map/ppermute | solution.py:614
  14.3 8.0 %collective-permute-start.4 = (bf16[192,128]{1,0:T(8,128)(2,1)S(1)}, bf16[192,128]{1,0:T(8,128)(2,1)S(1)}, u32[]{:S(2)}, u32[]{:S(2)}) collective-permute-start(bf16[192,128]{1,0:T(8,128)(2,1)S(1)} %shard_map.98.refs_4_.one), channel_id=1, source_target_pairs={{0,2},{1,3},{2,0},{3,1},{4,6},{5,7},{6,4},{7,5},{8,10},{9,11},{10,... | collective-permute-start | bytes 147464 | tf_op jit(solution)/shard_map/ppermute | solution.py:628
  16.8 12.6 %collective-permute-start.5 = (bf16[1024,128]{1,0:T(8,128)(2,1)S(1)}, bf16[1024,128]{1,0:T(8,128)(2,1)S(1)}, u32[]{:S(2)}, u32[]{:S(2)}) collective-permute-start(bf16[1024,128]{1,0:T(8,128)(2,1)S(1)} %get-tuple-element.33), channel_id=1, source_target_pairs={{1,2},{3,4},{5,6},{2,1},{4,3},{6,5},{9,10},{11,12},{13,14},{10,9},... | collective-permute-start | bytes 786440 | tf_op jit(solution)/shard_map/ppermute | solution.py:614
  22.5 6.9 %collective-permute-start.7 = (f32[2,4,512]{2,1,0:T(4,128)S(1)}, f32[2,4,512]{2,1,0:T(4,128)S(1)}, u32[]{:S(2)}, u32[]{:S(2)}) collective-permute-start(f32[2,4,512]{2,1,0:T(4,128)S(1)} %shard_map.104.refs_0_), channel_id=1, source_target_pairs={{0,24},{8,16},{16,8},{24,0},{1,25},{9,17},{17,9},{25,1},{2,26},{10... | collective-permute-start | bytes 49160 | tf_op jit(solution)/shard_map/ppermute | solution.py:637
  26.6 2.8 %collective-permute-start.8 = (f32[2,4,512]{2,1,0:T(4,128)S(1)}, f32[2,4,512]{2,1,0:T(4,128)S(1)}, u32[]{:S(2)}, u32[]{:S(2)}) collective-permute-start(f32[2,4,512]{2,1,0:T(4,128)S(1)} %shard_map.104.refs_0_), channel_id=1, source_target_pairs={{0,16},{8,24},{16,0},{24,8},{1,17},{9,25},{17,1},{25,9},{2,18},{10... | collective-permute-start | bytes 49160 | tf_op jit(solution)/shard_map/ppermute | solution.py:637
  26.9 2.5 %collective-permute-start.9 = (f32[2,4,512]{2,1,0:T(4,128)S(1)}, f32[2,4,512]{2,1,0:T(4,128)S(1)}, u32[]{:S(2)}, u32[]{:S(2)}) collective-permute-start(f32[2,4,512]{2,1,0:T(4,128)S(1)} %shard_map.104.refs_0_), channel_id=1, source_target_pairs={{0,8},{8,0},{16,24},{24,16},{1,9},{9,1},{17,25},{25,17},{2,10},{10... | collective-permute-start | bytes 49160 | tf_op jit(solution)/shard_map/ppermute | solution.py:637

commit v9 on v7

--- a/solution.py
+++ b/solution.py
@@ -12,7 +12,7 @@
 
 f32 = jnp.float32
 bf16 = jnp.bfloat16
-CHUNK = 64
+CHUNK = 128
 LONG = 10**10
 PAD = 8
 ANY = pl.BlockSpec(memory_space=pl.ANY)

time: 30.6 us -> 30.7 us (level)
  no operation moved by 1% of the time
where the time goes in v9:
time: 30.7 us; the launch traced here: 30.5 us
  starting transfers between devices  13.3 us (43%)
  Pallas kernels  8.48 us (28%)
  waiting for transfers between devices  7.32 us (24%)
  between operations  1.44 us (5%)
    ppermute x5, starting transfers between devices, send(): return lax.ppermute(v, 'slab', pairs[side])  8.56 us
    ppermute x5, waiting for transfers between devices, send(): return lax.ppermute(v, 'slab', pairs[side])  4.81 us
    ppermute x3, starting transfers between devices, on_device(): lax.ppermute(part, 'cond', [(i, i ^ k) for i in range(4)])  4.61 us
    ppermute x1, waiting for transfers between devices, on_device(): lax.ppermute(pair, 'slab', [(i, i ^ 4) for i in range(count)])  2.5 us
    pallas_call x1, Pallas kernels, make_first_local(): call(lambda *refs: first_local(count, *refs), (jax.ShapeDtypeStruct(adjoi...  2.33 us
    pallas_call x1, Pallas kernels, make_second_local(): call(lambda *refs: second_local(count, *refs), (jax.ShapeDtypeStruct((lay...  1.76 us
    pallas_call x1, Pallas kernels, make_first_message(): call(first_message, (jax.ShapeDtypeStruct((2 * rows + extra, depth), bf16...  1.42 us
    pallas_call x1, Pallas kernels, make_final(): call(final, (jax.ShapeDtypeStruct(state.shape, f32), jax.ShapeDtypeStruct...  1.04 us
  transfers between devices with their start and end apart: 10, of which 4 were waited for; matrix products, arithmetic and copies ran while one was open for 0% of the time, Pallas kernels for 20%

profile of v9, /device:TPU:25, one launch (start us, length us, event | category | flops | bytes accessed | tf_op | source)
XLA Modules:
  0.0 30.5 jit_solution(13718820252438521610)
XLA Ops:
  0.6 0.0 copy-start
  0.7 1.4 %shard_map.95 = (bf16[1072,128]{1,0:T(8,128)(2,1)S(1)}, f32[1,8]{1,0:T(1,128)S(1)}) custom-call(f32[4,512,128]{2,1,0:T(8,128)} %bitcast.13, bf16[32,128]{1,0:T(8,128)(2,1)} %bitcast.16, s32[1,32]{1,0:T(1,128)} %bitcast.17, s32[1,32]{1,0:T(1,128)} %cells.1, f32[1,8]{1,0:T(1,128)} %bitcast.18), custom_call_target="tpu_custom_call" | custom-call | flops 10000000000 | bytes 1 | tf_op jit(solution)/shard_map/pallas_call | solution.py:177
  2.1 1.3 %collective-permute-start = (bf16[1072,128]{1,0:T(8,128)(2,1)S(1)}, bf16[1072,128]{1,0:T(8,128)(2,1)S(1)}, u32[]{:S(2)}, u32[]{:S(2)}) collective-permute-start(bf16[1072,128]{1,0:T(8,128)(2,1)S(1)} %get-tuple-element.21.refs_5_.first), channel_id=1, source_target_pairs={{0,1},{1,0},{2,3},{3,2},{4,5},{5,4},{6,7},{7,6},{8,9},{9,8},{10,11... | collective-permute-start | bytes 823304 | tf_op jit(solution)/shard_map/ppermute | solution.py:614
  4.0 0.0 copy-done
  4.1 0.0 copy-done.1
  4.1 0.0 copy-done.2
  4.1 2.3 %shard_map.96 = (f32[4,512,128]{2,1,0:T(8,128)S(1)}, bf16[1088,128]{1,0:T(8,128)(2,1)S(1)}, f32[8,128]{1,0:T(8,128)S(1)}, f32[2,4,512]{2,1,0:T(4,128)S(1)}, f32[8,512]{1,0:T(8,128)S(1)}) custom-call(f32[4,512,128]{2,1,0:T(8,128)S(1)} %bitcast.14, bf16[4,512,128]{2,1,0:T(8,128)(2,1)S(1)} %bitcast.6, f32[1,8]{1,0:T(1,128)S(1)} %get-tuple-element.22.refs_2_, ...), custom_call_target="tpu_custom_call" | custom-call | flops 10000000000 | bytes 1 | tf_op jit(solution)/shard_map/pallas_call | solution.py:232
  6.4 2.0 %collective-permute-start.2 = (bf16[1088,128]{1,0:T(8,128)(2,1)S(1)}, bf16[1088,128]{1,0:T(8,128)(2,1)S(1)}, u32[]{:S(2)}, u32[]{:S(2)}) collective-permute-start(bf16[1088,128]{1,0:T(8,128)(2,1)S(1)} %get-tuple-element.26), channel_id=1, source_target_pairs={{1,2},{3,4},{5,6},{2,1},{4,3},{6,5},{9,10},{11,12},{13,14},{10,9},... | collective-permute-start | bytes 835592 | tf_op jit(solution)/shard_map/ppermute | solution.py:614
  8.4 1.1 %collective-permute-done.message = bf16[1072,128]{1,0:T(8,128)(2,1)S(1)} collective-permute-done((bf16[1072,128]{1,0:T(8,128)(2,1)S(1)}, bf16[1072,128]{1,0:T(8,128)(2,1)S(1)}, u32[]{:S(2)}, u32[]{:S(2)}) %collective-permute-start) | collective-permute-done | bytes 274464 | tf_op jit(solution)/shard_map/ppermute | solution.py:614
  9.6 0.7 %shard_map.97 = (f32[2,528,128]{2,1,0:T(8,128)S(1)}, bf16[1024,128]{1,0:T(8,128)(2,1)S(1)}, bf16[32,128]{1,0:T(8,128)(2,1)S(1)}, bf16[96,128]{1,0:T(8,128)(2,1)S(1)}) custom-call(bf16[1072,128]{1,0:T(8,128)(2,1)S(1)} %collective-permute-done.message, f32[4,512,128]{2,1,0:T(8,128)S(1)} %get-tuple-element.23.pre.refs_1_, bf16[4,512,128]{2,1,0:T(8,128)(2,1)S(1)} %bitcast.7, ...), custom_call_target="tpu_custom_call" | custom-call | flops 10000000000 | bytes 1 | tf_op jit(solution)/shard_map/pallas_call | solution.py:340
  10.3 0.1 collective-permute-start.3
  10.4 1.2 %collective-permute-start.6 = (bf16[32,128]{1,0:T(8,128)(2,1)S(1)}, bf16[32,128]{1,0:T(8,128)(2,1)S(1)}, u32[]{:S(2)}, u32[]{:S(2)}) collective-permute-start(bf16[32,128]{1,0:T(8,128)(2,1)S(1)} %get-tuple-element.35), channel_id=1, source_target_pairs={{0,1},{1,0},{2,3},{3,2},{4,5},{5,4},{6,7},{7,6},{8,9},{9,8},{10,11... | collective-permute-start | bytes 24584 | tf_op jit(solution)/shard_map/ppermute | solution.py:614
  11.6 0.2 collective-permute-start.1
  11.8 2.5 %collective-permute-done.3.two = bf16[96,128]{1,0:T(8,128)(2,1)S(1)} collective-permute-done((bf16[96,128]{1,0:T(8,128)(2,1)S(1)}, bf16[96,128]{1,0:T(8,128)(2,1)S(1)}, u32[]{:S(2)}, u32[]{:S(2)}) %collective-permute-start.3) | collective-permute-done | bytes 24608 | tf_op jit(solution)/shard_map/ppermute | solution.py:627
  14.3 0.0 collective-permute-start.4
  14.4 2.1 %collective-permute-done.2.refs_0_ = bf16[1088,128]{1,0:T(8,128)(2,1)S(1)} collective-permute-done((bf16[1088,128]{1,0:T(8,128)(2,1)S(1)}, bf16[1088,128]{1,0:T(8,128)(2,1)S(1)}, u32[]{:S(2)}, u32[]{:S(2)}) %collective-permute-start.2) | collective-permute-done | bytes 278560 | tf_op jit(solution)/shard_map/ppermute | solution.py:614
  16.5 0.4 %shard_map.99 = (f32[2,528,128]{2,1,0:T(8,128)S(1)}, bf16[1024,128]{1,0:T(8,128)(2,1)S(1)}, f32[8,512]{1,0:T(8,128)S(1)}) custom-call(bf16[1088,128]{1,0:T(8,128)(2,1)S(1)} %collective-permute-done.2.refs_0_, f32[4,512,128]{2,1,0:T(8,128)S(1)} %get-tuple-element.23.pre.refs_1_, bf16[4,512,128]{2,1,0:T(8,128)(2,1)S(1)} %bitcast.8, ...), custom_call_target="tpu_custom_call" | custom-call | flops 600000000 | bytes 1 | tf_op jit(solution)/shard_map/pallas_call | solution.py:384
  16.9 3.8 %collective-permute-start.5 = (bf16[1024,128]{1,0:T(8,128)(2,1)S(1)}, bf16[1024,128]{1,0:T(8,128)(2,1)S(1)}, u32[]{:S(2)}, u32[]{:S(2)}) collective-permute-start(bf16[1024,128]{1,0:T(8,128)(2,1)S(1)} %get-tuple-element.33), channel_id=1, source_target_pairs={{1,2},{3,4},{5,6},{2,1},{4,3},{6,5},{9,10},{11,12},{13,14},{10,9},... | collective-permute-start | bytes 786440 | tf_op jit(solution)/shard_map/ppermute | solution.py:614
  20.7 1.8 %shard_map.100 = (f32[4,512,128]{2,1,0:T(8,128)S(1)}, f32[4,8,512]{2,1,0:T(8,128)S(1)}, f32[4,8,512]{2,1,0:T(8,128)S(1)}) custom-call(f32[2,528,128]{2,1,0:T(8,128)S(1)} %get-tuple-element.25.refs_0_, f32[2,528,128]{2,1,0:T(8,128)S(1)} %get-tuple-element.29.refs_1_, bf16[4,512,128]{2,1,0:T(8,128)(2,1)S(1)} %bitcast.9, f32[8,128]{1,0:T(8,128)S(1)} %get-tuple-element.30.refs_3_), custom_call_target="tpu_custom_call" | custom-call | flops 1300000000 | bytes 1 | tf_op jit(solution)/shard_map/pallas_call | solution.py:436
  22.4 0.0 collective-permute-done.4.two
  22.5 0.0 collective-permute-done.6.early_a
  22.5 4.1 %collective-permute-start.7 = (f32[2,4,512]{2,1,0:T(4,128)S(1)}, f32[2,4,512]{2,1,0:T(4,128)S(1)}, u32[]{:S(2)}, u32[]{:S(2)}) collective-permute-start(f32[2,4,512]{2,1,0:T(4,128)S(1)} %shard_map.104.refs_0_), channel_id=1, source_target_pairs={{0,24},{8,16},{16,8},{24,0},{1,25},{9,17},{17,9},{25,1},{2,26},{10... | collective-permute-start | bytes 49160 | tf_op jit(solution)/shard_map/ppermute | solution.py:637
  26.7 0.3 collective-permute-start.8
  26.9 0.2 collective-permute-start.9
  27.1 0.5 %shard_map.102.state = f32[4,512,128]{2,1,0:T(8,128)S(1)} custom-call(bf16[4,512,128]{2,1,0:T(8,128)(2,1)S(1)} %bitcast.10, f32[4,512,128]{2,1,0:T(8,128)S(1)} %get-tuple-element.31.refs_1_, bf16[384,128]{1,0:T(8,128)(2,1)S(1)} %shard_map.101.refs_2_.after), custom_call_target="tpu_custom_call" | custom-call | flops 1 | bytes 1 | tf_op jit(solution)/shard_map/pallas_call | solution.py:476
  27.6 1.6 %collective-permute-done.1.message = bf16[1024,128]{1,0:T(8,128)(2,1)S(1)} collective-permute-done((bf16[1024,128]{1,0:T(8,128)(2,1)S(1)}, bf16[1024,128]{1,0:T(8,128)(2,1)S(1)}, u32[]{:S(2)}, u32[]{:S(2)}) %collective-permute-start.1) | collective-permute-done | bytes 262176 | tf_op jit(solution)/shard_map/ppermute | solution.py:614
  29.2 0.2 shard_map.103.at_a
  29.4 0.0 collective-permute-done.7.refs_1_
  29.4 0.0 collective-permute-done.8.refs_2_
  29.4 0.0 collective-permute-done.9.refs_3_
  29.5 0.0 collective-permute-done.5.message_b
  29.5 1.0 %shard_map.105 = (f32[4,512,128]{2,1,0:T(8,128)}, f32[2,4,512]{2,1,0:T(4,128)}) custom-call(f32[2,512,128]{2,1,0:T(8,128)S(1)} %shard_map.103.at_a, bf16[1024,128]{1,0:T(8,128)(2,1)S(1)} %collective-permute-done.5.message_b, f32[4,512,128]{2,1,0:T(8,128)S(1)} %shard_map.102.state, bf16[4,512,128]{2,1,0:T(8,128)(2,1)S(1)} %bitcast.12, ...), custom_call_target="tpu_custom_call" | custom-call | flops 1 | bytes 1 | tf_op jit(solution)/shard_map/pallas_call | solution.py:589
  (5 shorter events, 0.1 us)
Async XLA Ops:
  0.6 3.4 %copy-start = (bf16[1,4,512,128]{3,2,1,0:T(8,128)(2,1)S(1)}, bf16[1,4,512,128]{3,2,1,0:T(8,128)(2,1)}, u32[]{:S(2)}) copy-start(bf16[1,4,512,128]{3,2,1,0:T(8,128)(2,1)} %param.9) | copy-start | bytes 1572868
  0.6 3.4 %copy-start.1 = (f32[1,4,512,128]{3,2,1,0:T(8,128)S(1)}, f32[1,4,512,128]{3,2,1,0:T(8,128)}, u32[]{:S(2)}) copy-start(f32[1,4,512,128]{3,2,1,0:T(8,128)} %param.8) | copy-start | bytes 3145732
  0.7 3.4 %copy-start.2 = (s32[2,4,512]{2,1,0:T(4,128)S(1)}, s32[2,4,512]{2,1,0:T(4,128)}, u32[]{:S(2)}) copy-start(s32[2,4,512]{2,1,0:T(4,128)} %refs_4_.1) | copy-start | bytes 49156
  2.1 7.5 %collective-permute-start = (bf16[1072,128]{1,0:T(8,128)(2,1)S(1)}, bf16[1072,128]{1,0:T(8,128)(2,1)S(1)}, u32[]{:S(2)}, u32[]{:S(2)}) collective-permute-start(bf16[1072,128]{1,0:T(8,128)(2,1)S(1)} %get-tuple-element.21.refs_5_.first), channel_id=1, source_target_pairs={{0,1},{1,0},{2,3},{3,2},{4,5},{5,4},{6,7},{7,6},{8,9},{9,8},{10,11... | collective-permute-start | bytes 823304 | tf_op jit(solution)/shard_map/ppermute | solution.py:614
  6.4 10.0 %collective-permute-start.2 = (bf16[1088,128]{1,0:T(8,128)(2,1)S(1)}, bf16[1088,128]{1,0:T(8,128)(2,1)S(1)}, u32[]{:S(2)}, u32[]{:S(2)}) collective-permute-start(bf16[1088,128]{1,0:T(8,128)(2,1)S(1)} %get-tuple-element.26), channel_id=1, source_target_pairs={{1,2},{3,4},{5,6},{2,1},{4,3},{6,5},{9,10},{11,12},{13,14},{10,9},... | collective-permute-start | bytes 835592 | tf_op jit(solution)/shard_map/ppermute | solution.py:614
  10.3 4.0 %collective-permute-start.3 = (bf16[96,128]{1,0:T(8,128)(2,1)S(1)}, bf16[96,128]{1,0:T(8,128)(2,1)S(1)}, u32[]{:S(2)}, u32[]{:S(2)}) collective-permute-start(bf16[96,128]{1,0:T(8,128)(2,1)S(1)} %get-tuple-element.28.one.after), channel_id=1, source_target_pairs={{0,4},{1,5},{2,6},{3,7},{4,0},{5,1},{6,2},{7,3},{8,12},{9,13},{10,... | collective-permute-start | bytes 73736 | tf_op jit(solution)/shard_map/ppermute | solution.py:627
  10.4 12.1 %collective-permute-start.6 = (bf16[32,128]{1,0:T(8,128)(2,1)S(1)}, bf16[32,128]{1,0:T(8,128)(2,1)S(1)}, u32[]{:S(2)}, u32[]{:S(2)}) collective-permute-start(bf16[32,128]{1,0:T(8,128)(2,1)S(1)} %get-tuple-element.35), channel_id=1, source_target_pairs={{0,1},{1,0},{2,3},{3,2},{4,5},{5,4},{6,7},{7,6},{8,9},{9,8},{10,11... | collective-permute-start | bytes 24584 | tf_op jit(solution)/shard_map/ppermute | solution.py:614
  11.6 17.6 %collective-permute-start.1 = (bf16[1024,128]{1,0:T(8,128)(2,1)S(1)}, bf16[1024,128]{1,0:T(8,128)(2,1)S(1)}, u32[]{:S(2)}, u32[]{:S(2)}) collective-permute-start(bf16[1024,128]{1,0:T(8,128)(2,1)S(1)} %get-tuple-element.24), channel_id=1, source_target_pairs={{0,1},{1,0},{2,3},{3,2},{4,5},{5,4},{6,7},{7,6},{8,9},{9,8},{10,11... | collective-permute-start | bytes 786440 | tf_op jit(solution)/shard_map/ppermute | solution.py:614
  14.3 8.1 %collective-permute-start.4 = (bf16[192,128]{1,0:T(8,128)(2,1)S(1)}, bf16[192,128]{1,0:T(8,128)(2,1)S(1)}, u32[]{:S(2)}, u32[]{:S(2)}) collective-permute-start(bf16[192,128]{1,0:T(8,128)(2,1)S(1)} %shard_map.98.refs_4_.one), channel_id=1, source_target_pairs={{0,2},{1,3},{2,0},{3,1},{4,6},{5,7},{6,4},{7,5},{8,10},{9,11},{10,... | collective-permute-start | bytes 147464 | tf_op jit(solution)/shard_map/ppermute | solution.py:628
  16.9 12.6 %collective-permute-start.5 = (bf16[1024,128]{1,0:T(8,128)(2,1)S(1)}, bf16[1024,128]{1,0:T(8,128)(2,1)S(1)}, u32[]{:S(2)}, u32[]{:S(2)}) collective-permute-start(bf16[1024,128]{1,0:T(8,128)(2,1)S(1)} %get-tuple-element.33), channel_id=1, source_target_pairs={{1,2},{3,4},{5,6},{2,1},{4,3},{6,5},{9,10},{11,12},{13,14},{10,9},... | collective-permute-start | bytes 786440 | tf_op jit(solution)/shard_map/ppermute | solution.py:614
  22.5 6.9 %collective-permute-start.7 = (f32[2,4,512]{2,1,0:T(4,128)S(1)}, f32[2,4,512]{2,1,0:T(4,128)S(1)}, u32[]{:S(2)}, u32[]{:S(2)}) collective-permute-start(f32[2,4,512]{2,1,0:T(4,128)S(1)} %shard_map.104.refs_0_), channel_id=1, source_target_pairs={{0,24},{8,16},{16,8},{24,0},{1,25},{9,17},{17,9},{25,1},{2,26},{10... | collective-permute-start | bytes 49160 | tf_op jit(solution)/shard_map/ppermute | solution.py:637
  26.7 2.8 %collective-permute-start.8 = (f32[2,4,512]{2,1,0:T(4,128)S(1)}, f32[2,4,512]{2,1,0:T(4,128)S(1)}, u32[]{:S(2)}, u32[]{:S(2)}) collective-permute-start(f32[2,4,512]{2,1,0:T(4,128)S(1)} %shard_map.104.refs_0_), channel_id=1, source_target_pairs={{0,16},{8,24},{16,0},{24,8},{1,17},{9,25},{17,1},{25,9},{2,18},{10... | collective-permute-start | bytes 49160 | tf_op jit(solution)/shard_map/ppermute | solution.py:637
  26.9 2.5 %collective-permute-start.9 = (f32[2,4,512]{2,1,0:T(4,128)S(1)}, f32[2,4,512]{2,1,0:T(4,128)S(1)}, u32[]{:S(2)}, u32[]{:S(2)}) collective-permute-start(f32[2,4,512]{2,1,0:T(4,128)S(1)} %shard_map.104.refs_0_), channel_id=1, source_target_pairs={{0,8},{8,0},{16,24},{24,16},{1,9},{9,1},{17,25},{25,17},{2,10},{10... | collective-permute-start | bytes 49160 | tf_op jit(solution)/shard_map/ppermute | solution.py:637
